TPU v7x, 128 devices: a whole 4x4x4 slice. The times are simulated.
128 devices in a mesh: dp: 64 (over z, x_lo, y, core), fsdp: 2 (over x_hi).
Axes of the slice: x: 4 (x_hi: 2, x_lo: 2; x = x_hi * 2 + x_lo), y: 4, z: 4, core: 2. Of those that a mesh axis runs over, the one named last changes fastest.
Arguments:
- latents: bfloat16 [64, 256, 1280], P('dp'), may hold values from -6 to 6
- script_ids: int32 [64], P('dp'), may hold values from 0 to 15
- gain_table: bfloat16 [1280, 16], P(('dp', 'fsdp')), may hold values from 0.099609375 to 1.8984375
- bias_one: bfloat16 [1280], P(('dp', 'fsdp')), may hold values from -2.390625 to 2.390625
- w_qkv: bfloat16 [1280, 3840], P(('dp', 'fsdp')), may hold values from -0.15625 to 0.15625
- w_out: bfloat16 [1280, 1280], P(('dp', 'fsdp')), may hold values from -0.625 to 0.625
- gain_two: bfloat16 [1280], P(('dp', 'fsdp')), may hold values from 0.099609375 to 1.8984375
- bias_two: bfloat16 [1280], P(('dp', 'fsdp')), may hold values from -2.390625 to 2.390625
- w_up: bfloat16 [1280, 1280], P(('dp', 'fsdp')), may hold values from -0.15625 to 0.15625
- w_down: bfloat16 [1280, 1280], P(('dp', 'fsdp')), may hold values from -0.25 to 0.25
- cotangent: bfloat16 [64, 256, 1280], P('dp'), may hold values from -6 to 6
Outputs:
- latents_out: bfloat16 [64, 256, 1280], P('dp')
- input_grad: float32 [64, 256, 1280], P('dp')
- gain_table_grad: float32 [1280, 16], P(('dp', 'fsdp'))
- bias_one_grad: float32 [1280], P(('dp', 'fsdp'))
- w_qkv_grad: float32 [1280, 3840], P(('dp', 'fsdp'))
- w_out_grad: float32 [1280, 1280], P(('dp', 'fsdp'))
- gain_two_grad: float32 [1280], P(('dp', 'fsdp'))
- bias_two_grad: float32 [1280], P(('dp', 'fsdp'))
- w_up_grad: float32 [1280, 1280], P(('dp', 'fsdp'))
- w_down_grad: float32 [1280, 1280], P(('dp', 'fsdp'))
All inputs are finite; a program needn't handle non-finite values.
Results may differ from a plain program's by a relative error of at most 0.012.
Values may be sent and summed in bfloat16 or wider, within the bound.
A program may use at most 256 MiB of HBM per device.

v0:
```python
import math

import jax
import jax.numpy as jnp
from jax import lax
from jax.sharding import PartitionSpec as P

HEADS = 8


EPSILON = 1e-05
PRECISE = lax.Precision.HIGHEST


def in_one_piece(arrays, axis, dim, along):
    widths = [a.shape[along] for a in arrays]
    both = jnp.concatenate(arrays, axis=along)
    whole = lax.all_gather(both, axis, axis=dim, tiled=True)
    return tuple(jnp.split(whole, [sum(widths[:k]) for k in range(1, len(widths))], axis=along))


def layer_norm(inputs):
    average = jnp.mean(inputs, axis=-1, keepdims=True)
    centered = inputs - average
    variance = jnp.mean(centered * centered, axis=-1, keepdims=True)
    inv_scale = lax.rsqrt(variance + EPSILON)
    return (centered * inv_scale, inv_scale)


def norm_back(grad_normed, normed, inv_scale):
    first_mean = jnp.mean(grad_normed, axis=-1, keepdims=True)
    second_mean = jnp.mean(grad_normed * normed, axis=-1, keepdims=True)
    return inv_scale * (grad_normed - first_mean - normed * second_mean)


def times_t(left, right):
    return lax.dot_general(
        left, right, (((1,), (1,)), ((), ())), preferred_element_type=jnp.float32
    )


def forward_pass(latents, script_ids, gathered):
    full_qkv, full_out, full_up, full_down, full_small = gathered
    items, length, width = latents.shape
    rows_all = items * length
    head_dim = width // HEADS
    scripts = full_small.shape[1] - 3
    small_float = full_small.astype(jnp.float32)
    table = small_float[:, :scripts]
    bias_first = small_float[:, scripts]
    gain_second = small_float[:, scripts + 1]
    bias_second = small_float[:, scripts + 2]
    one_hot = (script_ids[:, None] == jnp.arange(scripts, dtype=jnp.int32)[None, :]).astype(
        jnp.float32
    )
    gains_item = lax.dot_general(
        one_hot,
        table,
        (((1,), (1,)), ((), ())),
        precision=PRECISE,
        preferred_element_type=jnp.float32,
    )
    gains_rows = jnp.broadcast_to(gains_item[:, None, :], (items, length, width)).reshape(
        rows_all, width
    )
    inputs = latents.astype(jnp.float32).reshape(rows_all, width)
    normed_one, inv_one = layer_norm(inputs)
    first = (normed_one * gains_rows + bias_first).astype(jnp.bfloat16)
    projected = jnp.dot(first, full_qkv, preferred_element_type=jnp.float32).astype(jnp.bfloat16)
    split = projected.reshape(items, length, 3, HEADS, head_dim)
    queries = split[:, :, 0]
    key_rows = split[:, :, 1]
    values = split[:, :, 2]
    score_scale = 1.0 / math.sqrt(head_dim)
    scores = (
        jnp.einsum("ashe,athe->ahst", queries, key_rows, preferred_element_type=jnp.float32)
        * score_scale
    )
    row_max = jnp.max(scores, axis=-1, keepdims=True)
    exp_scores = jnp.exp(scores - row_max)
    probs = exp_scores / jnp.sum(exp_scores, axis=-1, keepdims=True)
    probs_low = probs.astype(jnp.bfloat16)
    mixed = jnp.einsum("ahst,athe->ashe", probs_low, values, preferred_element_type=jnp.float32)
    mixed = mixed.reshape(rows_all, width).astype(jnp.bfloat16)
    middle = inputs + jnp.dot(mixed, full_out, preferred_element_type=jnp.float32)
    normed_two, inv_two = layer_norm(middle)
    second = (normed_two * gain_second + bias_second).astype(jnp.bfloat16)
    upper = jnp.dot(second, full_up, preferred_element_type=jnp.float32)
    active = jax.nn.gelu(upper).astype(jnp.bfloat16)
    output = middle + jnp.dot(active, full_down, preferred_element_type=jnp.float32)
    kept = (
        one_hot,
        gains_rows,
        gain_second,
        normed_one,
        inv_one,
        first,
        queries,
        key_rows,
        values,
        probs,
        probs_low,
        mixed,
        normed_two,
        inv_two,
        second,
        upper,
        active,
    )
    return (output, kept)


def per_device(
    latents,
    script_ids,
    gain_table,
    bias_one,
    w_qkv,
    w_out,
    gain_two,
    bias_two,
    w_up,
    w_down,
    cotangent,
):
    small = jnp.concatenate(
        [gain_table, bias_one[:, None], gain_two[:, None], bias_two[:, None]], axis=1
    )
    gathered = in_one_piece((w_qkv, w_out, w_up, w_down, small), ("dp", "fsdp"), 0, 1)
    output, kept = forward_pass(latents, script_ids, gathered)
    gathered = in_one_piece((w_qkv, w_out, w_up, w_down, small), ("dp", "fsdp"), 0, 1)
    output_again, kept = forward_pass(latents, script_ids, gathered)
    full_qkv, full_out, full_up, full_down, full_small = gathered
    (
        one_hot,
        gains_rows,
        gain_second,
        normed_one,
        inv_one,
        first,
        queries,
        key_rows,
        values,
        probs,
        probs_low,
        mixed,
        normed_two,
        inv_two,
        second,
        upper,
        active,
    ) = kept
    items, length, width = latents.shape
    rows_all = items * length
    head_dim = width // HEADS
    score_scale = 1.0 / math.sqrt(head_dim)
    scripts = one_hot.shape[1]
    share = rows_all // lax.axis_size("fsdp")
    start = lax.axis_index("fsdp") * share

    def select(values_in):
        return lax.dynamic_slice_in_dim(values_in, start, share, 0)

    def weight_grad(left, right):
        return lax.dot_general(
            select(left),
            select(right),
            (((0,), (0,)), ((), ())),
            preferred_element_type=jnp.float32,
        )

    grad_out = cotangent.astype(jnp.float32).reshape(rows_all, width)
    grad_branch = grad_out.astype(jnp.bfloat16)
    down_grad = weight_grad(active, grad_branch)
    grad_active = times_t(grad_branch, full_down)
    upper_value, gelu_back = jax.vjp(jax.nn.gelu, upper)
    grad_upper = gelu_back(grad_active)[0].astype(jnp.bfloat16)
    up_grad = weight_grad(second, grad_upper)
    grad_second = times_t(grad_upper, full_up)
    grad_middle = grad_out + norm_back(grad_second * gain_second, normed_two, inv_two)
    grad_attn_out = grad_middle.astype(jnp.bfloat16)
    out_grad = weight_grad(mixed, grad_attn_out)
    grad_mixed = (
        times_t(grad_attn_out, full_out)
        .astype(jnp.bfloat16)
        .reshape(items, length, HEADS, head_dim)
    )
    grad_probs = jnp.einsum(
        "ashe,athe->ahst", grad_mixed, values, preferred_element_type=jnp.float32
    )
    grad_values = jnp.einsum(
        "ahst,ashe->athe", probs_low, grad_mixed, preferred_element_type=jnp.float32
    )
    row_total = jnp.sum(grad_probs * probs, axis=-1, keepdims=True)
    grad_scores = (probs * (grad_probs - row_total)).astype(jnp.bfloat16)
    grad_queries = (
        jnp.einsum("ahst,athe->ashe", grad_scores, key_rows, preferred_element_type=jnp.float32)
        * score_scale
    )
    grad_keys = (
        jnp.einsum("ahst,ashe->athe", grad_scores, queries, preferred_element_type=jnp.float32)
        * score_scale
    )
    grad_projected = jnp.concatenate(
        [
            grad_queries.reshape(rows_all, width),
            grad_keys.reshape(rows_all, width),
            grad_values.reshape(rows_all, width),
        ],
        axis=1,
    ).astype(jnp.bfloat16)
    qkv_grad = weight_grad(first, grad_projected)
    grad_first = times_t(grad_projected, full_qkv)
    input_grad = grad_middle + norm_back(grad_first * gains_rows, normed_one, inv_one)
    hot_rows = jnp.broadcast_to(one_hot[:, None, :], (items, length, scripts)).reshape(
        rows_all, scripts
    )
    table_grad = lax.dot_general(
        select(grad_first * normed_one),
        select(hot_rows),
        (((0,), (0,)), ((), ())),
        precision=PRECISE,
        preferred_element_type=jnp.float32,
    )
    bias_first_grad = jnp.sum(select(grad_first), axis=0)
    gain_second_grad = jnp.sum(select(grad_second * normed_two), axis=0)
    bias_second_grad = jnp.sum(select(grad_second), axis=0)
    small_grad = jnp.concatenate(
        [
            table_grad,
            bias_first_grad[:, None],
            gain_second_grad[:, None],
            bias_second_grad[:, None],
        ],
        axis=1,
    )
    owned = (
        lax.psum_scatter(qkv_grad, ("dp", "fsdp"), scatter_dimension=0, tiled=True),
        lax.psum_scatter(out_grad, ("dp", "fsdp"), scatter_dimension=0, tiled=True),
        lax.psum_scatter(up_grad, ("dp", "fsdp"), scatter_dimension=0, tiled=True),
        lax.psum_scatter(down_grad, ("dp", "fsdp"), scatter_dimension=0, tiled=True),
        lax.psum_scatter(small_grad, ("dp", "fsdp"), scatter_dimension=0, tiled=True),
    )
    qkv_own, out_own, up_own, down_own, small_own = owned
    latents_out = output.reshape(items, length, width).astype(jnp.bfloat16)
    input_grad = input_grad.reshape(items, length, width)
    return (
        latents_out,
        input_grad,
        small_own[:, :scripts],
        small_own[:, scripts],
        qkv_own,
        out_own,
        small_own[:, scripts + 1],
        small_own[:, scripts + 2],
        up_own,
        down_own,
    )


def solution(mesh):
    return jax.shard_map(
        per_device,
        mesh=mesh,
        in_specs=(
            P("dp", None, None),
            P("dp"),
            P(("dp", "fsdp"), None),
            P(("dp", "fsdp")),
            P(("dp", "fsdp"), None),
            P(("dp", "fsdp"), None),
            P(("dp", "fsdp")),
            P(("dp", "fsdp")),
            P(("dp", "fsdp"), None),
            P(("dp", "fsdp"), None),
            P("dp", None, None),
        ),
        out_specs=(
            P("dp", None, None),
            P("dp", None, None),
            P(("dp", "fsdp"), None),
            P(("dp", "fsdp")),
            P(("dp", "fsdp"), None),
            P(("dp", "fsdp"), None),
            P(("dp", "fsdp")),
            P(("dp", "fsdp")),
            P(("dp", "fsdp"), None),
            P(("dp", "fsdp"), None),
        ),
        check_vma=False,
    )
```

profile of v0, /device:TPU:1, one launch (start us, length us, event | category | flops | bytes accessed | tf_op | source)
XLA Modules:
  0.0 793.3 jit_solution(2016784254813567190)
XLA Ops:
  7.2 0.0 copy-start
  7.2 0.0 all-gather.3.cloned.1.call-start
  7.2 0.8 copy.46
  8.0 0.8 copy.47
  8.8 0.8 copy.48
  9.5 1.7 concatenate.14
  11.3 0.0 all-gather.3.cloned.1.call-update
  11.3 0.0 all-reduce.8.cloned.1.call-start
  12.0 1.3 convert_reduce_fusion
  13.3 0.3 fusion.44
  13.6 348.1 %all-gather.3.cloned.1.call-done = bf16[128,10,7699]{2,1,0:T(8,128)(2,1)} async-done(((bf16[1,10,7699]{2,1,0:T(8,128)(2,1)}), bf16[128,10,7699]{2,1,0:T(8,128)(2,1)}) %all-gather.3.cloned.1.call-update) | async-done | bytes 19709456 | tf_op jit(solution)/shard_map/all_gather | solution.py:18
  361.7 31.7 %reshape.211 = bf16[1280,7699]{1,0:T(8,128)(2,1)} reshape(bf16[128,10,7699]{2,1,0:T(8,128)(2,1)} %all-gather.3.cloned.1.call-done) | data formatting | bytes 39418880
  393.4 1.0 slice_convert_fusion
  394.4 1.1 slice_reduce_fusion.1
  395.6 1.2 convolution_reduce_fusion
  396.8 1.4 fusion.40
  398.1 0.8 copy-done.16
  399.0 7.8 fusion.5
  406.8 2.8 copy.49
  409.7 2.2 fusion.89
  411.9 1.9 convolution_convert_fusion.1
  413.9 3.3 fusion.90
  417.2 0.3 multiply_reduce_fusion.4
  417.5 0.3 add_convert_fusion
  417.8 4.2 multiply_convert_fusion.1
  422.0 3.4 fusion.51
  425.5 3.4 multiply_reduce_fusion.6
  428.9 1.5 fusion.88
  430.4 0.9 copy-done.14
  431.2 3.8 fusion.29
  435.1 2.2 copy.52
  437.3 2.4 convolution_convert_fusion
  439.7 0.6 copy-done.9
  440.3 0.1 copy-done.18
  440.4 0.6 multiply_reduce_fusion
  441.0 0.4 multiply_convert_fusion
  441.4 0.5 fusion.43
  441.9 0.3 fusion.42
  442.2 7.1 multiply_reduce_fusion.5
  449.3 0.1 pad_maximum_fusion
  449.4 1.6 copy-done.8
  451.1 0.1 fusion.57
  451.2 1.0 copy-done.15
  452.2 0.2 copy-done.21
  452.4 3.8 fusion.73
  456.2 3.8 fusion.70
  460.0 0.1 dynamic-slice_reduce_fusion.1
  460.1 0.0 copy-start.13
  460.1 0.0 copy-start.19
  460.1 8.2 %fusion.55 = f32[1280,3840]{1,0:T(8,128)} fusion(bf16[256,3840]{0,1:T(8,128)(2,1)S(1)} %pad_maximum_fusion, s32[]{:T(128)S(6)} %select_n.2, bf16[256,1280]{1,0:T(8,128)(2,1)S(1)} %copy-done.17), kind=kOutput, calls=%fused_computation.65 | convolution fusion | flops 1258291200 | bytes 20972544 | tf_op jit(solution)/shard_map/dot_general | solution.py:165
  468.3 3.8 fusion.66
  472.1 0.5 fusion.58
  472.6 0.7 pad_maximum_fusion.1
  473.3 0.0 all-reduce.8.cloned.1.call-update
  473.4 3.9 fusion.35
  477.3 1.5 add_bitcast_fusion
  478.9 298.4 %all-reduce.8.cloned.1.call-done = (f32[1280,19]{0,1:T(8,128)}, f32[1280,3840]{1,0:T(8,128)}, f32[1280,1280]{1,0:T(8,128)}, f32[1280,1280]{1,0:T(8,128)}, f32[1280,1280]{1,0:T(8,128)}) async-done(((f32[1280,19]{0,1:T(8,128)}, f32[1280,3840]{1,0:T(8,128)}, f32[1280,1280]{1,0:T(8,128)}, f32[1280,1280]{1,0:T(8,128)}, f32[1280,1280]{1,0:T(8,128)}), (f32[1280,19]{0,1:T(8,128)}, f32[1280,3840]{1,0:T(8,128)}, ...) | async-done | bytes 39418896
  777.2 0.8 constant_dynamic-slice_fusion
  778.0 0.7 copy.56
  778.7 1.7 constant_dynamic-slice_fusion.4
  780.4 1.5 constant_dynamic-slice_fusion.3
  782.0 1.5 constant_dynamic-slice_fusion.2
  783.5 1.5 constant_dynamic-slice_fusion.1
  785.0 1.4 dynamic-slice_bitcast_fusion
  (49 shorter events, 0.1 us)
Async XLA Ops:
  7.2 6.1 copy-start
  7.2 354.5 %all-gather.3.cloned.1.call-start = ((), (), s32[]{:S(2)}) async-start(), calls=%async_computation | async-start | bytes 32231424 | tf_op jit(solution)/shard_map/all_gather | solution.py:18
  11.3 765.9 %all-reduce.8.cloned.1.call-start = ((), (), s32[]{:S(2)}) async-start(), calls=%async_computation.1 | async-start | bytes 78888960
  398.1 0.8 copy-start.16
  409.7 2.2 copy-start.1
  413.8 3.3 copy-start.20
  417.8 4.2 copy-start.10
  417.8 4.2 copy-start.12
  425.5 3.4 copy-start.22
  428.9 1.5 copy-start.7
  430.4 0.9 copy-start.14
  437.3 2.5 copy-start.2
  437.3 3.0 copy-start.9
  437.3 3.1 copy-start.18
  449.3 22.8 %copy-start.3 = (f32[256,1280]{1,0:T(8,128)}, f32[256,1280]{1,0:T(8,128)S(1)}, u32[]{:S(2)}) copy-start(f32[256,1280]{1,0:T(8,128)S(1)} %get-tuple-element.72) | copy-start | bytes 3932164
  449.3 1.8 copy-start.8
  451.1 1.1 copy-start.15
  451.1 1.3 copy-start.21
  452.4 3.8 copy-start.11
  452.4 3.8 copy-start.23
  456.2 3.9 copy-start.17
  460.1 8.3 %copy-start.13 = (bf16[1,256,1280]{2,1,0:T(8,128)(2,1)S(1)}, bf16[1,256,1280]{2,1,0:T(8,128)(2,1)}, u32[]{:S(2)}) copy-start(bf16[1,256,1280]{2,1,0:T(8,128)(2,1)} %param.21) | copy-start | bytes 1966084
  460.1 8.2 %copy-start.19 = (bf16[256,1280]{1,0:T(8,128)(2,1)S(1)}, bf16[256,1280]{1,0:T(8,128)(2,1)}, u32[]{:S(2)}) copy-start(bf16[256,1280]{1,0:T(8,128)(2,1)} %get-tuple-element.67) | copy-start | bytes 1966084
  468.3 3.8 copy-start.6
  473.3 4.0 copy-start.4
  473.4 4.0 copy-start.5
Sparse Core Ops, SparseCore 0:
  11.4 350.2 all-gather.2
  473.4 303.7 all-reduce.7
where the time goes:
time: 795 us; the launch traced here: 793 us
  waiting for transfers between devices  646 us (81%)
  matrix products  66.3 us (8%)
  local copies, waits for them, and re-layouts  56.4 us (7%)
  between operations  15 us (2%)
  other arithmetic  8.98 us (1%)
    all_gather x1, waiting for transfers between devices, in_one_piece(): whole = lax.all_gather(both, axis, axis=dim, tiled=True)  348 us
    unnamed x3, waiting for transfers between devices  298 us
    unnamed x54, local copies, waits for them, and re-layouts  44 us
    dot_general x4, matrix products, weight_grad(): lax.dot_general(select(left), select(right), (((0,), (0,)), ((), ())), pr...  19.6 us
    dot_general x4, matrix products, times_t(): lax.dot_general(left, right, (((1,), (1,)), ((), ())), preferred_element_...  17.7 us
  transfers between devices with their start and end apart: 2, of which 2 were waited for; matrix products, arithmetic and copies ran while one was open for 1% of the time, Pallas kernels for 0%

commit v1 on v0

--- a/solution.py
+++ b/solution.py
@@ -4,6 +4,9 @@
 import jax.numpy as jnp
 from jax import lax
 from jax.sharding import PartitionSpec as P
+
+from jax.experimental import pallas as pl
+from jax.experimental.pallas import tpu as pltpu
 
 HEADS = 8
 
@@ -17,6 +20,253 @@
     both = jnp.concatenate(arrays, axis=along)
     whole = lax.all_gather(both, axis, axis=dim, tiled=True)
     return tuple(jnp.split(whole, [sum(widths[:k]) for k in range(1, len(widths))], axis=along))
+
+
+MESH = pl.DeviceIdType.MESH
+CW = 640
+
+class Pos:
+    def __init__(s):
+        dp = lax.axis_index("dp"); s.xh = lax.axis_index("fsdp")
+        s.c = dp % 2; s.y = (dp // 2) % 4; s.xl = (dp // 8) % 2; s.z = dp // 16
+        s.x = s.xh * 2 + s.xl; s.h = s.y // 2; s.par = s.y % 2
+    def dev(s, x=None, y=None, z=None, c=None):
+        x = s.x if x is None else x; y = s.y if y is None else y
+        z = s.z if z is None else z; c = s.c if c is None else c
+        return (((z * 2 + x % 2) * 4 + y) * 2 + c, x // 2)
+    def ring(s, ax, d):
+        if ax == 0: return s.dev(x=(s.x + d) % 4)
+        if ax == 1: return s.dev(y=(s.y + d) % 4)
+        return s.dev(z=(s.z + d) % 4)
+    def coord(s, ax, d):
+        return ((s.x, s.y, s.z)[ax] + d) % 4
+
+class AG:
+
+    def __init__(s, p, W, stg, pieces, ssem, rsem, sib_r, s0s, s0r):
+        s.p, s.W, s.stg, s.pieces = p, W, stg, pieces
+        s.ssem, s.rsem, s.s0s, s.s0r = ssem, rsem, s0s, s0r
+    def partners(s):
+        p = s.p
+        out = []
+        for ax in range(3):
+            for d in (1, 2, 3): out.append(p.ring(ax, d))
+        for dy in (0, 1):
+            for dx in (0, 1):
+                for dc in (0, 1):
+                    if (dy, dx, dc) == (0, 0, 0): continue
+                    if (dy, dx, dc) == (0, 1, 0): continue
+                    y = p.y ^ dy if dy else p.y
+                    x = (p.x + 2 * dx) % 4
+                    out.append(p.dev(x=x, y=y, c=(p.c + dc) % 2))
+        return out
+    def s0_targets(s):
+        p = s.p
+        res = []
+        for dy in (0, 1):
+            for dx in (0, 1):
+                y = p.y ^ dy if dy else p.y
+                x = (p.x + 2 * dx) % 4
+                res.append((dy, dx, y, x))
+        return res
+    def s0_src(s):
+        p = s.p
+        return (p.par * 2 + p.c) * 2 + p.xh
+    def s0(s, ph, act):
+        p = s.p; o = s.s0_src()
+        for tc in (0, 1):
+            cond = (o <= 4) if tc == 0 else (o >= 4)
+            @pl.when(cond)
+            def _(tc=tc):
+                for i, (dy, dx, y, x) in enumerate(s.s0_targets()):
+                    chunk = (x // 2) * 2 + y % 2
+                    src = s.pieces.at[ph, chunk]
+                    dst = s.stg.at[ph, o - 4 * tc]
+                    if dy == 0 and dx == 0:
+                        @pl.when(p.c == tc)
+                        def _():
+                            cp = pltpu.make_async_copy(src, dst, s.s0r.at[ph, o - 4 * tc])
+                            if act == 'start': cp.start()
+                        @pl.when(p.c != tc)
+                        def _():
+                            cp = pltpu.make_async_remote_copy(src, dst, s.s0s.at[ph, i * 2 + tc], s.s0r.at[ph, o - 4 * tc], device_id=p.dev(y=y, x=x, c=tc), device_id_type=MESH)
+                            if act == 'start': cp.start()
+                            else: cp.wait_send()
+                    else:
+                        cp = pltpu.make_async_remote_copy(src, dst, s.s0s.at[ph, i * 2 + tc], s.s0r.at[ph, o - 4 * tc], device_id=p.dev(y=y, x=x, c=tc), device_id_type=MESH)
+                        if act == 'start': cp.start()
+                        else: cp.wait_send()
+    def s0_recv(s, ph):
+        p = s.p
+        for k in range(5):
+            def w(k=k):
+                pltpu.make_async_copy(s.pieces.at[ph, 0], s.stg.at[ph, k], s.s0r.at[ph, k]).wait()
+            if k < 4: w()
+            else: pl.when(p.c == 0)(w)
+    def compact(s, ph):
+        p = s.p
+        i = lax.broadcasted_iota(jnp.int32, (48, 80), 0)
+        k = lax.broadcasted_iota(jnp.int32, (48, 80), 1)
+        r = 48 * p.c + i
+        q = (r * 205) >> 11
+        col = (q - 4 * p.c) * 16 + (r - q * 10)
+        P = jnp.where(k == col, 1.0, 0.0).astype(jnp.bfloat16)
+        res = jnp.dot(P, s.stg[ph].reshape(80, CW), preferred_element_type=jnp.float32).astype(jnp.bfloat16)
+        def put(ts):
+            s.W[ph, p.xh, p.par, p.z, p.xl, p.h, 3 * p.c + ts] = res[ts * 16:(ts + 1) * 16]
+        put(0); put(1)
+        pl.when(p.c == 0)(lambda: put(2))
+    def order(s, ph, ts):
+        a = (ph + ts) % 3
+        return ((a + 1) % 3, (a + 2) % 3, a)
+    def region(s, ph, t, full, over=None):
+        p = s.p; o = over or {}
+        x = o.get(0); y = o.get(1); z = o.get(2)
+        xh, xl = (p.xh, p.xl) if x is None else (x // 2, x % 2)
+        h, par = (p.h, p.par) if y is None else (y // 2, y % 2)
+        zz = p.z if z is None else z
+        if 0 in full: xh = xl = slice(None)
+        if 1 in full: h = par = slice(None)
+        if 2 in full: zz = slice(None)
+        return [ph, xh, par, zz, xl, h, t]
+    def ref(s, reg): return s.W.at[tuple(reg)]
+    def cp(s, reg, slot, k, dev):
+        r = s.ref(reg)
+        return pltpu.make_async_remote_copy(r, r, s.ssem.at[slot, k], s.rsem.at[slot, k], device_id=dev, device_id_type=MESH)
+    def half(s, reg, full, hf):
+        reg = list(reg)
+        i = 3 if 2 in full else (1 if 0 in full else 2)
+        reg[i] = pl.ds(hf * 2, 2) if i == 3 else pl.ds(hf, 1)
+        return reg
+    def slot(s, ph, ts): return ph * 3 + ts
+    def t(s, ts): return 3 * s.p.c + ts
+    def g(s, ts, f):
+        if ts < 2: f()
+        else: pl.when(s.p.c == 0)(f)
+    def direct(s, stage, ph, ts, act):
+        a = s.order(ph, ts); full = a[:stage]; ax = a[stage]
+        for d in (1, 3, 2):
+            k = stage * 3 + d - 1
+            if act == 'recv':
+                s.cp(s.region(ph, s.t(ts), full, {ax: s.p.coord(ax, -d)}), s.slot(ph, ts), k, s.p.ring(ax, d)).wait_recv()
+            else:
+                c = s.cp(s.region(ph, s.t(ts), full), s.slot(ph, ts), k, s.p.ring(ax, d))
+                c.start() if act == 'start' else c.wait_send()
+    def s3(s, ph, ts, what, act):
+        a = s.order(ph, ts); full = a[:2]; ax = a[2]; sl = s.slot(ph, ts); tt = s.t(ts)
+        R, L = s.p.ring(ax, 1), s.p.ring(ax, 3)
+        own = s.region(ph, tt, full)
+        fl = s.region(ph, tt, full, {ax: s.p.coord(ax, -1)})
+        fr = s.region(ph, tt, full, {ax: s.p.coord(ax, 1)})
+        op = s.region(ph, tt, full, {ax: s.p.coord(ax, 2)})
+        if what == 'own':
+            if act == 'recvL': s.cp(fl, sl, 6, R).wait_recv()
+            elif act == 'recvR': s.cp(fr, sl, 7, L).wait_recv()
+            else:
+                for reg, k, dv in ((own, 6, R), (own, 7, L)):
+                    c = s.cp(reg, sl, k, dv)
+                    c.start() if act == 'start' else c.wait_send()
+        elif what == 'fwdR':
+            if act == 'recv': s.cp(s.half(op, full, 0), sl, 8, R).wait_recv()
+            else:
+                c = s.cp(s.half(fl, full, 0), sl, 8, R)
+                c.start() if act == 'start' else c.wait_send()
+        elif what == 'fwdL':
+            if act == 'recv': s.cp(s.half(op, full, 1), sl, 9, L).wait_recv()
+            else:
+                c = s.cp(s.half(fr, full, 1), sl, 9, L)
+                c.start() if act == 'start' else c.wait_send()
+    def sib(s, ph, ts, piece, act):
+        a = s.order(ph, ts); full = a[:2]; ax = a[2]
+        d = (0, -1, 1, 2)[piece]
+        dv = s.p.dev(c=1 - s.p.c)
+        t = s.t(ts) if act != 'recv' else 3 * (1 - s.p.c) + ts
+        c = s.cp(s.region(ph, t, full, {ax: s.p.coord(ax, d)}), s.slot(ph, ts), 10 + piece, dv)
+        if act == 'start': c.start()
+        elif act == 'recv': c.wait_recv()
+        else: c.wait_send()
+    def go(s, ts, f, other=False):
+        def h():
+            f()
+        if ts < 2: h()
+        else: pl.when(s.p.c == (1 if other else 0))(h)
+    def phase_a(s, ph):
+        for ts in range(3): s.go(ts, lambda ts=ts: s.direct(0, ph, ts, 'start'))
+    def phase_b(s, ph):
+        for ts in range(3):
+            s.go(ts, lambda ts=ts: (s.direct(0, ph, ts, 'recv'), s.direct(1, ph, ts, 'start')))
+    def phase_c(s, ph):
+        for ts in range(3):
+            s.go(ts, lambda ts=ts: (s.direct(1, ph, ts, 'recv'), s.s3(ph, ts, 'own', 'start'), s.sib(ph, ts, 0, 'start')))
+    def phase_d(s, ph):
+        for ts in range(3):
+            s.go(ts, lambda ts=ts: (
+                s.s3(ph, ts, 'own', 'recvL'), s.s3(ph, ts, 'fwdR', 'start'), s.sib(ph, ts, 1, 'start'),
+                s.s3(ph, ts, 'own', 'recvR'), s.s3(ph, ts, 'fwdL', 'start'), s.sib(ph, ts, 2, 'start')))
+    def phase_e(s, ph):
+        for ts in range(3):
+            s.go(ts, lambda ts=ts: (s.s3(ph, ts, 'fwdR', 'recv'), s.s3(ph, ts, 'fwdL', 'recv'), s.sib(ph, ts, 3, 'start')))
+    def phase_f(s, ph):
+        for ts in range(3):
+            s.go(ts, lambda ts=ts: [s.sib(ph, ts, k, 'recv') for k in range(4)], other=True)
+    def drain(s, ph):
+        s.s0(ph, 'wait_send')
+        for ts in range(3):
+            s.go(ts, lambda ts=ts: (s.direct(0, ph, ts, 'ws'), s.direct(1, ph, ts, 'ws'), s.s3(ph, ts, 'own', 'ws'),
+                 s.s3(ph, ts, 'fwdR', 'ws'), s.s3(ph, ts, 'fwdL', 'ws'), [s.sib(ph, ts, k, 'ws') for k in range(4)]))
+
+def barrier(partners):
+    b = pltpu.get_barrier_semaphore()
+    for d in partners:
+        pl.semaphore_signal(b, inc=1, device_id=d, device_id_type=MESH)
+    pl.semaphore_wait(b, len(partners))
+
+def ag_scratch():
+    return [
+        pltpu.VMEM((3, 2, 2, 4, 2, 2, 5, 16, CW), jnp.bfloat16),
+        pltpu.VMEM((3, 5, 16, CW), jnp.bfloat16),
+        pltpu.VMEM((3, 4, 16, CW), jnp.bfloat16),
+        pltpu.SemaphoreType.DMA((9, 14)),
+        pltpu.SemaphoreType.DMA((9, 14)),
+        pltpu.SemaphoreType.DMA((3, 8)),
+        pltpu.SemaphoreType.DMA((3, 5)),
+    ]
+def fill_pieces(pieces, wqkv, wout, wup, wdown):
+    mats = [(wqkv, 0), (wqkv, 1280), (wqkv, 2560), (wout, 0), (wup, 0), (wdown, 0)]
+    for ph in range(3):
+        for xh in range(2):
+            r, off = mats[2 * ph + xh]
+            for par in range(2):
+                v = r[:, off + par * 640: off + (par + 1) * 640]
+                pieces[ph, 2 * xh + par] = jnp.concatenate([v.astype(jnp.float32), jnp.zeros((6, 640), jnp.float32)], axis=0).astype(jnp.bfloat16)
+
+
+def gather_kernel(wq, wo, wu, wd, out, W, stg, pieces, ssem, rsem, s0s, s0r, osem):
+    p = Pos()
+    ag = AG(p, W, stg, pieces, ssem, rsem, None, s0s, s0r)
+    fill_pieces(pieces, wq, wo, wu, wd)
+    stg[...] = jnp.zeros_like(stg)
+    barrier(ag.partners())
+    for ph in range(3): ag.s0(ph, 'start')
+    for ph in range(3):
+        ag.s0_recv(ph); ag.compact(ph); ag.phase_a(ph)
+    for ph in range(3): ag.phase_b(ph)
+    for ph in range(3): ag.phase_c(ph)
+    for ph in range(3): ag.phase_d(ph)
+    for ph in range(3): ag.phase_e(ph)
+    for ph in range(3): ag.phase_f(ph)
+    for ph in range(3): ag.drain(ph)
+    cp = pltpu.make_async_copy(W, out, osem); cp.start(); cp.wait()
+
+
+def gather_all(wq, wo, wu, wd):
+    out = pl.pallas_call(gather_kernel, out_shape=jax.ShapeDtypeStruct((3,2,2,4,2,2,5,16,CW), jnp.bfloat16),
+        in_specs=[pl.BlockSpec(memory_space=pltpu.VMEM)]*4, out_specs=pl.BlockSpec(memory_space=pl.ANY),
+        scratch_shapes=ag_scratch()+[pltpu.SemaphoreType.DMA],
+        compiler_params=pltpu.CompilerParams(collective_id=0, has_side_effects=True, vmem_limit_bytes=56*2**20), name="gather_all")(wq, wo, wu, wd)
+    w = out.reshape(3, 4, 1280, CW)
+    panels = [jnp.concatenate([w[m // 2, 2 * (m % 2)], w[m // 2, 2 * (m % 2) + 1]], axis=1) for m in range(6)]
+    return jnp.concatenate(panels[:3], axis=1), panels[3], panels[4], panels[5]
 
 
 def layer_norm(inputs):
@@ -126,10 +376,9 @@
     small = jnp.concatenate(
         [gain_table, bias_one[:, None], gain_two[:, None], bias_two[:, None]], axis=1
     )
-    gathered = in_one_piece((w_qkv, w_out, w_up, w_down, small), ("dp", "fsdp"), 0, 1)
+    full_small, = in_one_piece((small,), ("dp", "fsdp"), 0, 1)
+    gathered = gather_all(w_qkv, w_out, w_up, w_down) + (full_small,)
     output, kept = forward_pass(latents, script_ids, gathered)
-    gathered = in_one_piece((w_qkv, w_out, w_up, w_down, small), ("dp", "fsdp"), 0, 1)
-    output_again, kept = forward_pass(latents, script_ids, gathered)
     full_qkv, full_out, full_up, full_down, full_small = gathered
     (
         one_hot,
@@ -235,13 +484,14 @@
         axis=1,
     )
     owned = (
-        lax.psum_scatter(qkv_grad, ("dp", "fsdp"), scatter_dimension=0, tiled=True),
-        lax.psum_scatter(out_grad, ("dp", "fsdp"), scatter_dimension=0, tiled=True),
-        lax.psum_scatter(up_grad, ("dp", "fsdp"), scatter_dimension=0, tiled=True),
-        lax.psum_scatter(down_grad, ("dp", "fsdp"), scatter_dimension=0, tiled=True),
+        lax.psum_scatter(qkv_grad.astype(jnp.bfloat16), ("dp", "fsdp"), scatter_dimension=0, tiled=True),
+        lax.psum_scatter(out_grad.astype(jnp.bfloat16), ("dp", "fsdp"), scatter_dimension=0, tiled=True),
+        lax.psum_scatter(up_grad.astype(jnp.bfloat16), ("dp", "fsdp"), scatter_dimension=0, tiled=True),
+        lax.psum_scatter(down_grad.astype(jnp.bfloat16), ("dp", "fsdp"), scatter_dimension=0, tiled=True),
         lax.psum_scatter(small_grad, ("dp", "fsdp"), scatter_dimension=0, tiled=True),
     )
     qkv_own, out_own, up_own, down_own, small_own = owned
+    qkv_own, out_own, up_own, down_own = (o.astype(jnp.float32) for o in (qkv_own, out_own, up_own, down_own))
     latents_out = output.reshape(items, length, width).astype(jnp.bfloat16)
     input_grad = input_grad.reshape(items, length, width)
     return (

time: 795 us -> 842 us (1.059)
  blocking collectives: 0 us -> 314 us
  waiting for transfers between devices: 646 us -> 340 us
  Pallas kernels: 0 us -> 66.8 us
  local copies, waits for them, and re-layouts: 56.4 us -> 36.9 us
  matrix products: 66.3 us -> 52.8 us
    all_gather x1 -> x0, waiting for transfers between devices: 348 us -> none  [in_one_piece(): whole = lax.all_gather(both, axis, axis=dim, tiled=True)]
    all_gather x0 -> x1, blocking collectives: none -> 314 us  [in_one_piece(): whole = lax.all_gather(both, axis, axis=dim, tiled=True)]
    pallas_call x0 -> x1, Pallas kernels: none -> 66.8 us  [gather_all(): pl.pallas_call(gather_kernel, out_shape=jax.ShapeDtypeStruct((3, 2, 2, 4,...]
    unnamed x3 -> x4, waiting for transfers between devices: 298 us -> 340 us
    unnamed x54 -> x70, local copies, waits for them, and re-layouts: 44 us -> 19.5 us
  transfers between devices with their start and end apart: 2 -> 2, of which waited for: 2 -> 2; matrix products, arithmetic and copies ran while one was open for 1% -> 3% of each run, Pallas kernels for 0% -> 0%
where the time goes in v1:
time: 842 us; the launch traced here: 841 us
  waiting for transfers between devices  340 us (40%)
  blocking collectives  314 us (37%)
  Pallas kernels  66.8 us (8%)
  matrix products  52.8 us (6%)
  local copies, waits for them, and re-layouts  36.9 us (4%)
  other arithmetic  15.7 us (2%)
  between operations  15.1 us (2%)
    unnamed x4, waiting for transfers between devices  340 us
    all_gather x1, blocking collectives, in_one_piece(): whole = lax.all_gather(both, axis, axis=dim, tiled=True)  314 us
    pallas_call x1, Pallas kernels, gather_all(): pl.pallas_call(gather_kernel, out_shape=jax.ShapeDtypeStruct((3, 2, 2, 4,...  66.8 us
    unnamed x70, local copies, waits for them, and re-layouts  19.5 us
  transfers between devices with their start and end apart: 2, of which 2 were waited for; matrix products, arithmetic and copies ran while one was open for 3% of the time, Pallas kernels for 0%

profile of v1, /device:TPU:1, one launch (start us, length us, event | category | flops | bytes accessed | tf_op | source)
XLA Modules:
  0.0 840.9 jit_solution(13769391874892612754)
XLA Ops:
  7.2 66.8 %gather_all.1 = bf16[3,2,2,4,2,2,5,16,640]{8,7,6,5,4,3,2,1,0:T(8,128)(2,1)} custom-call(bf16[10,3840]{1,0:T(8,128)(2,1)} %wq.1, bf16[10,1280]{1,0:T(8,128)(2,1)} %wo.1, bf16[10,1280]{1,0:T(8,128)(2,1)} %wu.1, bf16[10,1280]{1,0:T(8,128)(2,1)} %wd.1), custom_call_target="tpu_custom_call" | custom-call | tf_op jit(solution)/shard_map/gather_all/pallas_call | solution.py:263
  74.1 2.9 fusion.11
  77.0 7.2 slice_bitcast_fusion.1
  84.9 0.2 convert_reduce_fusion
  85.0 0.3 fusion.17
  85.4 0.1 copy.47
  85.5 0.1 copy.48
  85.6 0.1 copy.49
  85.7 0.1 maximum_bitcast_fusion
  85.8 313.8 %all-gather = bf16[128,10,19]{2,1,0:T(8,128)(2,1)S(1)} all-gather(bf16[1,10,19]{2,1,0:T(8,128)(2,1)S(1)} %maximum_bitcast_fusion), channel_id=1, replica_groups=mesh['dp'=64,'fsdp'=2] {'dp','fsdp'}, dimensions={0}, use_global_device_ids=true | all-gather | bytes 49020 | tf_op jit(solution)/shard_map/all_gather | solution.py:21
  399.6 0.2 reshape.214
  399.8 0.2 copy.64
  400.0 0.1 convolution_reduce_fusion
  400.1 2.8 fusion.10
  403.0 2.9 fusion.9
  405.8 2.9 fusion.8
  408.7 2.8 fusion.7
  411.5 2.9 fusion.6
  414.4 1.4 fusion.13
  415.8 0.8 copy-done.19
  416.6 7.7 convolution_convert_fusion.4
  424.4 2.7 copy.51
  427.1 2.2 fusion.63
  429.3 2.1 convolution_convert_fusion.7
  431.4 0.4 copy-done.10
  431.8 1.1 fusion.64
  433.0 0.3 multiply_reduce_fusion.4
  433.3 0.3 add_convert_fusion
  433.6 1.3 copy-done.11
  434.9 0.5 copy-done.12
  435.4 2.1 multiply_convert_fusion.1
  437.5 2.1 fusion.24
  439.6 1.2 multiply_reduce_fusion.6
  440.9 1.5 fusion.62
  442.4 0.8 copy-done.17
  443.2 1.9 convolution_convert_fusion.5
  445.1 2.2 copy.54
  447.3 3.3 convolution_convert_fusion.6
  450.6 0.6 multiply_reduce_fusion
  451.1 0.4 multiply_convert_fusion
  451.5 1.3 fusion.16
  452.8 1.2 fusion.15
  454.0 1.2 fusion.27
  455.3 7.5 multiply_reduce_fusion.5
  462.7 0.1 dynamic-slice_reduce_fusion.1
  462.8 0.5 fusion.28
  463.3 0.7 pad_maximum_fusion.12
  464.1 1.7 pad_maximum_fusion.9
  465.8 0.1 copy-done.26
  466.0 2.8 convolution_convert_fusion.2
  468.8 2.7 convolution_convert_fusion.3
  471.5 5.5 convolution_convert_fusion
  477.1 2.7 convolution_convert_fusion.1
  479.9 4.1 fusion.2
  484.0 1.5 add_bitcast_fusion
  485.5 114.6 %all-reduce.9.cloned.1.call-done = f32[1280,19]{0,1:T(8,128)} async-done(((f32[1280,19]{0,1:T(8,128)}), f32[1280,19]{0,1:T(8,128)}) %all-reduce.9.cloned.1.call-update) | async-done | bytes 97296
  600.1 0.8 constant_dynamic-slice_fusion
  600.9 0.7 copy.58
  601.5 1.4 dynamic-slice_bitcast_fusion
  602.9 225.0 %all-reduce.11.cloned.1.call-done = (bf16[1280,3840]{1,0:T(8,128)(2,1)}, bf16[1280,1280]{1,0:T(8,128)(2,1)}, bf16[1280,1280]{1,0:T(8,128)(2,1)}, bf16[1280,1280]{1,0:T(8,128)(2,1)}) async-done(((bf16[1280,3840]{1,0:T(8,128)(2,1)}, bf16[1280,1280]{1,0:T(8,128)(2,1)}, bf16[1280,1280]{1,0:T(8,128)(2,1)}, bf16[1280,1280]{1,0:T(8,128)(2,1)}), (bf16[1280,3840]{1,0:T(8,128)(2,1)}, bf16[1280,1280]{1,0:T(8,128)(2,1)}, ...) | async-done | bytes 19660816
  827.9 1.6 dynamic-slice_convert_fusion
  829.6 1.5 dynamic-slice_convert_fusion.3
  831.1 1.5 dynamic-slice_convert_fusion.2
  832.5 1.5 dynamic-slice_convert_fusion.1
  (73 shorter events, 0.3 us)
Async XLA Ops:
  7.2 592.9 %all-reduce.9.cloned.1.call-start = ((), (), s32[]{:S(2)}) async-start(), calls=%async_computation | async-start | bytes 245760
  77.0 7.8 copy-start
  77.0 8.4 copy-start.28
  77.0 8.5 %copy-start.29 = (bf16[10]{0:T(256)(128)(2,1)S(1)}, bf16[10]{0:T(256)(128)(2,1)}, u32[]{:S(2)}) copy-start(bf16[10]{0:T(256)(128)(2,1)} %param.17) | copy-start | bytes 64
  77.0 8.6 %copy-start.30 = (bf16[10]{0:T(256)(128)(2,1)S(1)}, bf16[10]{0:T(256)(128)(2,1)}, u32[]{:S(2)}) copy-start(bf16[10]{0:T(256)(128)(2,1)} %param.18) | copy-start | bytes 64
  77.0 8.7 %copy-start.27 = (bf16[10,16]{1,0:T(8,128)(2,1)S(1)}, bf16[10,16]{1,0:T(8,128)(2,1)}, u32[]{:S(2)}) copy-start(bf16[10,16]{1,0:T(8,128)(2,1)} %param.13) | copy-start | bytes 964
  415.8 0.8 copy-start.19
  427.1 2.2 copy-start.1
  429.3 2.1 copy-start.9
  429.3 2.6 copy-start.10
  431.4 1.6 copy-start.23
  433.3 1.7 copy-start.11
  433.3 2.2 copy-start.12
  433.6 3.9 copy-start.13
  435.4 2.1 copy-start.7
  435.4 2.1 copy-start.8
  435.4 2.1 copy-start.15
  439.6 1.2 copy-start.25
  440.8 1.5 copy-start.5
  442.4 0.8 copy-start.17
  447.3 3.3 copy-start.2
  447.3 3.3 copy-start.6
  447.3 3.3 copy-start.21
  455.3 7.6 copy-start.4
  464.0 363.9 %all-reduce.11.cloned.1.call-start = ((), (), s32[]{:S(2)}) async-start(), calls=%async_computation.1 | async-start | bytes 39321600
  464.1 1.7 copy-start.14
  464.1 1.9 copy-start.26
  466.0 2.8 copy-start.18
  466.0 2.8 copy-start.24
  468.7 2.7 copy-start.20
  471.5 5.6 copy-start.16
  471.5 5.6 copy-start.22
  479.9 4.1 copy-start.3
Sparse Core Ops, SparseCore 0:
  464.1 135.8 all-reduce.8
  607.3 220.5 all-reduce.10

commit v2 on v1

v2 whole, which is shorter than its diff:
```python
import math

import jax
import jax.numpy as jnp
from jax import lax
from jax.experimental import pallas as pl
from jax.experimental.pallas import tpu as pltpu
from jax.sharding import PartitionSpec as P

HEADS = 8
HD = 160
D = 1280
L = 256
EPS = 1e-5
SCALE = 1.0 / math.sqrt(HD)
BF = jnp.bfloat16
F32 = jnp.float32

MESH = pl.DeviceIdType.MESH
CW = 640

class Pos:
    def __init__(s):
        dp = lax.axis_index("dp"); s.xh = lax.axis_index("fsdp")
        s.c = dp % 2; s.y = (dp // 2) % 4; s.xl = (dp // 8) % 2; s.z = dp // 16
        s.x = s.xh * 2 + s.xl; s.h = s.y // 2; s.par = s.y % 2
    def dev(s, x=None, y=None, z=None, c=None):
        x = s.x if x is None else x; y = s.y if y is None else y
        z = s.z if z is None else z; c = s.c if c is None else c
        return (((z * 2 + x % 2) * 4 + y) * 2 + c, x // 2)
    def ring(s, ax, d):
        if ax == 0: return s.dev(x=(s.x + d) % 4)
        if ax == 1: return s.dev(y=(s.y + d) % 4)
        return s.dev(z=(s.z + d) % 4)
    def coord(s, ax, d):
        return ((s.x, s.y, s.z)[ax] + d) % 4

class AG:
    def __init__(s, p, W, stg, pieces, ssem, rsem, sib_r, s0s, s0r):
        s.p, s.W, s.stg, s.pieces = p, W, stg, pieces
        s.ssem, s.rsem, s.s0s, s.s0r = ssem, rsem, s0s, s0r
    def partners(s):
        p = s.p
        out = []
        for ax in range(3):
            for d in (1, 2, 3): out.append(p.ring(ax, d))
        for dy in (0, 1):
            for dx in (0, 1):
                for dc in (0, 1):
                    if (dy, dx, dc) == (0, 0, 0): continue
                    if (dy, dx, dc) == (0, 1, 0): continue
                    y = p.y ^ dy if dy else p.y
                    x = (p.x + 2 * dx) % 4
                    out.append(p.dev(x=x, y=y, c=(p.c + dc) % 2))
        return out
    def s0_targets(s):
        p = s.p
        res = []
        for dy in (0, 1):
            for dx in (0, 1):
                y = p.y ^ dy if dy else p.y
                x = (p.x + 2 * dx) % 4
                res.append((dy, dx, y, x))
        return res
    def s0_src(s):
        p = s.p
        return (p.par * 2 + p.c) * 2 + p.xh
    def s0(s, ph, act):
        p = s.p; o = s.s0_src()
        for tc in (0, 1):
            cond = (o <= 4) if tc == 0 else (o >= 4)
            @pl.when(cond)
            def _(tc=tc):
                for i, (dy, dx, y, x) in enumerate(s.s0_targets()):
                    chunk = (x // 2) * 2 + y % 2
                    src = s.pieces.at[ph, chunk]
                    dst = s.stg.at[ph, o - 4 * tc]
                    if dy == 0 and dx == 0:
                        @pl.when(p.c == tc)
                        def _():
                            cp = pltpu.make_async_copy(src, dst, s.s0r.at[ph, o - 4 * tc])
                            if act == 'start': cp.start()
                        @pl.when(p.c != tc)
                        def _():
                            cp = pltpu.make_async_remote_copy(src, dst, s.s0s.at[ph, i * 2 + tc], s.s0r.at[ph, o - 4 * tc], device_id=p.dev(y=y, x=x, c=tc), device_id_type=MESH)
                            if act == 'start': cp.start()
                            else: cp.wait_send()
                    else:
                        cp = pltpu.make_async_remote_copy(src, dst, s.s0s.at[ph, i * 2 + tc], s.s0r.at[ph, o - 4 * tc], device_id=p.dev(y=y, x=x, c=tc), device_id_type=MESH)
                        if act == 'start': cp.start()
                        else: cp.wait_send()
    def s0_recv(s, ph):
        p = s.p
        for k in range(5):
            def w(k=k):
                pltpu.make_async_copy(s.pieces.at[ph, 0], s.stg.at[ph, k], s.s0r.at[ph, k]).wait()
            if k < 4: w()
            else: pl.when(p.c == 0)(w)
    def compact(s, ph):
        p = s.p
        i = lax.broadcasted_iota(jnp.int32, (48, 80), 0)
        k = lax.broadcasted_iota(jnp.int32, (48, 80), 1)
        r = 48 * p.c + i
        q = (r * 205) >> 11
        col = (q - 4 * p.c) * 16 + (r - q * 10)
        P = jnp.where(k == col, 1.0, 0.0).astype(jnp.bfloat16)
        res = jnp.dot(P, s.stg[ph].reshape(80, CW), preferred_element_type=jnp.float32).astype(jnp.bfloat16)
        def put(ts):
            s.W[ph, p.xh, p.par, p.z, p.xl, p.h, 3 * p.c + ts] = res[ts * 16:(ts + 1) * 16]
        put(0); put(1)
        pl.when(p.c == 0)(lambda: put(2))
    def order(s, ph, ts):
        a = (ph + ts) % 3
        return ((a + 1) % 3, (a + 2) % 3, a)
    def region(s, ph, t, full, over=None):
        p = s.p; o = over or {}
        x = o.get(0); y = o.get(1); z = o.get(2)
        xh, xl = (p.xh, p.xl) if x is None else (x // 2, x % 2)
        h, par = (p.h, p.par) if y is None else (y // 2, y % 2)
        zz = p.z if z is None else z
        if 0 in full: xh = xl = slice(None)
        if 1 in full: h = par = slice(None)
        if 2 in full: zz = slice(None)
        return [ph, xh, par, zz, xl, h, t]
    def ref(s, reg): return s.W.at[tuple(reg)]
    def cp(s, reg, slot, k, dev):
        r = s.ref(reg)
        return pltpu.make_async_remote_copy(r, r, s.ssem.at[slot, k], s.rsem.at[slot, k], device_id=dev, device_id_type=MESH)
    def half(s, reg, full, hf):
        reg = list(reg)
        i = 3 if 2 in full else (1 if 0 in full else 2)
        reg[i] = pl.ds(hf * 2, 2) if i == 3 else pl.ds(hf, 1)
        return reg
    def slot(s, ph, ts): return ph * 3 + ts
    def t(s, ts): return 3 * s.p.c + ts
    def g(s, ts, f):
        if ts < 2: f()
        else: pl.when(s.p.c == 0)(f)
    def direct(s, stage, ph, ts, act):
        a = s.order(ph, ts); full = a[:stage]; ax = a[stage]
        for d in (1, 3, 2):
            k = stage * 3 + d - 1
            if act == 'recv':
                s.cp(s.region(ph, s.t(ts), full, {ax: s.p.coord(ax, -d)}), s.slot(ph, ts), k, s.p.ring(ax, d)).wait_recv()
            else:
                c = s.cp(s.region(ph, s.t(ts), full), s.slot(ph, ts), k, s.p.ring(ax, d))
                c.start() if act == 'start' else c.wait_send()
    def s3(s, ph, ts, what, act):
        a = s.order(ph, ts); full = a[:2]; ax = a[2]; sl = s.slot(ph, ts); tt = s.t(ts)
        R, L = s.p.ring(ax, 1), s.p.ring(ax, 3)
        own = s.region(ph, tt, full)
        fl = s.region(ph, tt, full, {ax: s.p.coord(ax, -1)})
        fr = s.region(ph, tt, full, {ax: s.p.coord(ax, 1)})
        op = s.region(ph, tt, full, {ax: s.p.coord(ax, 2)})
        if what == 'own':
            if act == 'recvL': s.cp(fl, sl, 6, R).wait_recv()
            elif act == 'recvR': s.cp(fr, sl, 7, L).wait_recv()
            else:
                for reg, k, dv in ((own, 6, R), (own, 7, L)):
                    c = s.cp(reg, sl, k, dv)
                    c.start() if act == 'start' else c.wait_send()
        elif what == 'fwdR':
            if act == 'recv': s.cp(s.half(op, full, 0), sl, 8, R).wait_recv()
            else:
                c = s.cp(s.half(fl, full, 0), sl, 8, R)
                c.start() if act == 'start' else c.wait_send()
        elif what == 'fwdL':
            if act == 'recv': s.cp(s.half(op, full, 1), sl, 9, L).wait_recv()
            else:
                c = s.cp(s.half(fr, full, 1), sl, 9, L)
                c.start() if act == 'start' else c.wait_send()
    def sib(s, ph, ts, piece, act):
        a = s.order(ph, ts); full = a[:2]; ax = a[2]
        d = (0, -1, 1, 2)[piece]
        dv = s.p.dev(c=1 - s.p.c)
        t = s.t(ts) if act != 'recv' else 3 * (1 - s.p.c) + ts
        c = s.cp(s.region(ph, t, full, {ax: s.p.coord(ax, d)}), s.slot(ph, ts), 10 + piece, dv)
        if act == 'start': c.start()
        elif act == 'recv': c.wait_recv()
        else: c.wait_send()
    def go(s, ts, f, other=False):
        def h():
            f()
        if ts < 2: h()
        else: pl.when(s.p.c == (1 if other else 0))(h)
    def phase_a(s, ph):
        for ts in range(3): s.go(ts, lambda ts=ts: s.direct(0, ph, ts, 'start'))
    def phase_b(s, ph):
        for ts in range(3):
            s.go(ts, lambda ts=ts: (s.direct(0, ph, ts, 'recv'), s.direct(1, ph, ts, 'start')))
    def phase_c(s, ph):
        for ts in range(3):
            s.go(ts, lambda ts=ts: (s.direct(1, ph, ts, 'recv'), s.s3(ph, ts, 'own', 'start'), s.sib(ph, ts, 0, 'start')))
    def phase_d(s, ph):
        for ts in range(3):
            s.go(ts, lambda ts=ts: (
                s.s3(ph, ts, 'own', 'recvL'), s.s3(ph, ts, 'fwdR', 'start'), s.sib(ph, ts, 1, 'start'),
                s.s3(ph, ts, 'own', 'recvR'), s.s3(ph, ts, 'fwdL', 'start'), s.sib(ph, ts, 2, 'start')))
    def phase_e(s, ph):
        for ts in range(3):
            s.go(ts, lambda ts=ts: (s.s3(ph, ts, 'fwdR', 'recv'), s.s3(ph, ts, 'fwdL', 'recv'), s.sib(ph, ts, 3, 'start')))
    def phase_f(s, ph):
        for ts in range(3):
            s.go(ts, lambda ts=ts: [s.sib(ph, ts, k, 'recv') for k in range(4)], other=True)
    def drain(s, ph):
        s.s0(ph, 'wait_send')
        for ts in range(3):
            s.go(ts, lambda ts=ts: (s.direct(0, ph, ts, 'ws'), s.direct(1, ph, ts, 'ws'), s.s3(ph, ts, 'own', 'ws'),
                 s.s3(ph, ts, 'fwdR', 'ws'), s.s3(ph, ts, 'fwdL', 'ws'), [s.sib(ph, ts, k, 'ws') for k in range(4)]))

def barrier(partners):
    b = pltpu.get_barrier_semaphore()
    for d in partners:
        pl.semaphore_signal(b, inc=1, device_id=d, device_id_type=MESH)
    pl.semaphore_wait(b, len(partners))

def fill_pieces(pieces, wqkv, wout, wup, wdown):
    mats = [(wqkv, 0), (wqkv, 1280), (wqkv, 2560), (wout, 0), (wup, 0), (wdown, 0)]
    for ph in range(3):
        for xh in range(2):
            r, off = mats[2 * ph + xh]
            for par in range(2):
                v = r[:, off + par * 640: off + (par + 1) * 640]
                pieces[ph, 2 * xh + par] = jnp.concatenate([v.astype(jnp.float32), jnp.zeros((6, 640), jnp.float32)], axis=0).astype(jnp.bfloat16)


def dot(a, b):
    return jnp.dot(a, b, preferred_element_type=F32)


def dot_nt(a, b):
    return lax.dot_general(a, b, (((1,), (1,)), ((), ())), preferred_element_type=F32)


def dot_tn(a, b):
    return lax.dot_general(a, b, (((0,), (0,)), ((), ())), preferred_element_type=F32)


class Small:
    def __init__(s, p, buf, recv, ssem, rsem, rings):
        s.p, s.buf, s.recv, s.ssem, s.rsem, s.rings = p, buf, recv, ssem, rsem, rings

    def cps(s, k):
        p = s.p
        n = len(s.rings)
        if k == 0 or k == n + 1:
            src = s.buf.at[1 - p.c] if k == 0 else s.buf.at[p.c]
            dst = s.recv.at[0, 0] if k == 0 else s.recv.at[0, 1]
            return [pltpu.make_async_remote_copy(src, dst, s.ssem.at[k, 0], s.rsem.at[k, 0], device_id=p.dev(c=1 - p.c), device_id_type=MESH)]
        return [pltpu.make_async_remote_copy(s.buf.at[p.c], s.recv.at[k, i], s.ssem.at[k, i], s.rsem.at[k, i], device_id=dv, device_id_type=MESH)
                for i, dv in enumerate(s.rings[k - 1])]

    def start(s, k):
        for c in s.cps(k): c.start()

    def finish(s, k):
        p = s.p
        n = len(s.rings)
        cs = s.cps(k)
        if k == n + 1:
            cs[0].wait_recv()
            cs[0].wait_send()
            s.buf[1 - p.c] = s.recv[0, 1]
            return
        for c in cs: c.wait_recv()
        for c in cs: c.wait_send()
        acc = s.buf[p.c].astype(F32)
        for i in range(len(cs)):
            acc = acc + s.recv[k, i].astype(F32)
        s.buf[p.c] = acc.astype(s.buf.dtype)


class RS:
    def __init__(s, p, G, RD, bufs, FR, EX, FIN, dss, drs, ss, rs, fs, fr):
        s.p, s.G, s.RD, s.bufs, s.FR, s.EX, s.FIN = p, G, RD, bufs, FR, EX, FIN
        s.dss, s.drs, s.ss, s.rs, s.fs, s.fr = dss, drs, ss, rs, fs, fr

    def gref(s, ph):
        return s.G[ph]

    def go(s, ts, f, other=False):
        def h():
            f()
        if ts < 2: h()
        else: pl.when(s.p.c == (1 if other else 0))(h)

    def d2d(s, ph, ts, act):
        p = s.p
        g = s.gref(ph)
        t = 3 * (1 - p.c) + ts if act != 'recv' else 3 * p.c + ts
        for par in range(2):
            cp = pltpu.make_async_remote_copy(g.at[par, :, :, :, t], s.RD.at[ph, ts, par], s.dss.at[ph * 3 + ts, par], s.drs.at[ph * 3 + ts, par], device_id=p.dev(c=1 - p.c), device_id_type=MESH)
            if act == 'start': cp.start()
            elif act == 'ws': cp.wait_send()
            else: cp.wait_recv()

    def d2d_start(s, ph):
        for ts in range(3): s.go(ts, lambda ts=ts: s.d2d(ph, ts, 'start'), other=True)

    def d2d_add(s, ph, ts):
        g = s.gref(ph)
        t = 3 * s.p.c + ts
        s.d2d(ph, ts, 'recv')
        for par in range(2):
            def body(z, _):
                g[par, z, :, :, t] = (g[par, z, :, :, t].astype(F32) + s.RD[ph, ts, par, z].astype(F32)).astype(BF)
                return 0
            lax.fori_loop(0, 4, body, 0)

    def order(s, ph, ts):
        f = (ph + ts) % 3
        return ((0, 1, 2), (1, 2, 0), (2, 1, 0))[f]

    def fidx(s, ph, ts):
        return (ph + ts) % 3

    def piece(s, ph, ts, st, k):
        p = s.p
        o = s.order(ph, ts)
        ax = o[st]
        done = o[:st]
        par = h = zz = xl = slice(None)
        if 0 in done: xl = p.xl
        if 1 in done: h, par = p.h, p.par
        if 2 in done: zz = p.z
        if ax == 0: xl = k
        if ax == 1: h, par = k // 2, k % 2
        if ax == 2: zz = k
        return s.gref(ph).at[par, zz, xl, h, 3 * p.c + ts]

    def half(s, ph, ts, st, k, hf):
        p = s.p
        o = s.order(ph, ts)
        ax = o[st]
        assert st == 0
        t = 3 * p.c + ts
        if ax == 1: return s.gref(ph).at[k % 2, pl.ds(2 * hf, 2), :, k // 2, t]
        return s.gref(ph).at[hf, k, :, :, t]

    def bhalf(s, ph, ts, hf):
        f = s.fidx(ph, ts)
        b = s.bufs[f][0]
        if f == 1: return b.at[ph, 2, pl.ds(2 * hf, 2)]
        return b.at[ph, 2, hf]

    def cp(s, src, dst, sl, k, dev):
        return pltpu.make_async_remote_copy(src, dst, s.ss.at[sl, k], s.rs.at[sl, k], device_id=dev, device_id_type=MESH)

    def add(s, dst, srcs):
        lead = dst.shape[:-2]
        if len(lead) >= 1 and lead[0] > 1:
            def body(i, _):
                acc = dst[i].astype(F32)
                for r in srcs: acc = acc + r[i].astype(F32)
                dst[i] = acc.astype(BF)
                return 0
            lax.fori_loop(0, lead[0], body, 0)
        else:
            acc = dst[...].astype(F32)
            for r in srcs: acc = acc + r[...].astype(F32)
            dst[...] = acc.astype(BF)

    def sem(s, st, i):
        return (0, 4, 7)[st] + i

    def ring_cps(s, ph, ts, st):
        p = s.p
        o = s.order(ph, ts)
        ax = o[st]
        f = s.fidx(ph, ts)
        sl = ph * 3 + ts
        b = s.bufs[f][st]
        if ax == 0:
            k = 1 - p.xl
            return [s.cp(s.piece(ph, ts, st, k), b.at[ph, 0], sl, s.sem(st, 0), p.dev(x=p.xh * 2 + k))]
        res = []
        for i, d in enumerate((1, 3, 2)):
            res.append(s.cp(s.piece(ph, ts, st, p.coord(ax, d)), b.at[ph, i], sl, s.sem(st, i), p.ring(ax, d)))
        return res

    def first_a(s, ph, ts):
        if s.order(ph, ts)[0] == 0:
            for c in s.ring_cps(ph, ts, 0): c.start()
            return
        for c in s.sf_half(ph, ts): c.start()

    def sf_half(s, ph, ts):
        p = s.p
        ax = s.order(ph, ts)[0]
        sl = ph * 3 + ts
        k = p.coord(ax, 2)
        return [s.cp(s.half(ph, ts, 0, k, 1), s.bhalf(ph, ts, 1), sl, 2, p.ring(ax, 1)),
                s.cp(s.half(ph, ts, 0, k, 0), s.bhalf(ph, ts, 0), sl, 3, p.ring(ax, 3))]

    def sf_full(s, ph, ts):
        p = s.p
        ax = s.order(ph, ts)[0]
        sl = ph * 3 + ts
        b = s.bufs[s.fidx(ph, ts)][0]
        return [s.cp(s.piece(ph, ts, 0, p.coord(ax, 1)), b.at[ph, 0], sl, 0, p.ring(ax, 1)),
                s.cp(s.piece(ph, ts, 0, p.coord(ax, 3)), b.at[ph, 1], sl, 1, p.ring(ax, 3))]

    def first_b(s, ph, ts):
        p = s.p
        o = s.order(ph, ts)
        ax = o[0]
        if ax == 0: return
        hb = s.sf_half(ph, ts)
        full = s.sf_full(ph, ts)
        hb[0].wait_recv()
        s.add(s.half(ph, ts, 0, p.coord(ax, 1), 1), [s.bhalf(ph, ts, 1)])
        full[0].start()
        hb[1].wait_recv()
        s.add(s.half(ph, ts, 0, p.coord(ax, 3), 0), [s.bhalf(ph, ts, 0)])
        full[1].start()

    def first_c(s, ph, ts):
        p = s.p
        o = s.order(ph, ts)
        ax = o[0]
        me = (p.xl, p.y, p.z)[ax]
        b = s.bufs[s.fidx(ph, ts)][0]
        cs = s.ring_cps(ph, ts, 0) if ax == 0 else s.sf_full(ph, ts)
        for c in cs: c.wait_recv()
        s.add(s.piece(ph, ts, 0, me), [b.at[ph, i] for i in range(len(cs))])

    def next_start(s, ph, ts, st):
        for c in s.ring_cps(ph, ts, st): c.start()

    def next_finish(s, ph, ts, st):
        p = s.p
        ax = s.order(ph, ts)[st]
        me = (p.xl, p.y, p.z)[ax]
        b = s.bufs[s.fidx(ph, ts)][st]
        cs = s.ring_cps(ph, ts, st)
        for c in cs: c.wait_recv()
        s.add(s.piece(ph, ts, st, me), [b.at[ph, i] for i in range(len(cs))])

    def each(s, f):
        for ts in range(3): s.go(ts, lambda ts=ts: f(ts))

    def step(s, ph, k):
        if k == 0: s.d2d_start(ph)
        elif k == 1: s.each(lambda ts: (s.d2d_add(ph, ts), s.first_a(ph, ts)))
        elif k == 2: s.each(lambda ts: s.first_b(ph, ts))
        elif k == 3: s.each(lambda ts: (s.first_c(ph, ts), s.next_start(ph, ts, 1)))
        elif k == 4: s.each(lambda ts: (s.next_finish(ph, ts, 1), s.next_start(ph, ts, 2)))
        elif k == 5:
            s.each(lambda ts: s.next_finish(ph, ts, 2))
            s.final_start(ph)

    def fin_cps(s, ph, k):
        p = s.p
        o = 4 * p.c + k
        chunk = 2 * p.xh + p.par
        dev = p.dev(x=(o % 2) * 2 + p.xl, y=2 * p.h + o // 4, c=(o // 2) % 2)
        return pltpu.make_async_remote_copy(s.EX.at[ph, k], s.FIN.at[ph, chunk, p.c], s.fs.at[ph, k], s.fr.at[ph, chunk * 2 + p.c], device_id=dev, device_id_type=MESH)

    def myo(s):
        p = s.p
        return (p.par * 2 + p.c) * 2 + p.xh

    def final_start(s, ph):
        p = s.p
        g = s.gref(ph)
        def put(ts):
            s.FR[ts] = g[p.par, p.z, p.xl, p.h, 3 * p.c + ts]
        put(0); put(1)
        pl.when(p.c == 0)(lambda: put(2))
        i = lax.broadcasted_iota(jnp.int32, (80, 48), 1)
        k = lax.broadcasted_iota(jnp.int32, (80, 48), 0)
        r = 48 * p.c + i
        q = (r * 205) >> 11
        col = (q - 4 * p.c) * 16 + (r - q * 10)
        pt = jnp.where(k == col, 1.0, 0.0).astype(BF)
        s.EX[ph] = dot(pt, s.FR[...].reshape(48, CW)).astype(BF).reshape(5, 16, CW)
        for k in range(5):
            def send(k=k):
                me = 4 * p.c + k == s.myo()
                @pl.when(me)
                def _():
                    s.FIN[ph, 2 * p.xh + p.par, p.c] = s.EX[ph, k]
                @pl.when(jnp.logical_not(me))
                def _():
                    s.fin_cps(ph, k).start()
            if k < 4: send()
            else: pl.when(p.c == 0)(send)

    def final_wait(s, ph):
        p = s.p
        o = s.myo()
        for chunk in range(4):
            for sc in range(2):
                c1 = (o <= 4) if sc == 0 else (o >= 4)
                mine = jnp.logical_and(chunk == 2 * p.xh + p.par, sc == p.c)
                @pl.when(jnp.logical_and(c1, jnp.logical_not(mine)))
                def _(chunk=chunk, sc=sc):
                    pltpu.make_async_remote_copy(s.EX.at[ph, 0], s.FIN.at[ph, chunk, sc], s.fs.at[ph, 0], s.fr.at[ph, chunk * 2 + sc], device_id=p.dev(c=1 - p.c), device_id_type=MESH).wait_recv()

    def drain(s, ph):
        p = s.p
        for ts in range(3):
            s.go(ts, lambda ts=ts: s.d2d(ph, ts, 'ws'), other=True)
            def ws(ts=ts):
                if s.order(ph, ts)[0] == 0:
                    for c in s.ring_cps(ph, ts, 0): c.wait_send()
                else:
                    for c in s.sf_half(ph, ts) + s.sf_full(ph, ts): c.wait_send()
                for st in (1, 2):
                    for c in s.ring_cps(ph, ts, st): c.wait_send()
            s.go(ts, ws)
        for k in range(5):
            def w(k=k):
                pl.when(4 * p.c + k != s.myo())(lambda: s.fin_cps(ph, k).wait_send())
            if k < 4: w()
            else: pl.when(p.c == 0)(w)


FIRST, Q, K, V, MIXED, SECOND, ACTIVE, GU, GAO, GMX, GQ, GK, GV = range(13)
RB = 32


def block_kernel(lat, cot, sid, small, wq, wo, wu, wd, o_lat, o_in, o_small, o_qkv, o_out, o_up, o_down,
                 W, stg, pieces, A, N1, N2, MID, DG, PR, I1, I2, VEC, CS, G2, RD, b00, b01, b02, b10, b11, b12, b20, b21, b22,
                 FR, EX, FIN, SB, SBR, SG, SGR,
                 ssem, rsem, s0s, s0r, dss, drs, gss, grs, fs, fr, sbs, sbr, sgs, sgr):
    p = Pos()
    ag = AG(p, W, stg, pieces, ssem, rsem, None, s0s, s0r)
    G = [W.at[2, 0], W.at[2, 1], G2]
    rs = RS(p, G, RD, [[b00, b01, b02], [b10, b11, b12], [b20, b21, b22]], FR, EX, FIN, dss, drs, gss, grs, fs, fr)
    ring3 = lambda ax: [p.ring(ax, d) for d in (1, 3, 2)]
    sb = Small(p, SB, SBR, sbs, sbr, [ring3(0), ring3(1), ring3(2)])
    sg = Small(p, SG, SGR, sgs, sgr, [ring3(1), ring3(2), [p.dev(x=p.xh * 2 + 1 - p.xl)]])
    idx = lax.axis_index("dp") * 2 + p.xh

    parts = ag.partners()
    bar = pltpu.get_barrier_semaphore()
    fill_pieces(pieces, wq, wo, wu, wd)
    stg[...] = jnp.zeros_like(stg)
    FIN[...] = jnp.zeros_like(FIN)
    FR[...] = jnp.zeros_like(FR)
    for d in parts:
        pl.semaphore_signal(bar, inc=1, device_id=d, device_id_type=MESH)
    j = lax.broadcasted_iota(jnp.int32, (16, D), 0)
    lane = lax.broadcasted_iota(jnp.int32, (16, D), 1)
    own = jnp.where(jnp.logical_and(lane == idx * 10 + j, j < 10), 1.0, 0.0)
    spread = dot_tn(small[...], own.astype(BF)).astype(BF)
    for k in range(2): SB[k] = spread[:, k * 640:(k + 1) * 640]
    pl.semaphore_wait(bar, len(parts))

    for ph in range(3): ag.s0(ph, 'start')
    sb.start(0)

    def ln1(r, _):
        rows = pl.ds(pl.multiple_of(r * RB, RB), RB)
        x = lat[rows, :].astype(F32)
        mu = jnp.mean(x, axis=-1, keepdims=True)
        xc = x - mu
        inv = lax.rsqrt(jnp.mean(xc * xc, axis=-1, keepdims=True) + EPS)
        N1[rows, :] = xc * inv
        I1[rows, :] = jnp.broadcast_to(inv, (RB, 128))
        return 0
    lax.fori_loop(0, L // RB, ln1, 0)
    A[MIXED] = jnp.zeros((L, D), BF)
    for k in (GQ, GK, GV): A[k] = jnp.zeros((L, D), BF)
    CS[...] = jnp.zeros_like(CS)

    sb.finish(0); sb.start(1)
    for ph in range(3):
        ag.s0_recv(ph); ag.compact(ph); ag.phase_a(ph)
        sb.finish(ph + 1); sb.start(ph + 2)
    ag.phase_b(0); ag.phase_c(0)
    ag.phase_b(1)
    ag.phase_b(2)
    ag.phase_c(1)
    sb.finish(4)
    lane32 = lax.broadcasted_iota(jnp.int32, (8, 32), 1)
    sub8 = lax.broadcasted_iota(jnp.int32, (8, 32), 0)
    tgt = jnp.where(sub8 == 0, sid[0], jnp.where(sub8 < 4, 15 + sub8, -1))
    pick = jnp.where(lane32 == tgt, 1.0, 0.0).astype(BF)
    for k in range(2): VEC[:, k * 640:(k + 1) * 640] = dot(pick, SB[k])

    def mk_first(r, _):
        rows = pl.ds(pl.multiple_of(r * RB, RB), RB)
        A[FIRST, rows, :] = (N1[rows, :] * VEC[0:1, :] + VEC[1:2, :]).astype(BF)
        return 0
    lax.fori_loop(0, L // RB, mk_first, 0)
    ag.phase_d(0)
    ag.phase_c(2)
    ag.phase_e(0)
    ag.phase_f(0)

    def wpan(ph, xh, par): return W[ph, xh, par].reshape(D, CW)
    def cols(par): return pl.ds(par * CW, CW)

    for xh, dst in ((0, Q), (1, K)):
        for par in range(2):
            A[dst, :, cols(par)] = dot(A[FIRST], wpan(0, xh, par)).astype(BF)
    ag.phase_d(1)
    ag.phase_e(1)
    ag.phase_f(1)
    for par in range(2):
        A[V, :, cols(par)] = dot(A[FIRST], wpan(1, 0, par)).astype(BF)
    ag.phase_d(2)

    lane256 = lax.broadcasted_iota(jnp.int32, (1, 256), 1)
    def masks(w):
        m = jnp.where(jnp.logical_and(lane256 >= 32 * w, lane256 < 32 * w + HD), 1.0, 0.0)
        return m, m.astype(BF)
    def win(pn, w):
        return pl.ds(pl.multiple_of(pn * CW + w * 128, 128), 256)

    for w in range(4):
        m32, m16 = masks(w)
        def att(pn, _, w=w, m32=m32, m16=m16):
            cw = win(pn, w)
            sc = dot_nt(A[Q, :, cw] * m16, A[K, :, cw]) * SCALE
            e = jnp.exp(sc - jnp.max(sc, axis=-1, keepdims=True))
            pr = e / jnp.sum(e, axis=-1, keepdims=True)
            PR[pn * 4 + w] = pr
            mx = dot(pr.astype(BF), A[V, :, cw]) * m32
            A[MIXED, :, cw] = A[MIXED, :, cw] + mx.astype(BF)
            return 0
        lax.fori_loop(0, 2, att, 0)
    ag.phase_e(2)
    for par in range(2):
        MID[:, cols(par)] = lat[:, cols(par)].astype(F32) + dot(A[MIXED], wpan(1, 1, par))

    def ln2(r, _):
        rows = pl.ds(pl.multiple_of(r * RB, RB), RB)
        x = MID[rows, :]
        mu = jnp.mean(x, axis=-1, keepdims=True)
        xc = x - mu
        inv = lax.rsqrt(jnp.mean(xc * xc, axis=-1, keepdims=True) + EPS)
        n = xc * inv
        N2[rows, :] = n
        I2[rows, :] = jnp.broadcast_to(inv, (RB, 128))
        A[SECOND, rows, :] = (n * VEC[2:3, :] + VEC[3:4, :]).astype(BF)
        return 0
    lax.fori_loop(0, L // RB, ln2, 0)
    ag.phase_f(2)
    for par in range(2):
        DG[:, cols(par)] = dot(A[SECOND], wpan(2, 0, par))

    def gelu(r, _):
        rows = pl.ds(pl.multiple_of(r * RB, RB), RB)
        u = DG[rows, :]
        c0 = math.sqrt(2.0 / math.pi)
        u2 = u * u
        th = jnp.tanh(c0 * (u + 0.044715 * u2 * u))
        hp = 0.5 * (1.0 + th)
        A[ACTIVE, rows, :] = (u * hp).astype(BF)
        DG[rows, :] = hp + 0.5 * u * (1.0 - th * th) * (c0 * (1.0 + 3 * 0.044715 * u2))
        return 0
    lax.fori_loop(0, L // RB, gelu, 0)

    def back(src, ph, xh, n):
        acc = None
        for par in range(2):
            t = dot_nt(src(par), W[ph, xh, par, 2 * n:2 * n + 2].reshape(CW, CW))
            acc = t if acc is None else acc + t
        return acc

    for n in range(2):
        A[GU, :, cols(n)] = (back(lambda par: cot[:, cols(par)], 2, 1, n) * DG[:, cols(n)]).astype(BF)

    def wgrad(ph, l0, l1, r0, r1):
        li = jnp.where(p.xh == 0, l0, l1)
        ri = jnp.where(p.xh == 0, r0, r1) if r1 is not None else None
        g = G[ph]
        for n in range(2):
            for par in range(2):
                if ri is None:
                    v = dot_tn(A[li, :, cols(n)], GR[:, cols(par)])
                else:
                    v = dot_tn(A[li, :, cols(n)], A[ri, :, cols(par)])
                g[par, 2 * n:2 * n + 2] = v.astype(BF).reshape(2, 2, 2, 5, 16, CW)

    for par in range(2):
        o_lat[:, cols(par)] = (MID[:, cols(par)] + dot(A[ACTIVE], wpan(2, 1, par))).astype(BF)
    A[GAO] = cot[...]
    wgrad(2, SECOND, ACTIVE, GU, GAO)
    rs.step(2, 0)

    for n in range(2):
        MID[:, cols(n)] = back(lambda par: A[GU, :, cols(par)], 2, 0, n)
    rs.step(2, 1)

    def ln2b(r, _):
        rows = pl.ds(pl.multiple_of(r * RB, RB), RB)
        gs = MID[rows, :]
        n = N2[rows, :]
        CS[1] += jnp.sum((gs * n).reshape(RB // 8, 8, D), axis=0)
        CS[2] += jnp.sum(gs.reshape(RB // 8, 8, D), axis=0)
        dn = gs * VEC[2:3, :]
        m1 = jnp.mean(dn, axis=-1, keepdims=True)
        m2 = jnp.mean(dn * n, axis=-1, keepdims=True)
        gm = cot[rows, :].astype(F32) + I2[rows, 0:1] * (dn - m1 - n * m2)
        N2[rows, :] = gm
        A[GAO, rows, :] = gm.astype(BF)
        return 0
    lax.fori_loop(0, L // RB, ln2b, 0)
    for n in range(2):
        A[GMX, :, cols(n)] = back(lambda par: A[GAO, :, cols(par)], 1, 1, n).astype(BF)
    rs.step(2, 2)

    for w in range(4):
        m32, m16 = masks(w)
        def attb(pn, _, w=w, m32=m32, m16=m16):
            cw = win(pn, w)
            gm = A[GMX, :, cw] * m16
            qm = A[Q, :, cw] * m16
            pr = PR[pn * 4 + w]
            gp = dot_nt(gm, A[V, :, cw])
            rt = jnp.sum(gp * pr, axis=-1, keepdims=True)
            gsc = (pr * (gp - rt)).astype(BF)
            A[GV, :, cw] = A[GV, :, cw] + dot_tn(pr.astype(BF), gm).astype(BF)
            A[GQ, :, cw] = A[GQ, :, cw] + (dot(gsc, A[K, :, cw]) * SCALE * m32).astype(BF)
            A[GK, :, cw] = A[GK, :, cw] + (dot_tn(gsc, qm) * SCALE).astype(BF)
            return 0
        lax.fori_loop(0, 2, attb, 0)
        if w == 1: rs.step(2, 3)
    ag.drain(0); ag.drain(1); ag.drain(2)
    wgrad(1, FIRST, MIXED, GV, GAO)
    rs.step(1, 0)
    wgrad(0, FIRST, FIRST, GQ, GK)
    rs.step(2, 4)
    rs.step(1, 1)
    rs.step(0, 0)
    rs.step(2, 5)
    rs.step(1, 2)
    rs.step(0, 1)

    for n in range(2):
        acc = None
        for g, (ph, xh) in ((GQ, (0, 0)), (GK, (0, 1)), (GV, (1, 0))):
            t = back(lambda par: A[g, :, cols(par)], ph, xh, n)
            acc = t if acc is None else acc + t
        MID[:, cols(n)] = acc
    rs.step(1, 3)
    rs.step(0, 2)

    def ln1b(r, _):
        rows = pl.ds(pl.multiple_of(r * RB, RB), RB)
        gf = MID[rows, :]
        n = N1[rows, :]
        CS[3] += jnp.sum((gf * n).reshape(RB // 8, 8, D), axis=0)
        CS[0] += jnp.sum(gf.reshape(RB // 8, 8, D), axis=0)
        dn = gf * VEC[0:1, :]
        m1 = jnp.mean(dn, axis=-1, keepdims=True)
        m2 = jnp.mean(dn * n, axis=-1, keepdims=True)
        o_in[rows, :] = N2[rows, :] + I1[rows, 0:1] * (dn - m1 - n * m2)
        return 0
    lax.fori_loop(0, L // RB, ln1b, 0)
    sub24 = lax.broadcasted_iota(jnp.int32, (24, 640), 0)
    for k in range(2):
        v = [jnp.sum(CS[i, :, k * 640:(k + 1) * 640], axis=0, keepdims=True) for i in range(4)]
        SG[k] = (jnp.where(sub24 == sid[0], v[3], 0.0) + jnp.where(sub24 == 16, v[0], 0.0)
                 + jnp.where(sub24 == 17, v[1], 0.0) + jnp.where(sub24 == 18, v[2], 0.0))
    sg.start(0)
    rs.step(1, 4)
    rs.step(0, 3)
    sg.finish(0); sg.start(1)
    rs.step(1, 5)
    rs.step(0, 4)
    sg.finish(1); sg.start(2)
    rs.step(0, 5)
    sg.finish(2); sg.start(3)

    outs = [(o_qkv, 0), (o_qkv, 1280), (o_qkv, 2560), (o_out, 0), (o_up, 0), (o_down, 0)]
    def emit(ph):
        rs.final_wait(ph)
        for xh in range(2):
            o, off = outs[2 * ph + xh]
            for par in range(2):
                v = FIN[ph, 2 * xh + par, 0].astype(F32) + FIN[ph, 2 * xh + par, 1].astype(F32)
                o[:, off + par * 640: off + (par + 1) * 640] = v[0:10]
    emit(2)
    sg.finish(3); sg.start(4)
    emit(1)
    sg.finish(4)
    acc = None
    for k in range(2):
        t = lax.dot_general(own[:, k * 640:(k + 1) * 640], SG[k], (((1,), (1,)), ((), ())), precision=lax.Precision.HIGHEST, preferred_element_type=F32)
        acc = t if acc is None else acc + t
    o_small[...] = acc[0:10]
    emit(0)
    for ph in range(3): rs.drain(ph)


def per_device(latents, script_ids, gain_table, bias_one, w_qkv, w_out, gain_two, bias_two, w_up, w_down, cotangent):
    small = jnp.concatenate([gain_table, bias_one[:, None], gain_two[:, None], bias_two[:, None]], axis=1)
    small = jnp.pad(small, ((0, 6), (0, 13)))
    V_ = pltpu.VMEM
    dma = pltpu.SemaphoreType.DMA
    blk = (16, CW)
    scratch = [
        V_((3, 2, 2, 4, 2, 2, 5, 16, CW), BF), V_((3, 5) + blk, BF), V_((3, 4) + blk, BF),
        V_((13, L, D), BF), V_((L, D), F32), V_((L, D), F32), V_((L, D), F32), V_((L, D), F32),
        V_((8, 256, 256), F32), V_((L, 128), F32), V_((L, 128), F32), V_((8, D), F32), V_((4, 8, D), F32),
        V_((2, 4, 2, 2, 5) + blk, BF), V_((3, 3, 2, 4, 2, 2) + blk, BF),
        V_((3, 1, 2, 4, 2) + blk, BF), V_((3, 3, 4) + blk, BF), V_((3, 3) + blk, BF),
        V_((3, 3, 4, 2) + blk, BF), V_((3, 3, 2) + blk, BF), V_((3, 1) + blk, BF),
        V_((3, 3, 2, 2, 2) + blk, BF), V_((3, 3, 2) + blk, BF), V_((3, 1) + blk, BF),
        V_((3,) + blk, BF), V_((3, 5) + blk, BF), V_((3, 4, 2) + blk, BF),
        V_((2, 32, 640), BF), V_((4, 3, 32, 640), BF), V_((2, 24, 640), F32), V_((4, 3, 24, 640), F32),
        dma((9, 14)), dma((9, 14)), dma((3, 8)), dma((3, 5)),
        dma((9, 2)), dma((9, 2)), dma((9, 10)), dma((9, 10)), dma((3, 5)), dma((3, 8)),
        dma((5, 3)), dma((5, 3)), dma((5, 3)), dma((5, 3)),
    ]
    vm = pl.BlockSpec(memory_space=pltpu.VMEM)
    sm = pl.BlockSpec(memory_space=pltpu.SMEM)
    res = pl.pallas_call(
        block_kernel,
        out_shape=[jax.ShapeDtypeStruct((L, D), BF), jax.ShapeDtypeStruct((L, D), F32), jax.ShapeDtypeStruct((10, 24), F32),
                   jax.ShapeDtypeStruct((10, 3 * D), F32)] + [jax.ShapeDtypeStruct((10, D), F32)] * 3,
        in_specs=[vm, vm, sm, vm, vm, vm, vm, vm],
        out_specs=[vm] * 7,
        scratch_shapes=scratch,
        compiler_params=pltpu.CompilerParams(collective_id=0, has_side_effects=True, vmem_limit_bytes=62 * 2**20),
        name="block",
    )(latents.reshape(L, D), cotangent.reshape(L, D), script_ids, small, w_qkv, w_out, w_up, w_down)
    o_lat, o_in, o_small, o_qkv, o_out, o_up, o_down = res
    return (o_lat.reshape(1, L, D), o_in.reshape(1, L, D), o_small[:, :16], o_small[:, 16], o_qkv, o_out,
            o_small[:, 17], o_small[:, 18], o_up, o_down)


def solution(mesh):
    row = P(("dp", "fsdp"), None)
    vec = P(("dp", "fsdp"))
    item = P("dp", None, None)
    return jax.shard_map(
        per_device,
        mesh=mesh,
        in_specs=(item, P("dp"), row, vec, row, row, vec, vec, row, row, item),
        out_specs=(item, item, row, vec, row, row, vec, vec, row, row),
        check_vma=False,
    )
```

time: 842 us -> 158 us (0.19)
  waiting for transfers between devices: 340 us -> 0 us
  blocking collectives: 314 us -> 0 us
  Pallas kernels: 66.8 us -> 145 us
  matrix products: 52.8 us -> 0 us
  local copies, waits for them, and re-layouts: 36.9 us -> 10.1 us
  other arithmetic: 15.7 us -> 1.37 us
  between operations: 15.1 us -> 1.33 us
    unnamed x4 -> x0, waiting for transfers between devices: 340 us -> none
    all_gather x1 -> x0, blocking collectives: 314 us -> none  [in_one_piece(): whole = lax.all_gather(both, axis, axis=dim, tiled=True)]
    pallas_call x1, Pallas kernels: 66.8 us -> 145 us  [per_device(): pl.pallas_call(block_kernel, out_shape=[jax.ShapeDtypeStruct((L, D), BF),...]
    dot_general x19 -> x0, matrix products: 50.6 us -> none  [the longest x4 13.8 us: weight_grad(): lax.dot_general(select(left), select(right), (((0,), (0,)), ((), ())), pr...]
    unnamed x70 -> x19, local copies, waits for them, and re-layouts: 19.5 us -> 6.24 us
    squeeze x2 -> x0, local copies, waits for them, and re-layouts: 8.57 us -> none  [the longest x1 7.17 us: gather_all(): w[m // 2, 2 * (m % 2)]]
  transfers between devices with their start and end apart: 2 -> 0, of which waited for: 2 -> 0; matrix products, arithmetic and copies ran while one was open for 3% -> 0% of each run, Pallas kernels for 0% -> 0%
where the time goes in v2:
time: 158 us
  Pallas kernels  145 us (92%)
  local copies, waits for them, and re-layouts  10.1 us (6%)
    pallas_call x1, Pallas kernels, per_device(): pl.pallas_call(block_kernel, out_shape=[jax.ShapeDtypeStruct((L, D), BF),...  145 us
    unnamed x19, local copies, waits for them, and re-layouts  6.24 us

profile of v2, /device:TPU:1, one launch (start us, length us, event | category | flops | bytes accessed | tf_op | source)
XLA Modules:
  0.0 157.6 jit_solution(8874550759491115296)
XLA Ops:
  1.3 0.7 copy.24
  2.0 0.8 copy.25
  2.8 0.8 copy.26
  3.5 1.4 fusion.8.small
  4.9 144.8 %block.1 = (bf16[256,1280]{1,0:T(8,128)(2,1)}, f32[256,1280]{1,0:T(8,128)}, f32[10,24]{1,0:T(8,128)}, f32[10,3840]{1,0:T(8,128)}, f32[10,1280]{1,0:T(8,128)}, /*index=5*/f32[10,1280]{1,0:T(8,128)}, f32[10,1280]{1,0:T(8,128)}) custom-call(bf16[256,1280]{1,0:T(8,128)(2,1)} %bitcast.9, bf16[256,1280]{1,0:T(8,128)(2,1)} %bitcast.10, s32[1]{0:T(128)S(6)} %copy.34.sid, ...), custom_call_target="tpu_custom_call" | custom-call | tf_op jit(solution)/shard_map/block/pallas_call | solution.py:813
  149.8 0.0 copy-start
  149.8 1.6 slice_reduce_fusion
  151.3 2.0 %copy.35 = bf16[1,256,1280]{2,1,0:T(8,128)(2,1)} copy(bf16[1,256,1280]{2,1,0:T(8,128)(2,1)} %bitcast.11) | data formatting | bytes 1310720
  153.3 0.0 copy-done
  153.3 0.0 copy-start.2
  153.3 0.0 copy-start.1
  153.3 0.0 copy-start.5
  153.3 0.0 copy-start.4
  153.3 0.0 copy-start.3
  153.3 1.1 copy.36
  154.4 0.0 copy-done.2
  154.4 0.6 copy.37
  155.0 0.0 copy-done.1
  155.0 0.7 copy.38
  155.7 0.0 copy-done.5
  155.7 0.6 copy.39
  156.3 0.0 copy-done.4
  156.3 0.6 copy.40
  157.0 0.0 copy-done.3
  157.0 0.6 copy.41
Async XLA Ops:
  149.8 3.5 %copy-start = (f32[256,1280]{1,0:T(8,128)S(1)}, f32[256,1280]{1,0:T(8,128)}, u32[]{:S(2)}) copy-start(f32[256,1280]{1,0:T(8,128)} %get-tuple-element.18) | copy-start | bytes 3932164
  153.3 1.1 copy-start.2
  153.3 1.7 %copy-start.1 = (f32[10,3840]{1,0:T(8,128)S(1)}, f32[10,3840]{1,0:T(8,128)}, u32[]{:S(2)}) copy-start(f32[10,3840]{1,0:T(8,128)} %get-tuple-element.41) | copy-start | bytes 460804
  153.3 2.4 %copy-start.5 = (f32[10,1280]{1,0:T(8,128)S(1)}, f32[10,1280]{1,0:T(8,128)}, u32[]{:S(2)}) copy-start(f32[10,1280]{1,0:T(8,128)} %get-tuple-element.42) | copy-start | bytes 153604
  153.3 3.0 %copy-start.4 = (f32[10,1280]{1,0:T(8,128)S(1)}, f32[10,1280]{1,0:T(8,128)}, u32[]{:S(2)}) copy-start(f32[10,1280]{1,0:T(8,128)} %get-tuple-element.45) | copy-start | bytes 153604
  153.3 3.6 %copy-start.3 = (f32[10,1280]{1,0:T(8,128)S(1)}, f32[10,1280]{1,0:T(8,128)}, u32[]{:S(2)}) copy-start(f32[10,1280]{1,0:T(8,128)} %get-tuple-element.46) | copy-start | bytes 153604

commit v3 on v2

--- a/solution.py
+++ b/solution.py
@@ -284,35 +284,33 @@
         if ts < 2: h()
         else: pl.when(s.p.c == (1 if other else 0))(h)
 
-    def d2d(s, ph, ts, act):
+    def d2d(s, ph, ts, act, par):
         p = s.p
         g = s.gref(ph)
         t = 3 * (1 - p.c) + ts if act != 'recv' else 3 * p.c + ts
-        for par in range(2):
+        if True:
             cp = pltpu.make_async_remote_copy(g.at[par, :, :, :, t], s.RD.at[ph, ts, par], s.dss.at[ph * 3 + ts, par], s.drs.at[ph * 3 + ts, par], device_id=p.dev(c=1 - p.c), device_id_type=MESH)
             if act == 'start': cp.start()
             elif act == 'ws': cp.wait_send()
             else: cp.wait_recv()
 
-    def d2d_start(s, ph):
-        for ts in range(3): s.go(ts, lambda ts=ts: s.d2d(ph, ts, 'start'), other=True)
-
-    def d2d_add(s, ph, ts):
+    def d2d_start(s, ph, par):
+        for ts in range(3): s.go(ts, lambda ts=ts: s.d2d(ph, ts, 'start', par), other=True)
+
+    def d2d_add(s, ph, ts, par):
         g = s.gref(ph)
         t = 3 * s.p.c + ts
-        s.d2d(ph, ts, 'recv')
-        for par in range(2):
-            def body(z, _):
-                g[par, z, :, :, t] = (g[par, z, :, :, t].astype(F32) + s.RD[ph, ts, par, z].astype(F32)).astype(BF)
-                return 0
-            lax.fori_loop(0, 4, body, 0)
+        s.d2d(ph, ts, 'recv', par)
+        def body(z, _):
+            g[par, z, :, :, t] = (g[par, z, :, :, t].astype(F32) + s.RD[ph, ts, par, z].astype(F32)).astype(BF)
+            return 0
+        lax.fori_loop(0, 4, body, 0)
 
     def order(s, ph, ts):
-        f = (ph + ts) % 3
-        return ((0, 1, 2), (1, 2, 0), (2, 1, 0))[f]
+        return ((1, 0, 2), (2, 0, 1), (0, 1, 2))[ts]
 
     def fidx(s, ph, ts):
-        return (ph + ts) % 3
+        return (1, 2, 0)[ts]
 
     def piece(s, ph, ts, st, k):
         p = s.p
@@ -372,17 +370,24 @@
         b = s.bufs[f][st]
         if ax == 0:
             k = 1 - p.xl
-            return [s.cp(s.piece(ph, ts, st, k), b.at[ph, 0], sl, s.sem(st, 0), p.dev(x=p.xh * 2 + k))]
+            src, dv = s.piece(ph, ts, st, k), p.dev(x=p.xh * 2 + k)
+            if st == 0: return [s.cp(src.at[par], b.at[ph, 0, par], sl, par, dv) for par in range(2)]
+            return [s.cp(src, b.at[ph, 0], sl, s.sem(st, 0), dv)]
         res = []
         for i, d in enumerate((1, 3, 2)):
             res.append(s.cp(s.piece(ph, ts, st, p.coord(ax, d)), b.at[ph, i], sl, s.sem(st, i), p.ring(ax, d)))
         return res
 
-    def first_a(s, ph, ts):
-        if s.order(ph, ts)[0] == 0:
-            for c in s.ring_cps(ph, ts, 0): c.start()
-            return
-        for c in s.sf_half(ph, ts): c.start()
+    def first_a(s, ph, ts, par):
+        ax = s.order(ph, ts)[0]
+        if ax == 0:
+            s.ring_cps(ph, ts, 0)[par].start()
+        elif ax == 2:
+            s.sf_half(ph, ts)[1 - par].start()
+        else:
+            @pl.when(s.p.par == par)
+            def _():
+                for c in s.sf_half(ph, ts): c.start()
 
     def sf_half(s, ph, ts):
         p = s.p
@@ -420,7 +425,12 @@
         ax = o[0]
         me = (p.xl, p.y, p.z)[ax]
         b = s.bufs[s.fidx(ph, ts)][0]
-        cs = s.ring_cps(ph, ts, 0) if ax == 0 else s.sf_full(ph, ts)
+        if ax == 0:
+            for par, c in enumerate(s.ring_cps(ph, ts, 0)):
+                c.wait_recv()
+                s.add(s.piece(ph, ts, 0, me).at[par], [b.at[ph, 0, par]])
+            return
+        cs = s.sf_full(ph, ts)
         for c in cs: c.wait_recv()
         s.add(s.piece(ph, ts, 0, me), [b.at[ph, i] for i in range(len(cs))])
 
@@ -439,10 +449,11 @@
     def each(s, f):
         for ts in range(3): s.go(ts, lambda ts=ts: f(ts))
 
+    def first(s, ph, par):
+        s.each(lambda ts: (s.d2d_add(ph, ts, par), s.first_a(ph, ts, par)))
+
     def step(s, ph, k):
-        if k == 0: s.d2d_start(ph)
-        elif k == 1: s.each(lambda ts: (s.d2d_add(ph, ts), s.first_a(ph, ts)))
-        elif k == 2: s.each(lambda ts: s.first_b(ph, ts))
+        if k == 2: s.each(lambda ts: s.first_b(ph, ts))
         elif k == 3: s.each(lambda ts: (s.first_c(ph, ts), s.next_start(ph, ts, 1)))
         elif k == 4: s.each(lambda ts: (s.next_finish(ph, ts, 1), s.next_start(ph, ts, 2)))
         elif k == 5:
@@ -500,7 +511,7 @@
     def drain(s, ph):
         p = s.p
         for ts in range(3):
-            s.go(ts, lambda ts=ts: s.d2d(ph, ts, 'ws'), other=True)
+            for par in range(2): s.go(ts, lambda ts=ts: s.d2d(ph, ts, 'ws', par), other=True)
             def ws(ts=ts):
                 if s.order(ph, ts)[0] == 0:
                     for c in s.ring_cps(ph, ts, 0): c.wait_send()
@@ -516,14 +527,24 @@
             else: pl.when(p.c == 0)(w)
 
 
+def clear_last(stg, FR):
+    stg[:, 4] = jnp.zeros((3, 16, CW), BF)
+    FR[2] = jnp.zeros((16, CW), BF)
+
+
 FIRST, Q, K, V, MIXED, SECOND, ACTIVE, GU, GAO, GMX, GQ, GK, GV = range(13)
 RB = 32
 
 
-def block_kernel(lat, cot, sid, small, wq, wo, wu, wd, o_lat, o_in, o_small, o_qkv, o_out, o_up, o_down,
+def block_kernel(lat_in, cot_in, sid, *refs):
+    small_in, (o_lat, o_in), small_out = refs[0:8], refs[8:10], refs[10:16]
+    block_body(lat_in, cot_in, sid, small_in, o_lat, o_in, small_out, *refs[16:])
+
+
+def block_body(lat_in, cot_in, sid, small_in, o_lat, o_in, small_out,
                  W, stg, pieces, A, N1, N2, MID, DG, PR, I1, I2, VEC, CS, G2, RD, b00, b01, b02, b10, b11, b12, b20, b21, b22,
                  FR, EX, FIN, SB, SBR, SG, SGR,
-                 ssem, rsem, s0s, s0r, dss, drs, gss, grs, fs, fr, sbs, sbr, sgs, sgr):
+                 lat, cot, gt, b1, g2, b2, wq, wo, wu, wd, o_tab, o_vec, o_qkv, o_out, o_up, o_down, ssem, rsem, s0s, s0r, dss, drs, gss, grs, fs, fr, sbs, sbr, sgs, sgr, io):
     p = Pos()
     ag = AG(p, W, stg, pieces, ssem, rsem, None, s0s, s0r)
     G = [W.at[2, 0], W.at[2, 1], G2]
@@ -535,21 +556,27 @@
 
     parts = ag.partners()
     bar = pltpu.get_barrier_semaphore()
-    fill_pieces(pieces, wq, wo, wu, wd)
-    stg[...] = jnp.zeros_like(stg)
-    FIN[...] = jnp.zeros_like(FIN)
-    FR[...] = jnp.zeros_like(FR)
     for d in parts:
         pl.semaphore_signal(bar, inc=1, device_id=d, device_id_type=MESH)
+    in_lat = pltpu.make_async_copy(lat_in, lat, io.at[0])
+    in_cot = pltpu.make_async_copy(cot_in, cot, io.at[1])
+    ins = [pltpu.make_async_copy(a, v, io.at[4 + i]) for i, (a, v) in enumerate(zip(small_in, (gt, b1, g2, b2, wq, wo, wu, wd)))]
+    for c in ins: c.start()
+    in_lat.start(); in_cot.start()
+    for c in ins: c.wait()
+    fill_pieces(pieces, wq, wo, wu, wd)
+    pl.when(p.c == 1)(lambda: clear_last(stg, FR))
     j = lax.broadcasted_iota(jnp.int32, (16, D), 0)
     lane = lax.broadcasted_iota(jnp.int32, (16, D), 1)
     own = jnp.where(jnp.logical_and(lane == idx * 10 + j, j < 10), 1.0, 0.0)
-    spread = dot_tn(small[...], own.astype(BF)).astype(BF)
+    own16 = own[0:10].astype(BF)
+    spread = [dot_tn(gt[...], own16)] + [dot(jnp.broadcast_to(b[...].reshape(1, 10), (8, 10)), own16)[0:1] for b in (b1, g2, b2)] + [jnp.zeros((13, D), F32)]
+    spread = jnp.concatenate(spread, axis=0).astype(BF)
     for k in range(2): SB[k] = spread[:, k * 640:(k + 1) * 640]
     pl.semaphore_wait(bar, len(parts))
 
+    sb.start(0)
     for ph in range(3): ag.s0(ph, 'start')
-    sb.start(0)
 
     def ln1(r, _):
         rows = pl.ds(pl.multiple_of(r * RB, RB), RB)
@@ -560,19 +587,25 @@
         N1[rows, :] = xc * inv
         I1[rows, :] = jnp.broadcast_to(inv, (RB, 128))
         return 0
+    in_lat.wait(); in_cot.wait()
     lax.fori_loop(0, L // RB, ln1, 0)
+    ag.s0_recv(0); ag.compact(0); ag.phase_a(0)
+    sb.finish(0); sb.start(1)
+    ag.s0_recv(1); ag.compact(1); ag.phase_a(1)
+    ag.phase_b(0)
+    sb.finish(1); sb.start(2)
+    ag.s0_recv(2); ag.compact(2); ag.phase_a(2)
+    ag.phase_b(1)
+    ag.phase_c(0)
+    sb.finish(2); sb.start(3)
+    ag.phase_b(2)
+    ag.phase_c(1)
+    sb.finish(3); sb.start(4)
     A[MIXED] = jnp.zeros((L, D), BF)
     for k in (GQ, GK, GV): A[k] = jnp.zeros((L, D), BF)
     CS[...] = jnp.zeros_like(CS)
-
-    sb.finish(0); sb.start(1)
-    for ph in range(3):
-        ag.s0_recv(ph); ag.compact(ph); ag.phase_a(ph)
-        sb.finish(ph + 1); sb.start(ph + 2)
-    ag.phase_b(0); ag.phase_c(0)
-    ag.phase_b(1)
-    ag.phase_b(2)
-    ag.phase_c(1)
+    ag.phase_d(0)
+    ag.phase_c(2)
     sb.finish(4)
     lane32 = lax.broadcasted_iota(jnp.int32, (8, 32), 1)
     sub8 = lax.broadcasted_iota(jnp.int32, (8, 32), 0)
@@ -585,23 +618,22 @@
         A[FIRST, rows, :] = (N1[rows, :] * VEC[0:1, :] + VEC[1:2, :]).astype(BF)
         return 0
     lax.fori_loop(0, L // RB, mk_first, 0)
-    ag.phase_d(0)
-    ag.phase_c(2)
+    ag.phase_d(1)
     ag.phase_e(0)
     ag.phase_f(0)
 
     def wpan(ph, xh, par): return W[ph, xh, par].reshape(D, CW)
     def cols(par): return pl.ds(par * CW, CW)
 
-    for xh, dst in ((0, Q), (1, K)):
-        for par in range(2):
-            A[dst, :, cols(par)] = dot(A[FIRST], wpan(0, xh, par)).astype(BF)
-    ag.phase_d(1)
+    for par in range(2):
+        A[Q, :, cols(par)] = dot(A[FIRST], wpan(0, 0, par)).astype(BF)
+    ag.phase_d(2)
+    for par in range(2):
+        A[K, :, cols(par)] = dot(A[FIRST], wpan(0, 1, par)).astype(BF)
     ag.phase_e(1)
     ag.phase_f(1)
     for par in range(2):
         A[V, :, cols(par)] = dot(A[FIRST], wpan(1, 0, par)).astype(BF)
-    ag.phase_d(2)
 
     lane256 = lax.broadcasted_iota(jnp.int32, (1, 256), 1)
     def masks(w):
@@ -610,18 +642,18 @@
     def win(pn, w):
         return pl.ds(pl.multiple_of(pn * CW + w * 128, 128), 256)
 
-    for w in range(4):
-        m32, m16 = masks(w)
-        def att(pn, _, w=w, m32=m32, m16=m16):
+    for pn in range(2):
+        def att(w, _, pn=pn):
             cw = win(pn, w)
+            m32, m16 = masks(w)
             sc = dot_nt(A[Q, :, cw] * m16, A[K, :, cw]) * SCALE
             e = jnp.exp(sc - jnp.max(sc, axis=-1, keepdims=True))
-            pr = e / jnp.sum(e, axis=-1, keepdims=True)
+            pr = e * (1.0 / jnp.sum(e, axis=-1, keepdims=True))
             PR[pn * 4 + w] = pr
             mx = dot(pr.astype(BF), A[V, :, cw]) * m32
             A[MIXED, :, cw] = A[MIXED, :, cw] + mx.astype(BF)
             return 0
-        lax.fori_loop(0, 2, att, 0)
+        lax.fori_loop(0, 4, att, 0, unroll=True)
     ag.phase_e(2)
     for par in range(2):
         MID[:, cols(par)] = lat[:, cols(par)].astype(F32) + dot(A[MIXED], wpan(1, 1, par))
@@ -664,31 +696,28 @@
     for n in range(2):
         A[GU, :, cols(n)] = (back(lambda par: cot[:, cols(par)], 2, 1, n) * DG[:, cols(n)]).astype(BF)
 
-    def wgrad(ph, l0, l1, r0, r1):
+    def wgrad(ph, l0, l1, r0, r1, par):
         li = jnp.where(p.xh == 0, l0, l1)
-        ri = jnp.where(p.xh == 0, r0, r1) if r1 is not None else None
-        g = G[ph]
+        ri = jnp.where(p.xh == 0, r0, r1)
         for n in range(2):
-            for par in range(2):
-                if ri is None:
-                    v = dot_tn(A[li, :, cols(n)], GR[:, cols(par)])
-                else:
-                    v = dot_tn(A[li, :, cols(n)], A[ri, :, cols(par)])
-                g[par, 2 * n:2 * n + 2] = v.astype(BF).reshape(2, 2, 2, 5, 16, CW)
-
+            v = dot_tn(A[li, :, cols(n)], A[ri, :, cols(par)])
+            G[ph][par, 2 * n:2 * n + 2] = v.astype(BF).reshape(2, 2, 2, 5, 16, CW)
+        rs.d2d_start(ph, par)
+
+    A[GAO] = cot[...]
+    wgrad(2, SECOND, ACTIVE, GU, GAO, 0)
+    wgrad(2, SECOND, ACTIVE, GU, GAO, 1)
+    for n in range(2):
+        DG[:, cols(n)] = back(lambda par: A[GU, :, cols(par)], 2, 0, n)
+        rs.first(2, n)
     for par in range(2):
-        o_lat[:, cols(par)] = (MID[:, cols(par)] + dot(A[ACTIVE], wpan(2, 1, par))).astype(BF)
-    A[GAO] = cot[...]
-    wgrad(2, SECOND, ACTIVE, GU, GAO)
-    rs.step(2, 0)
-
-    for n in range(2):
-        MID[:, cols(n)] = back(lambda par: A[GU, :, cols(par)], 2, 0, n)
-    rs.step(2, 1)
+        A[SECOND, :, cols(par)] = (MID[:, cols(par)] + dot(A[ACTIVE], wpan(2, 1, par))).astype(BF)
+    out_lat = pltpu.make_async_copy(A.at[SECOND], o_lat, io.at[2])
+    out_lat.start()
 
     def ln2b(r, _):
         rows = pl.ds(pl.multiple_of(r * RB, RB), RB)
-        gs = MID[rows, :]
+        gs = DG[rows, :]
         n = N2[rows, :]
         CS[1] += jnp.sum((gs * n).reshape(RB // 8, 8, D), axis=0)
         CS[2] += jnp.sum(gs.reshape(RB // 8, 8, D), axis=0)
@@ -702,12 +731,12 @@
     lax.fori_loop(0, L // RB, ln2b, 0)
     for n in range(2):
         A[GMX, :, cols(n)] = back(lambda par: A[GAO, :, cols(par)], 1, 1, n).astype(BF)
-    rs.step(2, 2)
-
-    for w in range(4):
-        m32, m16 = masks(w)
-        def attb(pn, _, w=w, m32=m32, m16=m16):
+        if n == 0: rs.step(2, 2)
+
+    for pn in range(2):
+        def attb(w, _, pn=pn):
             cw = win(pn, w)
+            m32, m16 = masks(w)
             gm = A[GMX, :, cw] * m16
             qm = A[Q, :, cw] * m16
             pr = PR[pn * 4 + w]
@@ -718,27 +747,27 @@
             A[GQ, :, cw] = A[GQ, :, cw] + (dot(gsc, A[K, :, cw]) * SCALE * m32).astype(BF)
             A[GK, :, cw] = A[GK, :, cw] + (dot_tn(gsc, qm) * SCALE).astype(BF)
             return 0
-        lax.fori_loop(0, 2, attb, 0)
-        if w == 1: rs.step(2, 3)
-    ag.drain(0); ag.drain(1); ag.drain(2)
-    wgrad(1, FIRST, MIXED, GV, GAO)
-    rs.step(1, 0)
-    wgrad(0, FIRST, FIRST, GQ, GK)
-    rs.step(2, 4)
-    rs.step(1, 1)
-    rs.step(0, 0)
-    rs.step(2, 5)
-    rs.step(1, 2)
-    rs.step(0, 1)
-
+        if pn == 0:
+            lax.fori_loop(0, 4, attb, 0, unroll=True)
+            ag.drain(2)
+        else:
+            lax.fori_loop(0, 2, attb, 0, unroll=True)
+            rs.first(1, 0)
+            rs.first(0, 0)
+            lax.fori_loop(2, 4, attb, 0, unroll=True)
+        wgrad(1, FIRST, MIXED, GV, GAO, pn)
+        wgrad(0, FIRST, FIRST, GQ, GK, pn)
+        rs.step(2, 3 + pn)
     for n in range(2):
         acc = None
         for g, (ph, xh) in ((GQ, (0, 0)), (GK, (0, 1)), (GV, (1, 0))):
             t = back(lambda par: A[g, :, cols(par)], ph, xh, n)
             acc = t if acc is None else acc + t
         MID[:, cols(n)] = acc
-    rs.step(1, 3)
+        rs.first(1 - n, 1)
+    rs.step(1, 2)
     rs.step(0, 2)
+    rs.step(2, 5)
 
     def ln1b(r, _):
         rows = pl.ds(pl.multiple_of(r * RB, RB), RB)
@@ -749,48 +778,70 @@
         dn = gf * VEC[0:1, :]
         m1 = jnp.mean(dn, axis=-1, keepdims=True)
         m2 = jnp.mean(dn * n, axis=-1, keepdims=True)
-        o_in[rows, :] = N2[rows, :] + I1[rows, 0:1] * (dn - m1 - n * m2)
+        DG[rows, :] = N2[rows, :] + I1[rows, 0:1] * (dn - m1 - n * m2)
         return 0
     lax.fori_loop(0, L // RB, ln1b, 0)
+    out_in = pltpu.make_async_copy(DG, o_in, io.at[3])
+    out_in.start()
     sub24 = lax.broadcasted_iota(jnp.int32, (24, 640), 0)
     for k in range(2):
         v = [jnp.sum(CS[i, :, k * 640:(k + 1) * 640], axis=0, keepdims=True) for i in range(4)]
         SG[k] = (jnp.where(sub24 == sid[0], v[3], 0.0) + jnp.where(sub24 == 16, v[0], 0.0)
                  + jnp.where(sub24 == 17, v[1], 0.0) + jnp.where(sub24 == 18, v[2], 0.0))
     sg.start(0)
+    ag.drain(0); ag.drain(1)
+    rs.step(1, 3)
+    sg.finish(0); sg.start(1)
+    rs.step(0, 3)
     rs.step(1, 4)
-    rs.step(0, 3)
-    sg.finish(0); sg.start(1)
+    sg.finish(1); sg.start(2)
+    rs.step(0, 4)
     rs.step(1, 5)
-    rs.step(0, 4)
-    sg.finish(1); sg.start(2)
+    sg.finish(2); sg.start(3)
     rs.step(0, 5)
-    sg.finish(2); sg.start(3)
 
     outs = [(o_qkv, 0), (o_qkv, 1280), (o_qkv, 2560), (o_out, 0), (o_up, 0), (o_down, 0)]
     def emit(ph):
         rs.final_wait(ph)
+        o_id = rs.myo()
+        sel = jnp.where(o_id > 4, 1, 0)
+        @pl.when(o_id == 4)
+        def _():
+            FIN[ph, :, 0] = FIN[ph, :, 0] + FIN[ph, :, 1]
         for xh in range(2):
             o, off = outs[2 * ph + xh]
             for par in range(2):
-                v = FIN[ph, 2 * xh + par, 0].astype(F32) + FIN[ph, 2 * xh + par, 1].astype(F32)
+                v = FIN[ph, 2 * xh + par, sel].astype(F32)
                 o[:, off + par * 640: off + (par + 1) * 640] = v[0:10]
     emit(2)
     sg.finish(3); sg.start(4)
     emit(1)
     sg.finish(4)
-    acc = None
+    tab = None
     for k in range(2):
-        t = lax.dot_general(own[:, k * 640:(k + 1) * 640], SG[k], (((1,), (1,)), ((), ())), precision=lax.Precision.HIGHEST, preferred_element_type=F32)
-        acc = t if acc is None else acc + t
-    o_small[...] = acc[0:10]
+        ok = own[:, k * 640:(k + 1) * 640]
+        t = lax.dot_general(ok, SG[k], (((1,), (1,)), ((), ())), precision=lax.Precision.HIGHEST, preferred_element_type=F32)
+        u = lax.dot_general(SG[k, 16:24], ok, (((1,), (1,)), ((), ())), precision=lax.Precision.HIGHEST, preferred_element_type=F32)
+        tab, vec = (t, u) if tab is None else (tab + t, vec + u)
+    o_tab[...] = tab[0:10, 0:16]
+    o_vec[...] = vec[:, 0:10]
     emit(0)
+    outs = [pltpu.make_async_copy(v, o, io.at[4 + i]) for i, (v, o) in enumerate(zip((o_tab, o_vec, o_qkv, o_out, o_up, o_down), small_out))]
+    for c in outs: c.start()
     for ph in range(3): rs.drain(ph)
+    out_lat.wait(); out_in.wait()
+    for c in outs: c.wait()
+
+
+def results_kernel(lat, inp, tab, vec, qkv, out, up, down, o_lat, o_in, o_tab, o_b1, o_g2, o_b2, o_qkv, o_out, o_up, o_down, sem):
+    cps = [pltpu.make_async_copy(a, o, sem.at[i]) for i, (a, o) in enumerate(((lat, o_lat), (inp, o_in), (qkv, o_qkv), (out, o_out), (up, o_up), (down, o_down)))]
+    for c in cps: c.start()
+    o_tab[...] = tab[...]
+    for i, o in enumerate((o_b1, o_g2, o_b2)): o[...] = vec[i]
+    for c in cps: c.wait()
 
 
 def per_device(latents, script_ids, gain_table, bias_one, w_qkv, w_out, gain_two, bias_two, w_up, w_down, cotangent):
-    small = jnp.concatenate([gain_table, bias_one[:, None], gain_two[:, None], bias_two[:, None]], axis=1)
-    small = jnp.pad(small, ((0, 6), (0, 13)))
     V_ = pltpu.VMEM
     dma = pltpu.SemaphoreType.DMA
     blk = (16, CW)
@@ -800,29 +851,38 @@
         V_((8, 256, 256), F32), V_((L, 128), F32), V_((L, 128), F32), V_((8, D), F32), V_((4, 8, D), F32),
         V_((2, 4, 2, 2, 5) + blk, BF), V_((3, 3, 2, 4, 2, 2) + blk, BF),
         V_((3, 1, 2, 4, 2) + blk, BF), V_((3, 3, 4) + blk, BF), V_((3, 3) + blk, BF),
-        V_((3, 3, 4, 2) + blk, BF), V_((3, 3, 2) + blk, BF), V_((3, 1) + blk, BF),
-        V_((3, 3, 2, 2, 2) + blk, BF), V_((3, 3, 2) + blk, BF), V_((3, 1) + blk, BF),
+        V_((3, 3, 4, 2) + blk, BF), V_((3, 1, 4) + blk, BF), V_((3, 3) + blk, BF),
+        V_((3, 3, 2, 2, 2) + blk, BF), V_((3, 1, 2, 2) + blk, BF), V_((3, 3) + blk, BF),
         V_((3,) + blk, BF), V_((3, 5) + blk, BF), V_((3, 4, 2) + blk, BF),
-        V_((2, 32, 640), BF), V_((4, 3, 32, 640), BF), V_((2, 24, 640), F32), V_((4, 3, 24, 640), F32),
+        V_((2, 32, 640), BF), V_((4, 3, 32, 640), BF), V_((2, 24, 640), F32), V_((4, 3, 24, 640), F32), V_((L, D), BF), V_((L, D), BF),
+        V_((10, 16), BF), V_((10,), BF), V_((10,), BF), V_((10,), BF), V_((10, 3 * D), BF), V_((10, D), BF), V_((10, D), BF), V_((10, D), BF),
+        V_((10, 16), F32), V_((8, 10), F32), V_((10, 3 * D), F32), V_((10, D), F32), V_((10, D), F32), V_((10, D), F32),
         dma((9, 14)), dma((9, 14)), dma((3, 8)), dma((3, 5)),
         dma((9, 2)), dma((9, 2)), dma((9, 10)), dma((9, 10)), dma((3, 5)), dma((3, 8)),
-        dma((5, 3)), dma((5, 3)), dma((5, 3)), dma((5, 3)),
+        dma((5, 3)), dma((5, 3)), dma((5, 3)), dma((5, 3)), dma((12,)),
     ]
     vm = pl.BlockSpec(memory_space=pltpu.VMEM)
     sm = pl.BlockSpec(memory_space=pltpu.SMEM)
+    hbm = pl.BlockSpec(memory_space=pl.ANY)
+    f32 = lambda *d: jax.ShapeDtypeStruct(d, F32)
     res = pl.pallas_call(
         block_kernel,
-        out_shape=[jax.ShapeDtypeStruct((L, D), BF), jax.ShapeDtypeStruct((L, D), F32), jax.ShapeDtypeStruct((10, 24), F32),
-                   jax.ShapeDtypeStruct((10, 3 * D), F32)] + [jax.ShapeDtypeStruct((10, D), F32)] * 3,
-        in_specs=[vm, vm, sm, vm, vm, vm, vm, vm],
-        out_specs=[vm] * 7,
+        out_shape=[jax.ShapeDtypeStruct((L, D), BF), f32(L, D), f32(10, 16), f32(8, 10), f32(10, 3 * D), f32(10, D), f32(10, D), f32(10, D)],
+        in_specs=[hbm, hbm, sm] + [hbm] * 8,
+        out_specs=[hbm] * 8,
         scratch_shapes=scratch,
         compiler_params=pltpu.CompilerParams(collective_id=0, has_side_effects=True, vmem_limit_bytes=62 * 2**20),
         name="block",
-    )(latents.reshape(L, D), cotangent.reshape(L, D), script_ids, small, w_qkv, w_out, w_up, w_down)
-    o_lat, o_in, o_small, o_qkv, o_out, o_up, o_down = res
-    return (o_lat.reshape(1, L, D), o_in.reshape(1, L, D), o_small[:, :16], o_small[:, 16], o_qkv, o_out,
-            o_small[:, 17], o_small[:, 18], o_up, o_down)
+    )(latents.reshape(L, D), cotangent.reshape(L, D), script_ids, gain_table, bias_one, gain_two, bias_two, w_qkv, w_out, w_up, w_down)
+    o_lat, o_in, o_tab, o_b1, o_g2, o_b2, o_qkv, o_out, o_up, o_down = pl.pallas_call(
+        results_kernel,
+        out_shape=[jax.ShapeDtypeStruct((L, D), BF), f32(L, D), f32(10, 16), f32(10), f32(10), f32(10), f32(10, 3 * D), f32(10, D), f32(10, D), f32(10, D)],
+        in_specs=[vm] * 8,
+        out_specs=[hbm, hbm] + [vm] * 4 + [hbm] * 4,
+        scratch_shapes=[dma((6,))],
+        name="results",
+    )(*res)
+    return (o_lat.reshape(1, L, D), o_in.reshape(1, L, D), o_tab, o_b1, o_qkv, o_out, o_g2, o_b2, o_up, o_down)
 
 
 def solution(mesh):

time: 158 us -> 127 us (0.80)
  Pallas kernels: 145 us -> 126 us
  local copies, waits for them, and re-layouts: 10.1 us -> 0 us
    pallas_call x1, Pallas kernels: 145 us -> 122 us  [per_device(): pl.pallas_call(block_kernel, out_shape=[jax.ShapeDtypeStruct((L, D), BF),...]
    unnamed x19 -> x0, local copies, waits for them, and re-layouts: 6.24 us -> none
    pallas_call x0 -> x1, Pallas kernels: none -> 3.73 us  [per_device(): pl.pallas_call(results_kernel, out_shape=[jax.ShapeDtypeStruct((L, D), BF...]
    broadcast_in_dim x3 -> x0, local copies, waits for them, and re-layouts: 2.26 us -> none  [the longest x1 0.76 us: per_device(): bias_two[:, None]]
where the time goes in v3:
time: 127 us
  Pallas kernels  126 us (99%)
  between operations  1.46 us (1%)
    pallas_call x1, Pallas kernels, per_device(): pl.pallas_call(block_kernel, out_shape=[jax.ShapeDtypeStruct((L, D), BF),...  122 us
    pallas_call x1, Pallas kernels, per_device(): pl.pallas_call(results_kernel, out_shape=[jax.ShapeDtypeStruct((L, D), BF...  3.73 us

profile of v3, /device:TPU:1, one launch (start us, length us, event | category | flops | bytes accessed | tf_op | source)
XLA Modules:
  0.0 127.3 jit_solution(3452545138276890093)
XLA Ops:
  1.3 122.1 %block.1 = (bf16[256,1280]{1,0:T(8,128)(2,1)}, f32[256,1280]{1,0:T(8,128)}, f32[10,16]{1,0:T(8,128)}, f32[8,10]{1,0:T(8,128)}, f32[10,3840]{1,0:T(8,128)}, /*ind...) custom-call(bf16[256,1280]{1,0:T(8,128)(2,1)} %bitcast.4, bf16[256,1280]{1,0:T(8,128)(2,1)} %bitcast.5, ...), custom_call_target="tpu_custom_call" | custom-call | tf_op jit(solution)/shard_map/block/pallas_call | solution.py:868
  123.4 3.7 %results.1 = (bf16[256,1280]{1,0:T(8,128)(2,1)}, f32[256,1280]{1,0:T(8,128)}, f32[10,16]{1,0:T(8,128)}, f32[10]{0:T(128)}, f32[10]{0:T(128)}, /*index=5*/f32[10]...) custom-call(bf16[256,1280]{1,0:T(8,128)(2,1)} %get-tuple-element.28.lat, ...), custom_call_target="tpu_custom_call" | custom-call | tf_op jit(solution)/shard_map/results/pallas_call | solution.py:877

commit v4 on v3

--- a/solution.py
+++ b/solution.py
@@ -35,6 +35,9 @@
     def coord(s, ax, d):
         return ((s.x, s.y, s.z)[ax] + d) % 4
 
+def wait(ref, sem):
+    pltpu.make_async_copy(ref, ref, sem).wait()
+
 class AG:
     def __init__(s, p, W, stg, pieces, ssem, rsem, sib_r, s0s, s0r):
         s.p, s.W, s.stg, s.pieces = p, W, stg, pieces
@@ -65,37 +68,29 @@
     def s0_src(s):
         p = s.p
         return (p.par * 2 + p.c) * 2 + p.xh
-    def s0(s, ph, act):
+    def s0(s, ph):
         p = s.p; o = s.s0_src()
         for tc in (0, 1):
             cond = (o <= 4) if tc == 0 else (o >= 4)
             @pl.when(cond)
             def _(tc=tc):
-                for i, (dy, dx, y, x) in enumerate(s.s0_targets()):
-                    chunk = (x // 2) * 2 + y % 2
-                    src = s.pieces.at[ph, chunk]
+                for dy, dx, y, x in s.s0_targets():
+                    src = s.pieces.at[ph, (x // 2) * 2 + y % 2]
                     dst = s.stg.at[ph, o - 4 * tc]
+                    def send(sem):
+                        pltpu.make_async_remote_copy(src, dst, s.s0s.at[sem], s.s0r.at[ph], device_id=p.dev(y=y, x=x, c=tc), device_id_type=MESH).start()
                     if dy == 0 and dx == 0:
                         @pl.when(p.c == tc)
                         def _():
-                            cp = pltpu.make_async_copy(src, dst, s.s0r.at[ph, o - 4 * tc])
-                            if act == 'start': cp.start()
+                            pltpu.make_async_copy(src, dst, s.s0r.at[ph]).start()
                         @pl.when(p.c != tc)
                         def _():
-                            cp = pltpu.make_async_remote_copy(src, dst, s.s0s.at[ph, i * 2 + tc], s.s0r.at[ph, o - 4 * tc], device_id=p.dev(y=y, x=x, c=tc), device_id_type=MESH)
-                            if act == 'start': cp.start()
-                            else: cp.wait_send()
+                            send(2)
                     else:
-                        cp = pltpu.make_async_remote_copy(src, dst, s.s0s.at[ph, i * 2 + tc], s.s0r.at[ph, o - 4 * tc], device_id=p.dev(y=y, x=x, c=tc), device_id_type=MESH)
-                        if act == 'start': cp.start()
-                        else: cp.wait_send()
+                        send(tc)
     def s0_recv(s, ph):
-        p = s.p
-        for k in range(5):
-            def w(k=k):
-                pltpu.make_async_copy(s.pieces.at[ph, 0], s.stg.at[ph, k], s.s0r.at[ph, k]).wait()
-            if k < 4: w()
-            else: pl.when(p.c == 0)(w)
+        pl.when(s.p.c == 0)(lambda: wait(s.stg.at[ph], s.s0r.at[ph]))
+        pl.when(s.p.c == 1)(lambda: wait(s.stg.at[ph, 0:4], s.s0r.at[ph]))
     def compact(s, ph):
         p = s.p
         i = lax.broadcasted_iota(jnp.int32, (48, 80), 0)
@@ -123,90 +118,72 @@
         if 2 in full: zz = slice(None)
         return [ph, xh, par, zz, xl, h, t]
     def ref(s, reg): return s.W.at[tuple(reg)]
-    def cp(s, reg, slot, k, dev):
+    def cp(s, reg, ph, ts, kind, k, dev):
         r = s.ref(reg)
-        return pltpu.make_async_remote_copy(r, r, s.ssem.at[slot, k], s.rsem.at[slot, k], device_id=dev, device_id_type=MESH)
+        return pltpu.make_async_remote_copy(r, r, s.ssem.at[kind + (4 if ts == 2 else 0)], s.rsem.at[ph * 3 + ts, k], device_id=dev, device_id_type=MESH)
     def half(s, reg, full, hf):
         reg = list(reg)
         i = 3 if 2 in full else (1 if 0 in full else 2)
         reg[i] = pl.ds(hf * 2, 2) if i == 3 else pl.ds(hf, 1)
         return reg
-    def slot(s, ph, ts): return ph * 3 + ts
     def t(s, ts): return 3 * s.p.c + ts
-    def g(s, ts, f):
-        if ts < 2: f()
-        else: pl.when(s.p.c == 0)(f)
-    def direct(s, stage, ph, ts, act):
+    def direct(s, stage, ph, ts):
         a = s.order(ph, ts); full = a[:stage]; ax = a[stage]
         for d in (1, 3, 2):
-            k = stage * 3 + d - 1
-            if act == 'recv':
-                s.cp(s.region(ph, s.t(ts), full, {ax: s.p.coord(ax, -d)}), s.slot(ph, ts), k, s.p.ring(ax, d)).wait_recv()
-            else:
-                c = s.cp(s.region(ph, s.t(ts), full), s.slot(ph, ts), k, s.p.ring(ax, d))
-                c.start() if act == 'start' else c.wait_send()
-    def s3(s, ph, ts, what, act):
-        a = s.order(ph, ts); full = a[:2]; ax = a[2]; sl = s.slot(ph, ts); tt = s.t(ts)
+            s.cp(s.region(ph, s.t(ts), full), ph, ts, stage, stage, s.p.ring(ax, d)).start()
+    def got(s, ph, ts, k):
+        r = s.W.at[ph]
+        ref = (lambda: r.at[0, 0, 0:3, 0, 0, 0], lambda: r.at[0, 0, 0:3, :, :, 0], lambda: r.at[0, 0, :, :, :, 0],
+               lambda: r.at[0, 0, :, :, :, 0], lambda: r.at[0, 0, :, :, :, 0], lambda: r.at[:, :, :, :, :, 0])[k]()
+        wait(ref, s.rsem.at[ph * 3 + ts, k])
+    def s3(s, ph, ts, what):
+        a = s.order(ph, ts); full = a[:2]; ax = a[2]; tt = s.t(ts)
         R, L = s.p.ring(ax, 1), s.p.ring(ax, 3)
-        own = s.region(ph, tt, full)
-        fl = s.region(ph, tt, full, {ax: s.p.coord(ax, -1)})
-        fr = s.region(ph, tt, full, {ax: s.p.coord(ax, 1)})
-        op = s.region(ph, tt, full, {ax: s.p.coord(ax, 2)})
+        reg = lambda d: s.region(ph, tt, full, {ax: s.p.coord(ax, d)})
         if what == 'own':
-            if act == 'recvL': s.cp(fl, sl, 6, R).wait_recv()
-            elif act == 'recvR': s.cp(fr, sl, 7, L).wait_recv()
-            else:
-                for reg, k, dv in ((own, 6, R), (own, 7, L)):
-                    c = s.cp(reg, sl, k, dv)
-                    c.start() if act == 'start' else c.wait_send()
-        elif what == 'fwdR':
-            if act == 'recv': s.cp(s.half(op, full, 0), sl, 8, R).wait_recv()
-            else:
-                c = s.cp(s.half(fl, full, 0), sl, 8, R)
-                c.start() if act == 'start' else c.wait_send()
-        elif what == 'fwdL':
-            if act == 'recv': s.cp(s.half(op, full, 1), sl, 9, L).wait_recv()
-            else:
-                c = s.cp(s.half(fr, full, 1), sl, 9, L)
-                c.start() if act == 'start' else c.wait_send()
-    def sib(s, ph, ts, piece, act):
+            s.cp(reg(0), ph, ts, 2, 2, R).start()
+            s.cp(reg(0), ph, ts, 2, 3, L).start()
+        elif what == 'fwdR': s.cp(s.half(reg(-1), full, 0), ph, ts, 2, 4, R).start()
+        else: s.cp(s.half(reg(1), full, 1), ph, ts, 2, 4, L).start()
+    def sib(s, ph, ts, piece):
         a = s.order(ph, ts); full = a[:2]; ax = a[2]
         d = (0, -1, 1, 2)[piece]
-        dv = s.p.dev(c=1 - s.p.c)
-        t = s.t(ts) if act != 'recv' else 3 * (1 - s.p.c) + ts
-        c = s.cp(s.region(ph, t, full, {ax: s.p.coord(ax, d)}), s.slot(ph, ts), 10 + piece, dv)
-        if act == 'start': c.start()
-        elif act == 'recv': c.wait_recv()
-        else: c.wait_send()
+        s.cp(s.region(ph, s.t(ts), full, {ax: s.p.coord(ax, d)}), ph, ts, 3, 5, s.p.dev(c=1 - s.p.c)).start()
     def go(s, ts, f, other=False):
         def h():
             f()
         if ts < 2: h()
         else: pl.when(s.p.c == (1 if other else 0))(h)
+    def each(s, f, other=False):
+        for ts in range(3): s.go(ts, lambda ts=ts: f(ts), other)
     def phase_a(s, ph):
-        for ts in range(3): s.go(ts, lambda ts=ts: s.direct(0, ph, ts, 'start'))
+        s.each(lambda ts: s.direct(0, ph, ts))
     def phase_b(s, ph):
-        for ts in range(3):
-            s.go(ts, lambda ts=ts: (s.direct(0, ph, ts, 'recv'), s.direct(1, ph, ts, 'start')))
+        s.each(lambda ts: (s.got(ph, ts, 0), s.direct(1, ph, ts)))
     def phase_c(s, ph):
-        for ts in range(3):
-            s.go(ts, lambda ts=ts: (s.direct(1, ph, ts, 'recv'), s.s3(ph, ts, 'own', 'start'), s.sib(ph, ts, 0, 'start')))
+        s.each(lambda ts: (s.got(ph, ts, 1), s.s3(ph, ts, 'own'), s.sib(ph, ts, 0)))
     def phase_d(s, ph):
-        for ts in range(3):
-            s.go(ts, lambda ts=ts: (
-                s.s3(ph, ts, 'own', 'recvL'), s.s3(ph, ts, 'fwdR', 'start'), s.sib(ph, ts, 1, 'start'),
-                s.s3(ph, ts, 'own', 'recvR'), s.s3(ph, ts, 'fwdL', 'start'), s.sib(ph, ts, 2, 'start')))
+        s.each(lambda ts: (s.got(ph, ts, 2), s.s3(ph, ts, 'fwdR'), s.sib(ph, ts, 1), s.got(ph, ts, 3), s.s3(ph, ts, 'fwdL'), s.sib(ph, ts, 2)))
     def phase_e(s, ph):
-        for ts in range(3):
-            s.go(ts, lambda ts=ts: (s.s3(ph, ts, 'fwdR', 'recv'), s.s3(ph, ts, 'fwdL', 'recv'), s.sib(ph, ts, 3, 'start')))
+        s.each(lambda ts: (s.got(ph, ts, 4), s.sib(ph, ts, 3)))
     def phase_f(s, ph):
-        for ts in range(3):
-            s.go(ts, lambda ts=ts: [s.sib(ph, ts, k, 'recv') for k in range(4)], other=True)
-    def drain(s, ph):
-        s.s0(ph, 'wait_send')
-        for ts in range(3):
-            s.go(ts, lambda ts=ts: (s.direct(0, ph, ts, 'ws'), s.direct(1, ph, ts, 'ws'), s.s3(ph, ts, 'own', 'ws'),
-                 s.s3(ph, ts, 'fwdR', 'ws'), s.s3(ph, ts, 'fwdL', 'ws'), [s.sib(ph, ts, k, 'ws') for k in range(4)]))
+        s.each(lambda ts: s.got(ph, ts, 5), other=True)
+    def drain(s):
+        W = s.W
+        for ts, t in ((0, slice(0, 2)), (2, 0)):
+            def w(ts=ts, t=t):
+                k = 4 if ts == 2 else 0
+                wait(W.at[:, 0, 0, 0:3, 0, 0, t], s.ssem.at[k])
+                wait(W.at[:, 0, 0, 0:3, :, :, t], s.ssem.at[k + 1])
+                wait(W.at[:, :, :, 0:3, :, :, t], s.ssem.at[k + 2])
+                wait(W.at[:, :, :, :, :, :, t], s.ssem.at[k + 3])
+            if ts == 0: w()
+            else: pl.when(s.p.c == 0)(w)
+        o = s.s0_src()
+        for tc in (0, 1):
+            cond = (o <= 4) if tc == 0 else (o >= 4)
+            pl.when(cond)(lambda tc=tc: wait(s.pieces.at[:, 0:3], s.s0s.at[tc]))
+            pl.when(jnp.logical_and(cond, s.p.c != tc))(lambda: wait(s.pieces.at[:, 0], s.s0s.at[2]))
 
 def barrier(partners):
     b = pltpu.get_barrier_semaphore()
@@ -243,11 +220,11 @@
     def cps(s, k):
         p = s.p
         n = len(s.rings)
+        sems = (s.ssem.at[k], s.rsem.at[k])
         if k == 0 or k == n + 1:
             src = s.buf.at[1 - p.c] if k == 0 else s.buf.at[p.c]
-            dst = s.recv.at[0, 0] if k == 0 else s.recv.at[0, 1]
-            return [pltpu.make_async_remote_copy(src, dst, s.ssem.at[k, 0], s.rsem.at[k, 0], device_id=p.dev(c=1 - p.c), device_id_type=MESH)]
-        return [pltpu.make_async_remote_copy(s.buf.at[p.c], s.recv.at[k, i], s.ssem.at[k, i], s.rsem.at[k, i], device_id=dv, device_id_type=MESH)
+            return [pltpu.make_async_remote_copy(src, s.recv.at[0, 0 if k == 0 else 1], *sems, device_id=p.dev(c=1 - p.c), device_id_type=MESH)]
+        return [pltpu.make_async_remote_copy(s.buf.at[p.c], s.recv.at[k, i], *sems, device_id=dv, device_id_type=MESH)
                 for i, dv in enumerate(s.rings[k - 1])]
 
     def start(s, k):
@@ -256,23 +233,22 @@
     def finish(s, k):
         p = s.p
         n = len(s.rings)
-        cs = s.cps(k)
+        m = 1 if k in (0, n + 1) else len(s.rings[k - 1])
+        both = s.recv.at[0 if k == n + 1 else k, 0:m]
+        wait(both, s.rsem.at[k])
+        wait(both, s.ssem.at[k])
         if k == n + 1:
-            cs[0].wait_recv()
-            cs[0].wait_send()
             s.buf[1 - p.c] = s.recv[0, 1]
             return
-        for c in cs: c.wait_recv()
-        for c in cs: c.wait_send()
         acc = s.buf[p.c].astype(F32)
-        for i in range(len(cs)):
+        for i in range(m):
             acc = acc + s.recv[k, i].astype(F32)
         s.buf[p.c] = acc.astype(s.buf.dtype)
 
 
 class RS:
-    def __init__(s, p, G, RD, bufs, FR, EX, FIN, dss, drs, ss, rs, fs, fr):
-        s.p, s.G, s.RD, s.bufs, s.FR, s.EX, s.FIN = p, G, RD, bufs, FR, EX, FIN
+    def __init__(s, p, G, GW, RD, bufs, FR, EX, FIN, dss, drs, ss, rs, fs, fr):
+        s.p, s.G, s.GW, s.RD, s.bufs, s.FR, s.EX, s.FIN = p, G, GW, RD, bufs, FR, EX, FIN
         s.dss, s.drs, s.ss, s.rs, s.fs, s.fr = dss, drs, ss, rs, fs, fr
 
     def gref(s, ph):
@@ -288,11 +264,9 @@
         p = s.p
         g = s.gref(ph)
         t = 3 * (1 - p.c) + ts if act != 'recv' else 3 * p.c + ts
-        if True:
-            cp = pltpu.make_async_remote_copy(g.at[par, :, :, :, t], s.RD.at[ph, ts, par], s.dss.at[ph * 3 + ts, par], s.drs.at[ph * 3 + ts, par], device_id=p.dev(c=1 - p.c), device_id_type=MESH)
-            if act == 'start': cp.start()
-            elif act == 'ws': cp.wait_send()
-            else: cp.wait_recv()
+        cp = pltpu.make_async_remote_copy(g.at[par, :, :, :, t], s.RD.at[ph, ts, par], s.dss.at[ts // 2], s.drs.at[ph * 3 + ts, par], device_id=p.dev(c=1 - p.c), device_id_type=MESH)
+        if act == 'start': cp.start()
+        else: cp.wait_recv()
 
     def d2d_start(s, ph, par):
         for ts in range(3): s.go(ts, lambda ts=ts: s.d2d(ph, ts, 'start', par), other=True)
@@ -341,8 +315,8 @@
         if f == 1: return b.at[ph, 2, pl.ds(2 * hf, 2)]
         return b.at[ph, 2, hf]
 
-    def cp(s, src, dst, sl, k, dev):
-        return pltpu.make_async_remote_copy(src, dst, s.ss.at[sl, k], s.rs.at[sl, k], device_id=dev, device_id_type=MESH)
+    def cp(s, src, dst, sk, sl, k, dev):
+        return pltpu.make_async_remote_copy(src, dst, s.ss.at[sk], s.rs.at[sl, k], device_id=dev, device_id_type=MESH)
 
     def add(s, dst, srcs):
         lead = dst.shape[:-2]
@@ -358,9 +332,6 @@
             for r in srcs: acc = acc + r[...].astype(F32)
             dst[...] = acc.astype(BF)
 
-    def sem(s, st, i):
-        return (0, 4, 7)[st] + i
-
     def ring_cps(s, ph, ts, st):
         p = s.p
         o = s.order(ph, ts)
@@ -368,14 +339,15 @@
         f = s.fidx(ph, ts)
         sl = ph * 3 + ts
         b = s.bufs[f][st]
+        sk = st + (3 if ts == 2 else 0)
         if ax == 0:
             k = 1 - p.xl
             src, dv = s.piece(ph, ts, st, k), p.dev(x=p.xh * 2 + k)
-            if st == 0: return [s.cp(src.at[par], b.at[ph, 0, par], sl, par, dv) for par in range(2)]
-            return [s.cp(src, b.at[ph, 0], sl, s.sem(st, 0), dv)]
+            if st == 0: return [s.cp(src.at[par], b.at[ph, 0, par], sk, sl, par, dv) for par in range(2)]
+            return [s.cp(src, b.at[ph, 0], sk, sl, 2 + st, dv)]
         res = []
         for i, d in enumerate((1, 3, 2)):
-            res.append(s.cp(s.piece(ph, ts, st, p.coord(ax, d)), b.at[ph, i], sl, s.sem(st, i), p.ring(ax, d)))
+            res.append(s.cp(s.piece(ph, ts, st, p.coord(ax, d)), b.at[ph, i], sk, sl, 2 + st, p.ring(ax, d)))
         return res
 
     def first_a(s, ph, ts, par):
@@ -394,16 +366,16 @@
         ax = s.order(ph, ts)[0]
         sl = ph * 3 + ts
         k = p.coord(ax, 2)
-        return [s.cp(s.half(ph, ts, 0, k, 1), s.bhalf(ph, ts, 1), sl, 2, p.ring(ax, 1)),
-                s.cp(s.half(ph, ts, 0, k, 0), s.bhalf(ph, ts, 0), sl, 3, p.ring(ax, 3))]
+        return [s.cp(s.half(ph, ts, 0, k, 1), s.bhalf(ph, ts, 1), 0, sl, 0, p.ring(ax, 1)),
+                s.cp(s.half(ph, ts, 0, k, 0), s.bhalf(ph, ts, 0), 0, sl, 1, p.ring(ax, 3))]
 
     def sf_full(s, ph, ts):
         p = s.p
         ax = s.order(ph, ts)[0]
         sl = ph * 3 + ts
         b = s.bufs[s.fidx(ph, ts)][0]
-        return [s.cp(s.piece(ph, ts, 0, p.coord(ax, 1)), b.at[ph, 0], sl, 0, p.ring(ax, 1)),
-                s.cp(s.piece(ph, ts, 0, p.coord(ax, 3)), b.at[ph, 1], sl, 1, p.ring(ax, 3))]
+        return [s.cp(s.piece(ph, ts, 0, p.coord(ax, 1)), b.at[ph, 0], 0, sl, 2, p.ring(ax, 1)),
+                s.cp(s.piece(ph, ts, 0, p.coord(ax, 3)), b.at[ph, 1], 0, sl, 2, p.ring(ax, 3))]
 
     def first_b(s, ph, ts):
         p = s.p
@@ -430,9 +402,8 @@
                 c.wait_recv()
                 s.add(s.piece(ph, ts, 0, me).at[par], [b.at[ph, 0, par]])
             return
-        cs = s.sf_full(ph, ts)
-        for c in cs: c.wait_recv()
-        s.add(s.piece(ph, ts, 0, me), [b.at[ph, i] for i in range(len(cs))])
+        wait(b.at[ph, 0:2], s.rs.at[ph * 3 + ts, 2])
+        s.add(s.piece(ph, ts, 0, me), [b.at[ph, i] for i in range(2)])
 
     def next_start(s, ph, ts, st):
         for c in s.ring_cps(ph, ts, st): c.start()
@@ -442,9 +413,8 @@
         ax = s.order(ph, ts)[st]
         me = (p.xl, p.y, p.z)[ax]
         b = s.bufs[s.fidx(ph, ts)][st]
-        cs = s.ring_cps(ph, ts, st)
-        for c in cs: c.wait_recv()
-        s.add(s.piece(ph, ts, st, me), [b.at[ph, i] for i in range(len(cs))])
+        wait(b.at[ph], s.rs.at[ph * 3 + ts, 2 + st])
+        s.add(s.piece(ph, ts, st, me), [b.at[ph, i] for i in range(1 if ax == 0 else 3)])
 
     def each(s, f):
         for ts in range(3): s.go(ts, lambda ts=ts: f(ts))
@@ -465,7 +435,7 @@
         o = 4 * p.c + k
         chunk = 2 * p.xh + p.par
         dev = p.dev(x=(o % 2) * 2 + p.xl, y=2 * p.h + o // 4, c=(o // 2) % 2)
-        return pltpu.make_async_remote_copy(s.EX.at[ph, k], s.FIN.at[ph, chunk, p.c], s.fs.at[ph, k], s.fr.at[ph, chunk * 2 + p.c], device_id=dev, device_id_type=MESH)
+        return pltpu.make_async_remote_copy(s.EX.at[ph, k], s.FIN.at[ph, chunk, p.c], s.fs.at[0], s.fr.at[ph, p.c], device_id=dev, device_id_type=MESH)
 
     def myo(s):
         p = s.p
@@ -500,31 +470,28 @@
     def final_wait(s, ph):
         p = s.p
         o = s.myo()
-        for chunk in range(4):
-            for sc in range(2):
-                c1 = (o <= 4) if sc == 0 else (o >= 4)
-                mine = jnp.logical_and(chunk == 2 * p.xh + p.par, sc == p.c)
-                @pl.when(jnp.logical_and(c1, jnp.logical_not(mine)))
-                def _(chunk=chunk, sc=sc):
-                    pltpu.make_async_remote_copy(s.EX.at[ph, 0], s.FIN.at[ph, chunk, sc], s.fs.at[ph, 0], s.fr.at[ph, chunk * 2 + sc], device_id=p.dev(c=1 - p.c), device_id_type=MESH).wait_recv()
-
-    def drain(s, ph):
-        p = s.p
-        for ts in range(3):
-            for par in range(2): s.go(ts, lambda ts=ts: s.d2d(ph, ts, 'ws', par), other=True)
-            def ws(ts=ts):
-                if s.order(ph, ts)[0] == 0:
-                    for c in s.ring_cps(ph, ts, 0): c.wait_send()
-                else:
-                    for c in s.sf_half(ph, ts) + s.sf_full(ph, ts): c.wait_send()
-                for st in (1, 2):
-                    for c in s.ring_cps(ph, ts, st): c.wait_send()
-            s.go(ts, ws)
-        for k in range(5):
-            def w(k=k):
-                pl.when(4 * p.c + k != s.myo())(lambda: s.fin_cps(ph, k).wait_send())
-            if k < 4: w()
-            else: pl.when(p.c == 0)(w)
+        for sc in range(2):
+            used = (o <= 4) if sc == 0 else (o >= 4)
+            pl.when(jnp.logical_and(used, p.c == sc))(lambda: wait(s.FIN.at[ph, 0:3, 0], s.fr.at[ph, sc]))
+            pl.when(jnp.logical_and(used, p.c != sc))(lambda: wait(s.FIN.at[ph, :, 0], s.fr.at[ph, sc]))
+
+    def drain(s):
+        p = s.p
+        G = s.GW
+        wait(G.at[:, :, :, :, :, 0:2], s.dss.at[0])
+        pl.when(p.c == 1)(lambda: wait(G.at[:, :, :, :, :, 0], s.dss.at[1]))
+        wait(G.at[:, :, 0:3, :, :, 0:2], s.ss.at[0])
+        wait(G.at[:, 0, :, 0, 0, 0:2], s.ss.at[1])
+        wait(G.at[:, 0, 0:3, 0, 0, 0:2], s.ss.at[2])
+        @pl.when(p.c == 0)
+        def _():
+            wait(G.at[:, :, :, :, 0, 0], s.ss.at[3])
+            wait(G.at[:, 0, 0:3, :, :, 0], s.ss.at[4])
+            wait(G.at[:, 0, 0:3, 0, 0, 0], s.ss.at[5])
+        o = s.myo()
+        n = jnp.where(p.c == 0, jnp.where(o <= 4, 4, 5), jnp.where(o >= 4, 3, 4))
+        for k in (3, 4, 5):
+            pl.when(n == k)(lambda k=k: wait(s.EX.at[:, 0:k], s.fs.at[0]))
 
 
 def clear_last(stg, FR):
@@ -542,13 +509,13 @@
 
 
 def block_body(lat_in, cot_in, sid, small_in, o_lat, o_in, small_out,
-                 W, stg, pieces, A, N1, N2, MID, DG, PR, I1, I2, VEC, CS, G2, RD, b00, b01, b02, b10, b11, b12, b20, b21, b22,
+                 W, stg, pieces, A, N1, N2, MID, DG, PR, I1, I2, VEC, CS, GW, RD, b00, b01, b02, b10, b11, b12, b20, b21, b22,
                  FR, EX, FIN, SB, SBR, SG, SGR,
                  lat, cot, gt, b1, g2, b2, wq, wo, wu, wd, o_tab, o_vec, o_qkv, o_out, o_up, o_down, ssem, rsem, s0s, s0r, dss, drs, gss, grs, fs, fr, sbs, sbr, sgs, sgr, io):
     p = Pos()
     ag = AG(p, W, stg, pieces, ssem, rsem, None, s0s, s0r)
-    G = [W.at[2, 0], W.at[2, 1], G2]
-    rs = RS(p, G, RD, [[b00, b01, b02], [b10, b11, b12], [b20, b21, b22]], FR, EX, FIN, dss, drs, gss, grs, fs, fr)
+    G = [GW.at[0], GW.at[1], GW.at[2]]
+    rs = RS(p, G, GW, RD, [[b00, b01, b02], [b10, b11, b12], [b20, b21, b22]], FR, EX, FIN, dss, drs, gss, grs, fs, fr)
     ring3 = lambda ax: [p.ring(ax, d) for d in (1, 3, 2)]
     sb = Small(p, SB, SBR, sbs, sbr, [ring3(0), ring3(1), ring3(2)])
     sg = Small(p, SG, SGR, sgs, sgr, [ring3(1), ring3(2), [p.dev(x=p.xh * 2 + 1 - p.xl)]])
@@ -576,7 +543,7 @@
     pl.semaphore_wait(bar, len(parts))
 
     sb.start(0)
-    for ph in range(3): ag.s0(ph, 'start')
+    for ph in range(3): ag.s0(ph)
 
     def ln1(r, _):
         rows = pl.ds(pl.multiple_of(r * RB, RB), RB)
@@ -693,27 +660,21 @@
             acc = t if acc is None else acc + t
         return acc
 
+    half = pl.ds(pl.multiple_of(p.xh * CW, 128), CW)
+
+    def wgrad(ph, par, left, right):
+        for n in range(2):
+            v = dot_tn(A[left, :, cols(n)], right[:, half])
+            G[ph][par, 2 * n:2 * n + 2] = v.astype(BF).reshape(2, 2, 2, 5, 16, CW)
+        rs.d2d_start(ph, par)
+
+    wgrad(2, 1, ACTIVE, cot)
     for n in range(2):
         A[GU, :, cols(n)] = (back(lambda par: cot[:, cols(par)], 2, 1, n) * DG[:, cols(n)]).astype(BF)
-
-    def wgrad(ph, l0, l1, r0, r1, par):
-        li = jnp.where(p.xh == 0, l0, l1)
-        ri = jnp.where(p.xh == 0, r0, r1)
-        for n in range(2):
-            v = dot_tn(A[li, :, cols(n)], A[ri, :, cols(par)])
-            G[ph][par, 2 * n:2 * n + 2] = v.astype(BF).reshape(2, 2, 2, 5, 16, CW)
-        rs.d2d_start(ph, par)
-
-    A[GAO] = cot[...]
-    wgrad(2, SECOND, ACTIVE, GU, GAO, 0)
-    wgrad(2, SECOND, ACTIVE, GU, GAO, 1)
+    wgrad(2, 0, SECOND, A.at[GU])
     for n in range(2):
         DG[:, cols(n)] = back(lambda par: A[GU, :, cols(par)], 2, 0, n)
-        rs.first(2, n)
-    for par in range(2):
-        A[SECOND, :, cols(par)] = (MID[:, cols(par)] + dot(A[ACTIVE], wpan(2, 1, par))).astype(BF)
-    out_lat = pltpu.make_async_copy(A.at[SECOND], o_lat, io.at[2])
-    out_lat.start()
+        rs.first(2, 1 - n)
 
     def ln2b(r, _):
         rows = pl.ds(pl.multiple_of(r * RB, RB), RB)
@@ -729,11 +690,14 @@
         A[GAO, rows, :] = gm.astype(BF)
         return 0
     lax.fori_loop(0, L // RB, ln2b, 0)
+    wgrad(1, 1, MIXED, A.at[GAO])
     for n in range(2):
         A[GMX, :, cols(n)] = back(lambda par: A[GAO, :, cols(par)], 1, 1, n).astype(BF)
-        if n == 0: rs.step(2, 2)
-
-    for pn in range(2):
+    rs.step(2, 2)
+    rs.first(1, 1)
+
+    for i in range(2):
+        pn = p.xh if i == 0 else 1 - p.xh
         def attb(w, _, pn=pn):
             cw = win(pn, w)
             m32, m16 = masks(w)
@@ -747,31 +711,28 @@
             A[GQ, :, cw] = A[GQ, :, cw] + (dot(gsc, A[K, :, cw]) * SCALE * m32).astype(BF)
             A[GK, :, cw] = A[GK, :, cw] + (dot_tn(gsc, qm) * SCALE).astype(BF)
             return 0
-        if pn == 0:
-            lax.fori_loop(0, 4, attb, 0, unroll=True)
-            ag.drain(2)
-        else:
-            lax.fori_loop(0, 2, attb, 0, unroll=True)
+        lax.fori_loop(0, 4, attb, 0, unroll=True)
+        if i == 0:
+            wgrad(1, 0, FIRST, A.at[GV])
+            wgrad(0, 0, FIRST, A.at[GQ])
+            wgrad(0, 1, FIRST, A.at[GK])
+            rs.step(2, 3)
             rs.first(1, 0)
             rs.first(0, 0)
-            lax.fori_loop(2, 4, attb, 0, unroll=True)
-        wgrad(1, FIRST, MIXED, GV, GAO, pn)
-        wgrad(0, FIRST, FIRST, GQ, GK, pn)
-        rs.step(2, 3 + pn)
+            rs.first(0, 1)
+    rs.step(1, 2)
     for n in range(2):
         acc = None
         for g, (ph, xh) in ((GQ, (0, 0)), (GK, (0, 1)), (GV, (1, 0))):
             t = back(lambda par: A[g, :, cols(par)], ph, xh, n)
             acc = t if acc is None else acc + t
-        MID[:, cols(n)] = acc
-        rs.first(1 - n, 1)
-    rs.step(1, 2)
+        DG[:, cols(n)] = acc
+        if n == 0: rs.step(2, 4)
     rs.step(0, 2)
-    rs.step(2, 5)
 
     def ln1b(r, _):
         rows = pl.ds(pl.multiple_of(r * RB, RB), RB)
-        gf = MID[rows, :]
+        gf = DG[rows, :]
         n = N1[rows, :]
         CS[3] += jnp.sum((gf * n).reshape(RB // 8, 8, D), axis=0)
         CS[0] += jnp.sum(gf.reshape(RB // 8, 8, D), axis=0)
@@ -789,9 +750,14 @@
         SG[k] = (jnp.where(sub24 == sid[0], v[3], 0.0) + jnp.where(sub24 == 16, v[0], 0.0)
                  + jnp.where(sub24 == 17, v[1], 0.0) + jnp.where(sub24 == 18, v[2], 0.0))
     sg.start(0)
-    ag.drain(0); ag.drain(1)
     rs.step(1, 3)
+    rs.step(2, 5)
+    for par in range(2):
+        A[SECOND, :, cols(par)] = (MID[:, cols(par)] + dot(A[ACTIVE], wpan(2, 1, par))).astype(BF)
+    out_lat = pltpu.make_async_copy(A.at[SECOND], o_lat, io.at[2])
+    out_lat.start()
     sg.finish(0); sg.start(1)
+    ag.drain()
     rs.step(0, 3)
     rs.step(1, 4)
     sg.finish(1); sg.start(2)
@@ -809,10 +775,10 @@
         def _():
             FIN[ph, :, 0] = FIN[ph, :, 0] + FIN[ph, :, 1]
         for xh in range(2):
-            o, off = outs[2 * ph + xh]
             for par in range(2):
+                o, off = outs[2 * ph + par]
                 v = FIN[ph, 2 * xh + par, sel].astype(F32)
-                o[:, off + par * 640: off + (par + 1) * 640] = v[0:10]
+                o[:, off + xh * 640: off + (xh + 1) * 640] = v[0:10]
     emit(2)
     sg.finish(3); sg.start(4)
     emit(1)
@@ -828,7 +794,7 @@
     emit(0)
     outs = [pltpu.make_async_copy(v, o, io.at[4 + i]) for i, (v, o) in enumerate(zip((o_tab, o_vec, o_qkv, o_out, o_up, o_down), small_out))]
     for c in outs: c.start()
-    for ph in range(3): rs.drain(ph)
+    rs.drain()
     out_lat.wait(); out_in.wait()
     for c in outs: c.wait()
 
@@ -849,7 +815,7 @@
         V_((3, 2, 2, 4, 2, 2, 5, 16, CW), BF), V_((3, 5) + blk, BF), V_((3, 4) + blk, BF),
         V_((13, L, D), BF), V_((L, D), F32), V_((L, D), F32), V_((L, D), F32), V_((L, D), F32),
         V_((8, 256, 256), F32), V_((L, 128), F32), V_((L, 128), F32), V_((8, D), F32), V_((4, 8, D), F32),
-        V_((2, 4, 2, 2, 5) + blk, BF), V_((3, 3, 2, 4, 2, 2) + blk, BF),
+        V_((3, 2, 4, 2, 2, 5) + blk, BF), V_((3, 3, 2, 4, 2, 2) + blk, BF),
         V_((3, 1, 2, 4, 2) + blk, BF), V_((3, 3, 4) + blk, BF), V_((3, 3) + blk, BF),
         V_((3, 3, 4, 2) + blk, BF), V_((3, 1, 4) + blk, BF), V_((3, 3) + blk, BF),
         V_((3, 3, 2, 2, 2) + blk, BF), V_((3, 1, 2, 2) + blk, BF), V_((3, 3) + blk, BF),
@@ -857,9 +823,9 @@
         V_((2, 32, 640), BF), V_((4, 3, 32, 640), BF), V_((2, 24, 640), F32), V_((4, 3, 24, 640), F32), V_((L, D), BF), V_((L, D), BF),
         V_((10, 16), BF), V_((10,), BF), V_((10,), BF), V_((10,), BF), V_((10, 3 * D), BF), V_((10, D), BF), V_((10, D), BF), V_((10, D), BF),
         V_((10, 16), F32), V_((8, 10), F32), V_((10, 3 * D), F32), V_((10, D), F32), V_((10, D), F32), V_((10, D), F32),
-        dma((9, 14)), dma((9, 14)), dma((3, 8)), dma((3, 5)),
-        dma((9, 2)), dma((9, 2)), dma((9, 10)), dma((9, 10)), dma((3, 5)), dma((3, 8)),
-        dma((5, 3)), dma((5, 3)), dma((5, 3)), dma((5, 3)), dma((12,)),
+        dma((8,)), dma((9, 6)), dma((3,)), dma((3,)),
+        dma((2,)), dma((9, 2)), dma((6,)), dma((9, 5)), dma((1,)), dma((3, 2)),
+        dma((5,)), dma((5,)), dma((5,)), dma((5,)), dma((12,)),
     ]
     vm = pl.BlockSpec(memory_space=pltpu.VMEM)
     sm = pl.BlockSpec(memory_space=pltpu.SMEM)

time: 127 us -> 121 us (0.953)
  Pallas kernels: 126 us -> 120 us
    pallas_call x1, Pallas kernels: 122 us -> 116 us  [per_device(): pl.pallas_call(block_kernel, out_shape=[jax.ShapeDtypeStruct((L, D), BF),...]
where the time goes in v4:
time: 121 us
  Pallas kernels  120 us (99%)
  between operations  1.46 us (1%)
    pallas_call x1, Pallas kernels, per_device(): pl.pallas_call(block_kernel, out_shape=[jax.ShapeDtypeStruct((L, D), BF),...  116 us
    pallas_call x1, Pallas kernels, per_device(): pl.pallas_call(results_kernel, out_shape=[jax.ShapeDtypeStruct((L, D), BF...  3.73 us

profile of v4, /device:TPU:1, one launch (start us, length us, event | category | flops | bytes accessed | tf_op | source)
XLA Modules:
  0.0 121.1 jit_solution(4013644475398208070)
XLA Ops:
  1.3 115.9 %block.1 = (bf16[256,1280]{1,0:T(8,128)(2,1)}, f32[256,1280]{1,0:T(8,128)}, f32[10,16]{1,0:T(8,128)}, f32[8,10]{1,0:T(8,128)}, f32[10,3840]{1,0:T(8,128)}, /*ind...) custom-call(bf16[256,1280]{1,0:T(8,128)(2,1)} %bitcast.4, bf16[256,1280]{1,0:T(8,128)(2,1)} %bitcast.5, ...), custom_call_target="tpu_custom_call" | custom-call | tf_op jit(solution)/shard_map/block/pallas_call | solution.py:834
  117.2 3.7 %results.1 = (bf16[256,1280]{1,0:T(8,128)(2,1)}, f32[256,1280]{1,0:T(8,128)}, f32[10,16]{1,0:T(8,128)}, f32[10]{0:T(128)}, f32[10]{0:T(128)}, /*index=5*/f32[10]...) custom-call(bf16[256,1280]{1,0:T(8,128)(2,1)} %get-tuple-element.28.lat, ...), custom_call_target="tpu_custom_call" | custom-call | tf_op jit(solution)/shard_map/results/pallas_call | solution.py:843

commit v5 on v4

--- a/solution.py
+++ b/solution.py
@@ -213,37 +213,110 @@
     return lax.dot_general(a, b, (((0,), (0,)), ((), ())), preferred_element_type=F32)
 
 
-class Small:
-    def __init__(s, p, buf, recv, ssem, rsem, rings):
-        s.p, s.buf, s.recv, s.ssem, s.rsem, s.rings = p, buf, recv, ssem, rsem, rings
-
-    def cps(s, k):
-        p = s.p
-        n = len(s.rings)
-        sems = (s.ssem.at[k], s.rsem.at[k])
-        if k == 0 or k == n + 1:
-            src = s.buf.at[1 - p.c] if k == 0 else s.buf.at[p.c]
-            return [pltpu.make_async_remote_copy(src, s.recv.at[0, 0 if k == 0 else 1], *sems, device_id=p.dev(c=1 - p.c), device_id_type=MESH)]
-        return [pltpu.make_async_remote_copy(s.buf.at[p.c], s.recv.at[k, i], *sems, device_id=dv, device_id_type=MESH)
-                for i, dv in enumerate(s.rings[k - 1])]
+def at128(v):
+    return pl.multiple_of(v, 128)
+
+
+def window(z, xl):
+    return 320 * z - 64 * (z % 2) + 128 * xl
+
+
+class Spread:
+    def __init__(s, p, T, R0, R1, R2, T3, R3, out, ssem, rsem):
+        s.p, s.T, s.T3, s.out, s.ssem, s.rsem = p, T, T3, out, ssem, rsem
+        s.R = (R0, R1, R2, R3)
 
     def start(s, k):
-        for c in s.cps(k): c.start()
+        p = s.p
+        src = s.T3 if k == 3 else s.T
+        if k == 0: devs = [p.dev(c=1 - p.c)]
+        else: devs = [p.ring((1, 0, 2)[k - 1], d) for d in (1, 2, 3)]
+        for i, dv in enumerate(devs):
+            pltpu.make_async_remote_copy(src, s.R[k].at[i], s.ssem.at[k], s.rsem.at[k], device_id=dv, device_id_type=MESH).start()
 
     def finish(s, k):
         p = s.p
-        n = len(s.rings)
-        m = 1 if k in (0, n + 1) else len(s.rings[k - 1])
-        both = s.recv.at[0 if k == n + 1 else k, 0:m]
-        wait(both, s.rsem.at[k])
-        wait(both, s.ssem.at[k])
-        if k == n + 1:
-            s.buf[1 - p.c] = s.recv[0, 1]
+        R = s.R[k]
+        wait(R, s.rsem.at[k])
+        wait(R, s.ssem.at[k])
+        if k < 2:
+            acc = s.T[...].astype(F32)
+            for i in range(R.shape[0]): acc = acc + R[i].astype(F32)
+            s.T[...] = acc.astype(BF)
+        elif k == 2:
+            s.T3[...] = jnp.zeros((32, 384), BF)
+            mine = pl.ds(at128(128 * p.xl), 256)
+            other = pl.ds(at128(128 - 128 * p.xl), 256)
+            s.T3[:, mine] = (s.T[...].astype(F32) + R[1].astype(F32)).astype(BF)
+            s.T3[:, other] = (s.T3[:, other].astype(F32) + R[0].astype(F32) + R[2].astype(F32)).astype(BF)
+        else:
+            s.out[...] = jnp.zeros((32, D), BF)
+            for i in range(4):
+                lanes = pl.ds(at128(window((p.z + 4 - i) % 4, 0)), 384)
+                v = s.T3[...] if i == 0 else R[i - 1]
+                s.out[:, lanes] = (s.out[:, lanes].astype(F32) + v.astype(F32)).astype(BF)
+
+
+class Gather:
+    def __init__(s, p, buf, R0, R1, S1, R2, S2, R3, R4, ssem, rsem):
+        s.p, s.buf, s.R0, s.R1, s.S1, s.R2, s.S2, s.R3, s.R4 = p, buf, R0, R1, S1, R2, S2, R3, R4
+        s.ssem, s.rsem = ssem, rsem
+        s.active = p.z // 2 == p.c
+
+    def send(s, k, src, dst, dv):
+        pltpu.make_async_remote_copy(src, dst, s.ssem.at[k], s.rsem.at[k], device_id=dv, device_id_type=MESH).start()
+
+    def start(s, k):
+        p = s.p
+        if k == 0:
+            s.send(0, s.buf.at[1 - p.c], s.R0, p.dev(c=1 - p.c))
+        elif k == 1:
+            for d in (1, 2, 3):
+                z = (p.z + d) % 4
+                @pl.when(z // 2 == p.c)
+                def _(z=z, d=d):
+                    s.send(1, s.buf.at[p.c, :, pl.ds(at128(256 * (z % 2)), 384)], s.R1.at[d - 1], p.dev(z=z))
+        else:
+            @pl.when(s.active)
+            def _():
+                if k == 2:
+                    s.send(2, s.S1.at[:, pl.ds(at128(128 - 128 * p.xl), 256)], s.R2, p.dev(x=p.xh * 2 + 1 - p.xl))
+                elif k == 3:
+                    for d in (1, 2, 3): s.send(3, s.S2, s.R3.at[d - 1], p.ring(1, d))
+                else:
+                    s.send(4, s.S2, s.R4, p.dev(c=1 - p.c))
+
+    def finish(s, k):
+        p = s.p
+        if k == 0:
+            wait(s.R0, s.rsem.at[0])
+            wait(s.R0, s.ssem.at[0])
+            s.buf[p.c] = s.buf[p.c] + s.R0[...]
             return
-        acc = s.buf[p.c].astype(F32)
-        for i in range(m):
-            acc = acc + s.recv[k, i].astype(F32)
-        s.buf[p.c] = acc.astype(s.buf.dtype)
+        if k == 1:
+            pl.when(s.active)(lambda: wait(s.R1.at[0], s.ssem.at[1]))
+            pl.when(jnp.logical_not(s.active))(lambda: wait(s.R1.at[0:2], s.ssem.at[1]))
+        if k == 4:
+            @pl.when(jnp.logical_not(s.active))
+            def _():
+                wait(s.R4, s.rsem.at[4])
+                s.S2[...] = s.R4[...]
+            pl.when(s.active)(lambda: wait(s.R4, s.ssem.at[4]))
+            return
+        @pl.when(s.active)
+        def _():
+            if k == 1:
+                wait(s.R1, s.rsem.at[1])
+                mine = pl.ds(at128(256 * (p.z % 2)), 384)
+                s.S1[...] = s.buf[p.c, :, mine] + s.R1[0] + s.R1[1] + s.R1[2]
+            elif k == 2:
+                wait(s.R2, s.rsem.at[2])
+                wait(s.R2, s.ssem.at[2])
+                s.S2[...] = s.S1[:, pl.ds(at128(128 * p.xl), 256)] + s.R2[...]
+            else:
+                wait(s.R3, s.rsem.at[3])
+                wait(s.R3, s.ssem.at[3])
+                s.S2[...] = s.S2[...] + s.R3[0] + s.R3[1] + s.R3[2]
 
 
 class RS:
@@ -501,6 +574,7 @@
 
 FIRST, Q, K, V, MIXED, SECOND, ACTIVE, GU, GAO, GMX, GQ, GK, GV = range(13)
 RB = 32
+UNROLL = 4
 
 
 def block_kernel(lat_in, cot_in, sid, *refs):
@@ -508,17 +582,16 @@
     block_body(lat_in, cot_in, sid, small_in, o_lat, o_in, small_out, *refs[16:])
 
 
-def block_body(lat_in, cot_in, sid, small_in, o_lat, o_in, small_out,
+def block_body(lat_in, cot_in, sid_in, small_in, o_lat, o_in, small_out,
                  W, stg, pieces, A, N1, N2, MID, DG, PR, I1, I2, VEC, CS, GW, RD, b00, b01, b02, b10, b11, b12, b20, b21, b22,
-                 FR, EX, FIN, SB, SBR, SG, SGR,
-                 lat, cot, gt, b1, g2, b2, wq, wo, wu, wd, o_tab, o_vec, o_qkv, o_out, o_up, o_down, ssem, rsem, s0s, s0r, dss, drs, gss, grs, fs, fr, sbs, sbr, sgs, sgr, io):
+                 FR, EX, FIN, SB, SBT, SB0, SB1, SB2, SBT3, SB3, SG, SG0, SG1, SGS1, SG2, SGS2, SG3, SG4,
+                 lat, cot, sid, gt, b1, g2, b2, wq, wo, wu, wd, o_tab, o_vec, o_qkv, o_out, o_up, o_down, ssem, rsem, s0s, s0r, dss, drs, gss, grs, fs, fr, sbs, sbr, sgs, sgr, io):
     p = Pos()
     ag = AG(p, W, stg, pieces, ssem, rsem, None, s0s, s0r)
     G = [GW.at[0], GW.at[1], GW.at[2]]
     rs = RS(p, G, GW, RD, [[b00, b01, b02], [b10, b11, b12], [b20, b21, b22]], FR, EX, FIN, dss, drs, gss, grs, fs, fr)
-    ring3 = lambda ax: [p.ring(ax, d) for d in (1, 3, 2)]
-    sb = Small(p, SB, SBR, sbs, sbr, [ring3(0), ring3(1), ring3(2)])
-    sg = Small(p, SG, SGR, sgs, sgr, [ring3(1), ring3(2), [p.dev(x=p.xh * 2 + 1 - p.xl)]])
+    sb = Spread(p, SBT, SB0, SB1, SB2, SBT3, SB3, SB, sbs, sbr)
+    sg = Gather(p, SG, SG0, SG1, SGS1, SG2, SGS2, SG3, SG4, sgs, sgr)
     idx = lax.axis_index("dp") * 2 + p.xh
 
     parts = ag.partners()
@@ -527,19 +600,20 @@
         pl.semaphore_signal(bar, inc=1, device_id=d, device_id_type=MESH)
     in_lat = pltpu.make_async_copy(lat_in, lat, io.at[0])
     in_cot = pltpu.make_async_copy(cot_in, cot, io.at[1])
+    in_sid = pltpu.make_async_copy(sid_in, sid, io.at[12])
+    in_sid.start()
     ins = [pltpu.make_async_copy(a, v, io.at[4 + i]) for i, (a, v) in enumerate(zip(small_in, (gt, b1, g2, b2, wq, wo, wu, wd)))]
     for c in ins: c.start()
     in_lat.start(); in_cot.start()
     for c in ins: c.wait()
     fill_pieces(pieces, wq, wo, wu, wd)
     pl.when(p.c == 1)(lambda: clear_last(stg, FR))
-    j = lax.broadcasted_iota(jnp.int32, (16, D), 0)
-    lane = lax.broadcasted_iota(jnp.int32, (16, D), 1)
+    j = lax.broadcasted_iota(jnp.int32, (16, 256), 0)
+    lane = lax.broadcasted_iota(jnp.int32, (16, 256), 1) + window(p.z, p.xl)
     own = jnp.where(jnp.logical_and(lane == idx * 10 + j, j < 10), 1.0, 0.0)
     own16 = own[0:10].astype(BF)
-    spread = [dot_tn(gt[...], own16)] + [dot(jnp.broadcast_to(b[...].reshape(1, 10), (8, 10)), own16)[0:1] for b in (b1, g2, b2)] + [jnp.zeros((13, D), F32)]
-    spread = jnp.concatenate(spread, axis=0).astype(BF)
-    for k in range(2): SB[k] = spread[:, k * 640:(k + 1) * 640]
+    spread = [dot_tn(gt[...], own16)] + [dot(jnp.broadcast_to(b[...].reshape(1, 10), (8, 10)), own16)[0:1] for b in (b1, g2, b2)] + [jnp.zeros((13, 256), F32)]
+    SBT[...] = jnp.concatenate(spread, axis=0).astype(BF)
     pl.semaphore_wait(bar, len(parts))
 
     sb.start(0)
@@ -554,8 +628,8 @@
         N1[rows, :] = xc * inv
         I1[rows, :] = jnp.broadcast_to(inv, (RB, 128))
         return 0
-    in_lat.wait(); in_cot.wait()
-    lax.fori_loop(0, L // RB, ln1, 0)
+    in_lat.wait(); in_cot.wait(); in_sid.wait()
+    lax.fori_loop(0, L // RB, ln1, 0, unroll=UNROLL)
     ag.s0_recv(0); ag.compact(0); ag.phase_a(0)
     sb.finish(0); sb.start(1)
     ag.s0_recv(1); ag.compact(1); ag.phase_a(1)
@@ -567,24 +641,23 @@
     sb.finish(2); sb.start(3)
     ag.phase_b(2)
     ag.phase_c(1)
-    sb.finish(3); sb.start(4)
     A[MIXED] = jnp.zeros((L, D), BF)
     for k in (GQ, GK, GV): A[k] = jnp.zeros((L, D), BF)
     CS[...] = jnp.zeros_like(CS)
     ag.phase_d(0)
     ag.phase_c(2)
-    sb.finish(4)
+    sb.finish(3)
     lane32 = lax.broadcasted_iota(jnp.int32, (8, 32), 1)
     sub8 = lax.broadcasted_iota(jnp.int32, (8, 32), 0)
     tgt = jnp.where(sub8 == 0, sid[0], jnp.where(sub8 < 4, 15 + sub8, -1))
     pick = jnp.where(lane32 == tgt, 1.0, 0.0).astype(BF)
-    for k in range(2): VEC[:, k * 640:(k + 1) * 640] = dot(pick, SB[k])
+    VEC[...] = dot(pick, SB[...])
 
     def mk_first(r, _):
         rows = pl.ds(pl.multiple_of(r * RB, RB), RB)
         A[FIRST, rows, :] = (N1[rows, :] * VEC[0:1, :] + VEC[1:2, :]).astype(BF)
         return 0
-    lax.fori_loop(0, L // RB, mk_first, 0)
+    lax.fori_loop(0, L // RB, mk_first, 0, unroll=UNROLL)
     ag.phase_d(1)
     ag.phase_e(0)
     ag.phase_f(0)
@@ -636,7 +709,7 @@
         I2[rows, :] = jnp.broadcast_to(inv, (RB, 128))
         A[SECOND, rows, :] = (n * VEC[2:3, :] + VEC[3:4, :]).astype(BF)
         return 0
-    lax.fori_loop(0, L // RB, ln2, 0)
+    lax.fori_loop(0, L // RB, ln2, 0, unroll=UNROLL)
     ag.phase_f(2)
     for par in range(2):
         DG[:, cols(par)] = dot(A[SECOND], wpan(2, 0, par))
@@ -651,7 +724,7 @@
         A[ACTIVE, rows, :] = (u * hp).astype(BF)
         DG[rows, :] = hp + 0.5 * u * (1.0 - th * th) * (c0 * (1.0 + 3 * 0.044715 * u2))
         return 0
-    lax.fori_loop(0, L // RB, gelu, 0)
+    lax.fori_loop(0, L // RB, gelu, 0, unroll=UNROLL)
 
     def back(src, ph, xh, n):
         acc = None
@@ -674,7 +747,8 @@
     wgrad(2, 0, SECOND, A.at[GU])
     for n in range(2):
         DG[:, cols(n)] = back(lambda par: A[GU, :, cols(par)], 2, 0, n)
-        rs.first(2, 1 - n)
+
+    rs.first(2, 1)
 
     def ln2b(r, _):
         rows = pl.ds(pl.multiple_of(r * RB, RB), RB)
@@ -689,12 +763,11 @@
         N2[rows, :] = gm
         A[GAO, rows, :] = gm.astype(BF)
         return 0
-    lax.fori_loop(0, L // RB, ln2b, 0)
+    lax.fori_loop(0, L // RB, ln2b, 0, unroll=UNROLL)
     wgrad(1, 1, MIXED, A.at[GAO])
     for n in range(2):
         A[GMX, :, cols(n)] = back(lambda par: A[GAO, :, cols(par)], 1, 1, n).astype(BF)
-    rs.step(2, 2)
-    rs.first(1, 1)
+        if n == 0: rs.first(2, 0)
 
     for i in range(2):
         pn = p.xh if i == 0 else 1 - p.xh
@@ -711,24 +784,29 @@
             A[GQ, :, cw] = A[GQ, :, cw] + (dot(gsc, A[K, :, cw]) * SCALE * m32).astype(BF)
             A[GK, :, cw] = A[GK, :, cw] + (dot_tn(gsc, qm) * SCALE).astype(BF)
             return 0
-        lax.fori_loop(0, 4, attb, 0, unroll=True)
+        lax.fori_loop(0, 2, attb, 0, unroll=True)
+        if i == 0:
+            rs.first(1, 1)
+            rs.step(2, 2)
+        else:
+            rs.first(1, 0)
+            rs.first(0, 0)
+            rs.first(0, 1)
+            rs.step(2, 3)
+        lax.fori_loop(2, 4, attb, 0, unroll=True)
         if i == 0:
             wgrad(1, 0, FIRST, A.at[GV])
             wgrad(0, 0, FIRST, A.at[GQ])
             wgrad(0, 1, FIRST, A.at[GK])
-            rs.step(2, 3)
-            rs.first(1, 0)
-            rs.first(0, 0)
-            rs.first(0, 1)
     rs.step(1, 2)
+    rs.step(0, 2)
     for n in range(2):
         acc = None
         for g, (ph, xh) in ((GQ, (0, 0)), (GK, (0, 1)), (GV, (1, 0))):
             t = back(lambda par: A[g, :, cols(par)], ph, xh, n)
             acc = t if acc is None else acc + t
         DG[:, cols(n)] = acc
-        if n == 0: rs.step(2, 4)
-    rs.step(0, 2)
+    rs.step(2, 4)
 
     def ln1b(r, _):
         rows = pl.ds(pl.multiple_of(r * RB, RB), RB)
@@ -741,7 +819,7 @@
         m2 = jnp.mean(dn * n, axis=-1, keepdims=True)
         DG[rows, :] = N2[rows, :] + I1[rows, 0:1] * (dn - m1 - n * m2)
         return 0
-    lax.fori_loop(0, L // RB, ln1b, 0)
+    lax.fori_loop(0, L // RB, ln1b, 0, unroll=UNROLL)
     out_in = pltpu.make_async_copy(DG, o_in, io.at[3])
     out_in.start()
     sub24 = lax.broadcasted_iota(jnp.int32, (24, 640), 0)
@@ -751,20 +829,20 @@
                  + jnp.where(sub24 == 17, v[1], 0.0) + jnp.where(sub24 == 18, v[2], 0.0))
     sg.start(0)
     rs.step(1, 3)
-    rs.step(2, 5)
+    rs.step(0, 3)
     for par in range(2):
         A[SECOND, :, cols(par)] = (MID[:, cols(par)] + dot(A[ACTIVE], wpan(2, 1, par))).astype(BF)
     out_lat = pltpu.make_async_copy(A.at[SECOND], o_lat, io.at[2])
     out_lat.start()
     sg.finish(0); sg.start(1)
+    rs.step(2, 5)
+    rs.step(1, 4)
+    rs.step(0, 4)
+    sg.finish(1); sg.start(2)
     ag.drain()
-    rs.step(0, 3)
-    rs.step(1, 4)
-    sg.finish(1); sg.start(2)
-    rs.step(0, 4)
     rs.step(1, 5)
+    rs.step(0, 5)
     sg.finish(2); sg.start(3)
-    rs.step(0, 5)
 
     outs = [(o_qkv, 0), (o_qkv, 1280), (o_qkv, 2560), (o_out, 0), (o_up, 0), (o_down, 0)]
     def emit(ph):
@@ -783,12 +861,9 @@
     sg.finish(3); sg.start(4)
     emit(1)
     sg.finish(4)
-    tab = None
-    for k in range(2):
-        ok = own[:, k * 640:(k + 1) * 640]
-        t = lax.dot_general(ok, SG[k], (((1,), (1,)), ((), ())), precision=lax.Precision.HIGHEST, preferred_element_type=F32)
-        u = lax.dot_general(SG[k, 16:24], ok, (((1,), (1,)), ((), ())), precision=lax.Precision.HIGHEST, preferred_element_type=F32)
-        tab, vec = (t, u) if tab is None else (tab + t, vec + u)
+    hi = lax.Precision.HIGHEST
+    tab = lax.dot_general(own, SGS2[...], (((1,), (1,)), ((), ())), precision=hi, preferred_element_type=F32)
+    vec = lax.dot_general(SGS2[16:24], own, (((1,), (1,)), ((), ())), precision=hi, preferred_element_type=F32)
     o_tab[...] = tab[0:10, 0:16]
     o_vec[...] = vec[:, 0:10]
     emit(0)
@@ -799,12 +874,29 @@
     for c in outs: c.wait()
 
 
-def results_kernel(lat, inp, tab, vec, qkv, out, up, down, o_lat, o_in, o_tab, o_b1, o_g2, o_b2, o_qkv, o_out, o_up, o_down, sem):
-    cps = [pltpu.make_async_copy(a, o, sem.at[i]) for i, (a, o) in enumerate(((lat, o_lat), (inp, o_in), (qkv, o_qkv), (out, o_out), (up, o_up), (down, o_down)))]
-    for c in cps: c.start()
-    o_tab[...] = tab[...]
-    for i, o in enumerate((o_b1, o_g2, o_b2)): o[...] = vec[i]
-    for c in cps: c.wait()
+def results_kernel(lat, inp, tab, vec, qkv, out, up, down, o_lat, o_in, o_tab, o_b1, o_g2, o_b2, o_qkv, o_out, o_up, o_down,
+                   v_lat, v_in, v_tab, v_vec, v_qkv, v_out, v_up, v_down, v_b1, v_g2, v_b2, sem):
+    first = pltpu.make_async_copy(vec, v_vec, sem.at[0])
+    first.start()
+    moves = []
+    for a, v, o, n in ((inp, v_in, o_in, 4), (lat, v_lat, o_lat, 2), (qkv, v_qkv, o_qkv, 1), (out, v_out, o_out, 1), (up, v_up, o_up, 1), (down, v_down, o_down, 1), (tab, v_tab, o_tab, 1)):
+        for k in range(n):
+            c = a.shape[0] // n
+            cut = (lambda r: r.at[pl.ds(k * c, c)]) if n > 1 else (lambda r: r)
+            i = 2 + 2 * len(moves)
+            moves.append((pltpu.make_async_copy(cut(a), cut(v), sem.at[i]), pltpu.make_async_copy(cut(v), cut(o), sem.at[i + 1])))
+    for a, _ in moves: a.start()
+    first.wait()
+    small = []
+    for i, (v, o) in enumerate(((v_b1, o_b1), (v_g2, o_g2), (v_b2, o_b2))):
+        v[...] = v_vec[i]
+        small.append(pltpu.make_async_copy(v, o, sem.at[24 + i]))
+        small[-1].start()
+    for a, b in moves:
+        a.wait()
+        b.start()
+    for _, b in moves: b.wait()
+    for c in small: c.wait()
 
 
 def per_device(latents, script_ids, gain_table, bias_one, w_qkv, w_out, gain_two, bias_two, w_up, w_down, cotangent):
@@ -820,21 +912,20 @@
         V_((3, 3, 4, 2) + blk, BF), V_((3, 1, 4) + blk, BF), V_((3, 3) + blk, BF),
         V_((3, 3, 2, 2, 2) + blk, BF), V_((3, 1, 2, 2) + blk, BF), V_((3, 3) + blk, BF),
         V_((3,) + blk, BF), V_((3, 5) + blk, BF), V_((3, 4, 2) + blk, BF),
-        V_((2, 32, 640), BF), V_((4, 3, 32, 640), BF), V_((2, 24, 640), F32), V_((4, 3, 24, 640), F32), V_((L, D), BF), V_((L, D), BF),
+        V_((32, D), BF), V_((32, 256), BF), V_((1, 32, 256), BF), V_((3, 32, 256), BF), V_((3, 32, 256), BF), V_((32, 384), BF), V_((3, 32, 384), BF),
+        V_((2, 24, 640), F32), V_((24, 640), F32), V_((3, 24, 384), F32), V_((24, 384), F32), V_((24, 256), F32), V_((24, 256), F32), V_((3, 24, 256), F32), V_((24, 256), F32), V_((L, D), BF), V_((L, D), BF), pltpu.SMEM((1,), jnp.int32),
         V_((10, 16), BF), V_((10,), BF), V_((10,), BF), V_((10,), BF), V_((10, 3 * D), BF), V_((10, D), BF), V_((10, D), BF), V_((10, D), BF),
         V_((10, 16), F32), V_((8, 10), F32), V_((10, 3 * D), F32), V_((10, D), F32), V_((10, D), F32), V_((10, D), F32),
         dma((8,)), dma((9, 6)), dma((3,)), dma((3,)),
         dma((2,)), dma((9, 2)), dma((6,)), dma((9, 5)), dma((1,)), dma((3, 2)),
-        dma((5,)), dma((5,)), dma((5,)), dma((5,)), dma((12,)),
+        dma((4,)), dma((4,)), dma((5,)), dma((5,)), dma((13,)),
     ]
-    vm = pl.BlockSpec(memory_space=pltpu.VMEM)
-    sm = pl.BlockSpec(memory_space=pltpu.SMEM)
     hbm = pl.BlockSpec(memory_space=pl.ANY)
     f32 = lambda *d: jax.ShapeDtypeStruct(d, F32)
     res = pl.pallas_call(
         block_kernel,
         out_shape=[jax.ShapeDtypeStruct((L, D), BF), f32(L, D), f32(10, 16), f32(8, 10), f32(10, 3 * D), f32(10, D), f32(10, D), f32(10, D)],
-        in_specs=[hbm, hbm, sm] + [hbm] * 8,
+        in_specs=[hbm, hbm, pl.BlockSpec(memory_space=pltpu.HBM)] + [hbm] * 8,
         out_specs=[hbm] * 8,
         scratch_shapes=scratch,
         compiler_params=pltpu.CompilerParams(collective_id=0, has_side_effects=True, vmem_limit_bytes=62 * 2**20),
@@ -843,9 +934,11 @@
     o_lat, o_in, o_tab, o_b1, o_g2, o_b2, o_qkv, o_out, o_up, o_down = pl.pallas_call(
         results_kernel,
         out_shape=[jax.ShapeDtypeStruct((L, D), BF), f32(L, D), f32(10, 16), f32(10), f32(10), f32(10), f32(10, 3 * D), f32(10, D), f32(10, D), f32(10, D)],
-        in_specs=[vm] * 8,
-        out_specs=[hbm, hbm] + [vm] * 4 + [hbm] * 4,
-        scratch_shapes=[dma((6,))],
+        in_specs=[hbm] * 8,
+        out_specs=[hbm] * 10,
+        scratch_shapes=[V_((L, D), BF), V_((L, D), F32), V_((10, 16), F32), V_((8, 10), F32), V_((10, 3 * D), F32), V_((10, D), F32), V_((10, D), F32), V_((10, D), F32),
+                        V_((10,), F32), V_((10,), F32), V_((10,), F32), dma((27,))],
+        compiler_params=pltpu.CompilerParams(vmem_limit_bytes=62 * 2**20),
         name="results",
     )(*res)
     return (o_lat.reshape(1, L, D), o_in.reshape(1, L, D), o_tab, o_b1, o_qkv, o_out, o_g2, o_b2, o_up, o_down)

time: 121 us -> 118 us (0.975)
  Pallas kernels: 120 us -> 117 us
    pallas_call x1, Pallas kernels: 116 us -> 114 us  [per_device(): pl.pallas_call(block_kernel, out_shape=[jax.ShapeDtypeStruct((L, D), BF),...]
where the time goes in v5:
time: 118 us
  Pallas kernels  117 us (99%)
  between operations  1.48 us (1%)
    pallas_call x1, Pallas kernels, per_device(): pl.pallas_call(block_kernel, out_shape=[jax.ShapeDtypeStruct((L, D), BF),...  114 us
    pallas_call x1, Pallas kernels, per_device(): pl.pallas_call(results_kernel, out_shape=[jax.ShapeDtypeStruct((L, D), BF...  2.65 us

profile of v5, /device:TPU:1, one launch (start us, length us, event | category | flops | bytes accessed | tf_op | source)
XLA Modules:
  0.0 118.2 jit_solution(6278177341334006748)
XLA Ops:
  1.3 114.0 %block.1 = (bf16[256,1280]{1,0:T(8,128)(2,1)}, f32[256,1280]{1,0:T(8,128)}, f32[10,16]{1,0:T(8,128)}, f32[8,10]{1,0:T(8,128)}, f32[10,3840]{1,0:T(8,128)}, /*ind...) custom-call(bf16[256,1280]{1,0:T(8,128)(2,1)} %bitcast.4, bf16[256,1280]{1,0:T(8,128)(2,1)} %bitcast.5, ...), custom_call_target="tpu_custom_call" | custom-call | tf_op jit(solution)/shard_map/block/pallas_call | solution.py:925
  115.3 2.6 %results.1 = (bf16[256,1280]{1,0:T(8,128)(2,1)}, f32[256,1280]{1,0:T(8,128)}, f32[10,16]{1,0:T(8,128)}, f32[10]{0:T(128)}, f32[10]{0:T(128)}, /*index=5*/f32[10]...) custom-call(bf16[256,1280]{1,0:T(8,128)(2,1)} %get-tuple-element.28.lat, ...), custom_call_target="tpu_custom_call" | custom-call | tf_op jit(solution)/shard_map/results/pallas_call | solution.py:934

commit v6 on v5

--- a/solution.py
+++ b/solution.py
@@ -22,18 +22,20 @@
 class Pos:
     def __init__(s):
         dp = lax.axis_index("dp"); s.xh = lax.axis_index("fsdp")
-        s.c = dp % 2; s.y = (dp // 2) % 4; s.xl = (dp // 8) % 2; s.z = dp // 16
-        s.x = s.xh * 2 + s.xl; s.h = s.y // 2; s.par = s.y % 2
+        s.c = (dp & 1); s.y = (((dp >> 1)) & 3); s.xl = ((dp >> 3) & 1); s.z = dp >> 4
+        s.x = s.xh * 2 + s.xl; s.h = (s.y >> 1); s.par = (s.y & 1)
+        s.coords = [[(v + d) & 3 if d else v for d in range(4)] for v in (s.x, s.y, s.z)]
+        s.rings = [[s.dev(**{n: s.coords[ax][d]}) for d in range(4)] for ax, n in enumerate('xyz')]
+        s.sibling = s.dev(c=1 - s.c)
+        s.pair = s.dev(x=s.xh * 2 + 1 - s.xl)
     def dev(s, x=None, y=None, z=None, c=None):
         x = s.x if x is None else x; y = s.y if y is None else y
         z = s.z if z is None else z; c = s.c if c is None else c
-        return (((z * 2 + x % 2) * 4 + y) * 2 + c, x // 2)
+        return (((z * 2 + (x & 1)) * 4 + y) * 2 + c, (x >> 1))
     def ring(s, ax, d):
-        if ax == 0: return s.dev(x=(s.x + d) % 4)
-        if ax == 1: return s.dev(y=(s.y + d) % 4)
-        return s.dev(z=(s.z + d) % 4)
+        return s.rings[ax][d & 3]
     def coord(s, ax, d):
-        return ((s.x, s.y, s.z)[ax] + d) % 4
+        return s.coords[ax][d & 3]
 
 def wait(ref, sem):
     pltpu.make_async_copy(ref, ref, sem).wait()
@@ -53,8 +55,8 @@
                     if (dy, dx, dc) == (0, 0, 0): continue
                     if (dy, dx, dc) == (0, 1, 0): continue
                     y = p.y ^ dy if dy else p.y
-                    x = (p.x + 2 * dx) % 4
-                    out.append(p.dev(x=x, y=y, c=(p.c + dc) % 2))
+                    x = ((p.x + 2 * dx) & 3)
+                    out.append(p.dev(x=x, y=y, c=((p.c + dc) & 1)))
         return out
     def s0_targets(s):
         p = s.p
@@ -62,7 +64,7 @@
         for dy in (0, 1):
             for dx in (0, 1):
                 y = p.y ^ dy if dy else p.y
-                x = (p.x + 2 * dx) % 4
+                x = ((p.x + 2 * dx) & 3)
                 res.append((dy, dx, y, x))
         return res
     def s0_src(s):
@@ -75,7 +77,7 @@
             @pl.when(cond)
             def _(tc=tc):
                 for dy, dx, y, x in s.s0_targets():
-                    src = s.pieces.at[ph, (x // 2) * 2 + y % 2]
+                    src = s.pieces.at[ph, ((x >> 1)) * 2 + (y & 1)]
                     dst = s.stg.at[ph, o - 4 * tc]
                     def send(sem):
                         pltpu.make_async_remote_copy(src, dst, s.s0s.at[sem], s.s0r.at[ph], device_id=p.dev(y=y, x=x, c=tc), device_id_type=MESH).start()
@@ -110,8 +112,8 @@
     def region(s, ph, t, full, over=None):
         p = s.p; o = over or {}
         x = o.get(0); y = o.get(1); z = o.get(2)
-        xh, xl = (p.xh, p.xl) if x is None else (x // 2, x % 2)
-        h, par = (p.h, p.par) if y is None else (y // 2, y % 2)
+        xh, xl = (p.xh, p.xl) if x is None else ((x >> 1), (x & 1))
+        h, par = (p.h, p.par) if y is None else ((y >> 1), (y & 1))
         zz = p.z if z is None else z
         if 0 in full: xh = xl = slice(None)
         if 1 in full: h = par = slice(None)
@@ -148,7 +150,7 @@
     def sib(s, ph, ts, piece):
         a = s.order(ph, ts); full = a[:2]; ax = a[2]
         d = (0, -1, 1, 2)[piece]
-        s.cp(s.region(ph, s.t(ts), full, {ax: s.p.coord(ax, d)}), ph, ts, 3, 5, s.p.dev(c=1 - s.p.c)).start()
+        s.cp(s.region(ph, s.t(ts), full, {ax: s.p.coord(ax, d)}), ph, ts, 3, 5, s.p.sibling).start()
     def go(s, ts, f, other=False):
         def h():
             f()
@@ -218,7 +220,7 @@
 
 
 def window(z, xl):
-    return 320 * z - 64 * (z % 2) + 128 * xl
+    return 320 * z - 64 * ((z & 1)) + 128 * xl
 
 
 class Spread:
@@ -229,7 +231,7 @@
     def start(s, k):
         p = s.p
         src = s.T3 if k == 3 else s.T
-        if k == 0: devs = [p.dev(c=1 - p.c)]
+        if k == 0: devs = [p.sibling]
         else: devs = [p.ring((1, 0, 2)[k - 1], d) for d in (1, 2, 3)]
         for i, dv in enumerate(devs):
             pltpu.make_async_remote_copy(src, s.R[k].at[i], s.ssem.at[k], s.rsem.at[k], device_id=dv, device_id_type=MESH).start()
@@ -252,7 +254,7 @@
         else:
             s.out[...] = jnp.zeros((32, D), BF)
             for i in range(4):
-                lanes = pl.ds(at128(window((p.z + 4 - i) % 4, 0)), 384)
+                lanes = pl.ds(at128(window(((p.z + 4 - i) & 3), 0)), 384)
                 v = s.T3[...] if i == 0 else R[i - 1]
                 s.out[:, lanes] = (s.out[:, lanes].astype(F32) + v.astype(F32)).astype(BF)
 
@@ -261,7 +263,7 @@
     def __init__(s, p, buf, R0, R1, S1, R2, S2, R3, R4, ssem, rsem):
         s.p, s.buf, s.R0, s.R1, s.S1, s.R2, s.S2, s.R3, s.R4 = p, buf, R0, R1, S1, R2, S2, R3, R4
         s.ssem, s.rsem = ssem, rsem
-        s.active = p.z // 2 == p.c
+        s.active = (p.z >> 1) == p.c
 
     def send(s, k, src, dst, dv):
         pltpu.make_async_remote_copy(src, dst, s.ssem.at[k], s.rsem.at[k], device_id=dv, device_id_type=MESH).start()
@@ -269,22 +271,22 @@
     def start(s, k):
         p = s.p
         if k == 0:
-            s.send(0, s.buf.at[1 - p.c], s.R0, p.dev(c=1 - p.c))
+            s.send(0, s.buf.at[1 - p.c], s.R0, p.sibling)
         elif k == 1:
             for d in (1, 2, 3):
-                z = (p.z + d) % 4
-                @pl.when(z // 2 == p.c)
+                z = ((p.z + d) & 3)
+                @pl.when((z >> 1) == p.c)
                 def _(z=z, d=d):
-                    s.send(1, s.buf.at[p.c, :, pl.ds(at128(256 * (z % 2)), 384)], s.R1.at[d - 1], p.dev(z=z))
+                    s.send(1, s.buf.at[p.c, :, pl.ds(at128(256 * ((z & 1))), 384)], s.R1.at[d - 1], p.dev(z=z))
         else:
             @pl.when(s.active)
             def _():
                 if k == 2:
-                    s.send(2, s.S1.at[:, pl.ds(at128(128 - 128 * p.xl), 256)], s.R2, p.dev(x=p.xh * 2 + 1 - p.xl))
+                    s.send(2, s.S1.at[:, pl.ds(at128(128 - 128 * p.xl), 256)], s.R2, p.pair)
                 elif k == 3:
                     for d in (1, 2, 3): s.send(3, s.S2, s.R3.at[d - 1], p.ring(1, d))
                 else:
-                    s.send(4, s.S2, s.R4, p.dev(c=1 - p.c))
+                    s.send(4, s.S2, s.R4, p.sibling)
 
     def finish(s, k):
         p = s.p
@@ -307,7 +309,7 @@
         def _():
             if k == 1:
                 wait(s.R1, s.rsem.at[1])
-                mine = pl.ds(at128(256 * (p.z % 2)), 384)
+                mine = pl.ds(at128(256 * ((p.z & 1))), 384)
                 s.S1[...] = s.buf[p.c, :, mine] + s.R1[0] + s.R1[1] + s.R1[2]
             elif k == 2:
                 wait(s.R2, s.rsem.at[2])
@@ -337,7 +339,7 @@
         p = s.p
         g = s.gref(ph)
         t = 3 * (1 - p.c) + ts if act != 'recv' else 3 * p.c + ts
-        cp = pltpu.make_async_remote_copy(g.at[par, :, :, :, t], s.RD.at[ph, ts, par], s.dss.at[ts // 2], s.drs.at[ph * 3 + ts, par], device_id=p.dev(c=1 - p.c), device_id_type=MESH)
+        cp = pltpu.make_async_remote_copy(g.at[par, :, :, :, t], s.RD.at[ph, ts, par], s.dss.at[(ts >> 1)], s.drs.at[ph * 3 + ts, par], device_id=p.sibling, device_id_type=MESH)
         if act == 'start': cp.start()
         else: cp.wait_recv()
 
@@ -354,7 +356,7 @@
         lax.fori_loop(0, 4, body, 0)
 
     def order(s, ph, ts):
-        return ((1, 0, 2), (2, 0, 1), (0, 1, 2))[ts]
+        return ((1, 0, 2), (2, 0, 1), (0, 2, 1))[ts]
 
     def fidx(s, ph, ts):
         return (1, 2, 0)[ts]
@@ -369,7 +371,7 @@
         if 1 in done: h, par = p.h, p.par
         if 2 in done: zz = p.z
         if ax == 0: xl = k
-        if ax == 1: h, par = k // 2, k % 2
+        if ax == 1: h, par = (k >> 1), (k & 1)
         if ax == 2: zz = k
         return s.gref(ph).at[par, zz, xl, h, 3 * p.c + ts]
 
@@ -379,7 +381,7 @@
         ax = o[st]
         assert st == 0
         t = 3 * p.c + ts
-        if ax == 1: return s.gref(ph).at[k % 2, pl.ds(2 * hf, 2), :, k // 2, t]
+        if ax == 1: return s.gref(ph).at[(k & 1), pl.ds(2 * hf, 2), :, (k >> 1), t]
         return s.gref(ph).at[hf, k, :, :, t]
 
     def bhalf(s, ph, ts, hf):
@@ -415,7 +417,7 @@
         sk = st + (3 if ts == 2 else 0)
         if ax == 0:
             k = 1 - p.xl
-            src, dv = s.piece(ph, ts, st, k), p.dev(x=p.xh * 2 + k)
+            src, dv = s.piece(ph, ts, st, k), p.pair
             if st == 0: return [s.cp(src.at[par], b.at[ph, 0, par], sk, sl, par, dv) for par in range(2)]
             return [s.cp(src, b.at[ph, 0], sk, sl, 2 + st, dv)]
         res = []
@@ -507,7 +509,7 @@
         p = s.p
         o = 4 * p.c + k
         chunk = 2 * p.xh + p.par
-        dev = p.dev(x=(o % 2) * 2 + p.xl, y=2 * p.h + o // 4, c=(o // 2) % 2)
+        dev = p.dev(x=((o & 1)) * 2 + p.xl, y=2 * p.h + (o >> 2), c=(((o >> 1)) & 1))
         return pltpu.make_async_remote_copy(s.EX.at[ph, k], s.FIN.at[ph, chunk, p.c], s.fs.at[0], s.fr.at[ph, p.c], device_id=dev, device_id_type=MESH)
 
     def myo(s):
@@ -582,10 +584,10 @@
     block_body(lat_in, cot_in, sid, small_in, o_lat, o_in, small_out, *refs[16:])
 
 
-def block_body(lat_in, cot_in, sid_in, small_in, o_lat, o_in, small_out,
+def block_body(lat_in, cot_in, sid, small_in, o_lat, o_in, small_out,
                  W, stg, pieces, A, N1, N2, MID, DG, PR, I1, I2, VEC, CS, GW, RD, b00, b01, b02, b10, b11, b12, b20, b21, b22,
                  FR, EX, FIN, SB, SBT, SB0, SB1, SB2, SBT3, SB3, SG, SG0, SG1, SGS1, SG2, SGS2, SG3, SG4,
-                 lat, cot, sid, gt, b1, g2, b2, wq, wo, wu, wd, o_tab, o_vec, o_qkv, o_out, o_up, o_down, ssem, rsem, s0s, s0r, dss, drs, gss, grs, fs, fr, sbs, sbr, sgs, sgr, io):
+                 lat, cot, gt, b1, g2, b2, wq, wo, wu, wd, o_tab, o_vec, o_qkv, o_out, o_up, o_down, ssem, rsem, s0s, s0r, dss, drs, gss, grs, fs, fr, sbs, sbr, sgs, sgr, io):
     p = Pos()
     ag = AG(p, W, stg, pieces, ssem, rsem, None, s0s, s0r)
     G = [GW.at[0], GW.at[1], GW.at[2]]
@@ -600,8 +602,6 @@
         pl.semaphore_signal(bar, inc=1, device_id=d, device_id_type=MESH)
     in_lat = pltpu.make_async_copy(lat_in, lat, io.at[0])
     in_cot = pltpu.make_async_copy(cot_in, cot, io.at[1])
-    in_sid = pltpu.make_async_copy(sid_in, sid, io.at[12])
-    in_sid.start()
     ins = [pltpu.make_async_copy(a, v, io.at[4 + i]) for i, (a, v) in enumerate(zip(small_in, (gt, b1, g2, b2, wq, wo, wu, wd)))]
     for c in ins: c.start()
     in_lat.start(); in_cot.start()
@@ -628,7 +628,7 @@
         N1[rows, :] = xc * inv
         I1[rows, :] = jnp.broadcast_to(inv, (RB, 128))
         return 0
-    in_lat.wait(); in_cot.wait(); in_sid.wait()
+    in_lat.wait(); in_cot.wait()
     lax.fori_loop(0, L // RB, ln1, 0, unroll=UNROLL)
     ag.s0_recv(0); ag.compact(0); ag.phase_a(0)
     sb.finish(0); sb.start(1)
@@ -649,7 +649,8 @@
     sb.finish(3)
     lane32 = lax.broadcasted_iota(jnp.int32, (8, 32), 1)
     sub8 = lax.broadcasted_iota(jnp.int32, (8, 32), 0)
-    tgt = jnp.where(sub8 == 0, sid[0], jnp.where(sub8 < 4, 15 + sub8, -1))
+    script = jnp.broadcast_to(sid[...].reshape(1, 1), (1, 640))
+    tgt = jnp.where(sub8 == 0, script[:, 0:32], jnp.where(sub8 < 4, 15 + sub8, -1))
     pick = jnp.where(lane32 == tgt, 1.0, 0.0).astype(BF)
     VEC[...] = dot(pick, SB[...])
 
@@ -825,7 +826,7 @@
     sub24 = lax.broadcasted_iota(jnp.int32, (24, 640), 0)
     for k in range(2):
         v = [jnp.sum(CS[i, :, k * 640:(k + 1) * 640], axis=0, keepdims=True) for i in range(4)]
-        SG[k] = (jnp.where(sub24 == sid[0], v[3], 0.0) + jnp.where(sub24 == 16, v[0], 0.0)
+        SG[k] = (jnp.where(sub24 == script, v[3], 0.0) + jnp.where(sub24 == 16, v[0], 0.0)
                  + jnp.where(sub24 == 17, v[1], 0.0) + jnp.where(sub24 == 18, v[2], 0.0))
     sg.start(0)
     rs.step(1, 3)
@@ -908,24 +909,24 @@
         V_((13, L, D), BF), V_((L, D), F32), V_((L, D), F32), V_((L, D), F32), V_((L, D), F32),
         V_((8, 256, 256), F32), V_((L, 128), F32), V_((L, 128), F32), V_((8, D), F32), V_((4, 8, D), F32),
         V_((3, 2, 4, 2, 2, 5) + blk, BF), V_((3, 3, 2, 4, 2, 2) + blk, BF),
-        V_((3, 1, 2, 4, 2) + blk, BF), V_((3, 3, 4) + blk, BF), V_((3, 3) + blk, BF),
+        V_((3, 1, 2, 4, 2) + blk, BF), V_((3, 3, 2, 2) + blk, BF), V_((3, 3) + blk, BF),
         V_((3, 3, 4, 2) + blk, BF), V_((3, 1, 4) + blk, BF), V_((3, 3) + blk, BF),
         V_((3, 3, 2, 2, 2) + blk, BF), V_((3, 1, 2, 2) + blk, BF), V_((3, 3) + blk, BF),
         V_((3,) + blk, BF), V_((3, 5) + blk, BF), V_((3, 4, 2) + blk, BF),
         V_((32, D), BF), V_((32, 256), BF), V_((1, 32, 256), BF), V_((3, 32, 256), BF), V_((3, 32, 256), BF), V_((32, 384), BF), V_((3, 32, 384), BF),
-        V_((2, 24, 640), F32), V_((24, 640), F32), V_((3, 24, 384), F32), V_((24, 384), F32), V_((24, 256), F32), V_((24, 256), F32), V_((3, 24, 256), F32), V_((24, 256), F32), V_((L, D), BF), V_((L, D), BF), pltpu.SMEM((1,), jnp.int32),
+        V_((2, 24, 640), F32), V_((24, 640), F32), V_((3, 24, 384), F32), V_((24, 384), F32), V_((24, 256), F32), V_((24, 256), F32), V_((3, 24, 256), F32), V_((24, 256), F32), V_((L, D), BF), V_((L, D), BF),
         V_((10, 16), BF), V_((10,), BF), V_((10,), BF), V_((10,), BF), V_((10, 3 * D), BF), V_((10, D), BF), V_((10, D), BF), V_((10, D), BF),
         V_((10, 16), F32), V_((8, 10), F32), V_((10, 3 * D), F32), V_((10, D), F32), V_((10, D), F32), V_((10, D), F32),
         dma((8,)), dma((9, 6)), dma((3,)), dma((3,)),
         dma((2,)), dma((9, 2)), dma((6,)), dma((9, 5)), dma((1,)), dma((3, 2)),
-        dma((4,)), dma((4,)), dma((5,)), dma((5,)), dma((13,)),
+        dma((4,)), dma((4,)), dma((5,)), dma((5,)), dma((12,)),
     ]
     hbm = pl.BlockSpec(memory_space=pl.ANY)
     f32 = lambda *d: jax.ShapeDtypeStruct(d, F32)
     res = pl.pallas_call(
         block_kernel,
         out_shape=[jax.ShapeDtypeStruct((L, D), BF), f32(L, D), f32(10, 16), f32(8, 10), f32(10, 3 * D), f32(10, D), f32(10, D), f32(10, D)],
-        in_specs=[hbm, hbm, pl.BlockSpec(memory_space=pltpu.HBM)] + [hbm] * 8,
+        in_specs=[hbm, hbm, pl.BlockSpec(memory_space=pltpu.VMEM)] + [hbm] * 8,
         out_specs=[hbm] * 8,
         scratch_shapes=scratch,
         compiler_params=pltpu.CompilerParams(collective_id=0, has_side_effects=True, vmem_limit_bytes=62 * 2**20),

time: 118 us -> 117 us (level)
  no operation moved by 1% of the time
where the time goes in v6:
time: 117 us
  Pallas kernels  116 us (99%)
  between operations  1.48 us (1%)
    pallas_call x1, Pallas kernels, per_device(): pl.pallas_call(block_kernel, out_shape=[jax.ShapeDtypeStruct((L, D), BF),...  113 us
    pallas_call x1, Pallas kernels, per_device(): pl.pallas_call(results_kernel, out_shape=[jax.ShapeDtypeStruct((L, D), BF...  2.65 us

profile of v6, /device:TPU:1, one launch (start us, length us, event | category | flops | bytes accessed | tf_op | source)
XLA Modules:
  0.0 117.2 jit_solution(5661181692722709045)
XLA Ops:
  1.3 113.1 %block.1 = (bf16[256,1280]{1,0:T(8,128)(2,1)}, f32[256,1280]{1,0:T(8,128)}, f32[10,16]{1,0:T(8,128)}, f32[8,10]{1,0:T(8,128)}, f32[10,3840]{1,0:T(8,128)}, /*ind...) custom-call(bf16[256,1280]{1,0:T(8,128)(2,1)} %bitcast.4, bf16[256,1280]{1,0:T(8,128)(2,1)} %bitcast.5, ...), custom_call_target="tpu_custom_call" | custom-call | tf_op jit(solution)/shard_map/block/pallas_call | solution.py:926
  114.4 2.6 %results.1 = (bf16[256,1280]{1,0:T(8,128)(2,1)}, f32[256,1280]{1,0:T(8,128)}, f32[10,16]{1,0:T(8,128)}, f32[10]{0:T(128)}, f32[10]{0:T(128)}, /*index=5*/f32[10]...) custom-call(bf16[256,1280]{1,0:T(8,128)(2,1)} %get-tuple-element.28.lat, ...), custom_call_target="tpu_custom_call" | custom-call | tf_op jit(solution)/shard_map/results/pallas_call | solution.py:935

commit v7 on v6

--- a/solution.py
+++ b/solution.py
@@ -61,8 +61,8 @@
     def s0_targets(s):
         p = s.p
         res = []
-        for dy in (0, 1):
-            for dx in (0, 1):
+        for dy in (1, 0):
+            for dx in (1, 0):
                 y = p.y ^ dy if dy else p.y
                 x = ((p.x + 2 * dx) & 3)
                 res.append((dy, dx, y, x))
@@ -131,7 +131,7 @@
     def t(s, ts): return 3 * s.p.c + ts
     def direct(s, stage, ph, ts):
         a = s.order(ph, ts); full = a[:stage]; ax = a[stage]
-        for d in (1, 3, 2):
+        for d in (2, 1, 3):
             s.cp(s.region(ph, s.t(ts), full), ph, ts, stage, stage, s.p.ring(ax, d)).start()
     def got(s, ph, ts, k):
         r = s.W.at[ph]
@@ -421,7 +421,7 @@
             if st == 0: return [s.cp(src.at[par], b.at[ph, 0, par], sk, sl, par, dv) for par in range(2)]
             return [s.cp(src, b.at[ph, 0], sk, sl, 2 + st, dv)]
         res = []
-        for i, d in enumerate((1, 3, 2)):
+        for i, d in enumerate((2, 1, 3)):
             res.append(s.cp(s.piece(ph, ts, st, p.coord(ax, d)), b.at[ph, i], sk, sl, 2 + st, p.ring(ax, d)))
         return res
 

time: 117 us -> 116 us (level)
  Pallas kernels: 116 us -> 114 us
    pallas_call x1, Pallas kernels: 113 us -> 111 us  [per_device(): pl.pallas_call(block_kernel, out_shape=[jax.ShapeDtypeStruct((L, D), BF),...]
where the time goes in v7:
time: 116 us; the launch traced here: 115 us
  Pallas kernels  114 us (98%)
  between operations  1.48 us (1%)
    pallas_call x1, Pallas kernels, per_device(): pl.pallas_call(block_kernel, out_shape=[jax.ShapeDtypeStruct((L, D), BF),...  111 us
    pallas_call x1, Pallas kernels, per_device(): pl.pallas_call(results_kernel, out_shape=[jax.ShapeDtypeStruct((L, D), BF...  2.65 us

profile of v7, /device:TPU:1, one launch (start us, length us, event | category | flops | bytes accessed | tf_op | source)
XLA Modules:
  0.0 115.5 jit_solution(11918097228955986032)
XLA Ops:
  1.3 111.4 %block.1 = (bf16[256,1280]{1,0:T(8,128)(2,1)}, f32[256,1280]{1,0:T(8,128)}, f32[10,16]{1,0:T(8,128)}, f32[8,10]{1,0:T(8,128)}, f32[10,3840]{1,0:T(8,128)}, /*ind...) custom-call(bf16[256,1280]{1,0:T(8,128)(2,1)} %bitcast.4, bf16[256,1280]{1,0:T(8,128)(2,1)} %bitcast.5, ...), custom_call_target="tpu_custom_call" | custom-call | tf_op jit(solution)/shard_map/block/pallas_call | solution.py:926
  112.7 2.6 %results.1 = (bf16[256,1280]{1,0:T(8,128)(2,1)}, f32[256,1280]{1,0:T(8,128)}, f32[10,16]{1,0:T(8,128)}, f32[10]{0:T(128)}, f32[10]{0:T(128)}, /*index=5*/f32[10]...) custom-call(bf16[256,1280]{1,0:T(8,128)(2,1)} %get-tuple-element.28.lat, ...), custom_call_target="tpu_custom_call" | custom-call | tf_op jit(solution)/shard_map/results/pallas_call | solution.py:935
